TPU v7x, 32 devices: a whole 2x2x4 slice. The times are simulated.
32 devices in a mesh: bulk: 4 (over y, core), front: 8 (over z, x).
Axes of the slice: x: 2, y: 2, z: 4, core: 2. Of those that a mesh axis runs over, the one named last changes fastest.
Arguments:
- child_pivot: float32 [4, 2048, 2048], P('bulk', 'front'), may hold values from -20 to 40, as said below
- child_coupling: float32 [4, 2048, 2048], P('bulk', 'front'), may hold values from -0.75 to 0.75
- parent_arrow: float32 [8192, 1024], P(('bulk', 'front')), may hold values from -600 to 3000, as said below
- row_map: int32 [4, 2048], P('bulk', 'front'), may hold values from 0 to 8191, as said below
- block_pattern: int32 [64, 8], replicated, may hold values from 0 to 1, as said below
Outputs:
- child_factor_pivot: float32 [4, 2048, 2048], P('bulk', 'front')
- child_factor_coupling: float32 [4, 2048, 2048], P('bulk', 'front')
- parent_factor: float32 [8192, 1024], P(('bulk', 'front'))
Inputs may be any that keep to these rules, and one draw needn't show every extreme that they name: `child_pivot`: each child's matrix is symmetric and positive definite. `parent_arrow`: the first 1024 rows hold a symmetric block that stays positive definite when contribution is added. `row_map`: A child's 2048 entries are distinct. Entry i of a child names a row r with (r // 256) % (8) == i // 256. `block_pattern`: every block (i, i) with i < 8 is 1.
All inputs are finite; a program needn't handle non-finite values.
Results may differ from a plain program's by a relative error of at most 0.00022.
Values sent between devices are 32-bit elements; how exact they have to be, the bound alone decides.
No kernel may reach another device: no remote copies, remote signals or barrier semaphores. Data moves between devices by JAX's collectives and lax.ppermute only.
A program may use at most 128 MiB of HBM per device.

v0:
```python
import jax
import jax.numpy as jnp
from jax import lax
from jax.sharding import PartitionSpec as P

BLOCK = 128
PANEL = 512


HIGHEST_PRECISION = lax.Precision.HIGHEST


def broadcast(value, axis, source):
    kept = jnp.where(lax.axis_index(axis) == source, value, 0).astype(value.dtype)
    return lax.psum(kept, axis)


def mirror_lower(matrix):
    return jnp.tril(matrix) + jnp.tril(matrix, -1).T


def solve_right(lower_factor, matrix):
    return jax.scipy.linalg.solve_triangular(lower_factor, matrix.T, lower=True).T


def child_chain(own_rows, coupling, panel_width):
    row_count, total_cols = own_rows.shape
    first_row = lax.axis_index("front") * row_count
    global_rows = first_row + jnp.arange(row_count)
    row_ids = jnp.arange(total_cols)
    step_count = total_cols // panel_width

    def advance(step_now, carried):
        own_state, coupling_state = carried
        col_start = step_now * panel_width
        column = lax.dynamic_slice_in_dim(own_state, col_start, panel_width, 1)
        gathered = lax.all_gather(column, "front", axis=0, tiled=True)
        diag_block = lax.dynamic_slice_in_dim(gathered, col_start, panel_width, 0)
        factor = jnp.linalg.cholesky(mirror_lower(diag_block))
        solved = jnp.where((row_ids >= col_start)[:, None], solve_right(factor, gathered), 0.0)
        solved = lax.dynamic_update_slice_in_dim(solved, factor, col_start, 0)
        trailing = jnp.where((row_ids >= col_start + panel_width)[:, None], solved, 0.0)
        own_factor = lax.dynamic_slice_in_dim(solved, first_row, row_count, 0)
        own_state = own_state - jnp.dot(own_factor, trailing.T, precision=HIGHEST_PRECISION)
        kept_block = lax.dynamic_slice_in_dim(own_state, col_start, panel_width, 1)
        new_block = jnp.where((global_rows >= col_start)[:, None], own_factor, kept_block)
        own_state = lax.dynamic_update_slice_in_dim(own_state, new_block, col_start, 1)
        block_part = lax.dynamic_slice_in_dim(coupling_state, col_start, panel_width, 1)
        block_part = solve_right(factor, block_part)
        coupling_state = coupling_state - jnp.dot(
            block_part, trailing.T, precision=HIGHEST_PRECISION
        )
        coupling_state = lax.dynamic_update_slice_in_dim(coupling_state, block_part, col_start, 1)
        return (own_state, coupling_state)

    own_rows, coupling = lax.fori_loop(0, step_count, advance, (own_rows, coupling))
    own_rows = jnp.where(row_ids[None, :] <= global_rows[:, None], own_rows, 0.0)
    return (own_rows, coupling)


def parent_whole(assembled, first_row, pivots):
    row_count = assembled.shape[0]
    group_rows = lax.all_gather(assembled, "front", axis=0, tiled=True)
    pivot_block = broadcast(group_rows[:pivots], "bulk", 0)
    factor = jnp.linalg.cholesky(mirror_lower(pivot_block))
    pivot_factor = lax.dynamic_slice_in_dim(
        factor, jnp.minimum(first_row, pivots - row_count), row_count, 0
    )
    return jnp.where(first_row < pivots, pivot_factor, solve_right(factor, assembled))


def on_device(child_pivot, child_coupling, parent_arrow, row_map, block_pattern):
    own_rows = child_pivot[0]
    coupling_rows = child_coupling[0]
    parent_index = row_map[0]
    panel_width = PANEL
    lower_rows, coupling = child_chain(own_rows, coupling_rows, panel_width)
    parent_count, pivots = parent_arrow.shape
    front_index = lax.axis_index("front")
    front_groups = lax.axis_size("front")
    local_slot = parent_index - front_index * parent_count
    landing_hits = (local_slot[:, None] == jnp.arange(parent_count)[None, :]).astype(jnp.float32)
    landing_piece = jnp.dot(landing_hits.T, coupling, precision=HIGHEST_PRECISION)
    reached = -jnp.dot(
        coupling,
        lax.all_gather(landing_piece, "front", axis=0, tiled=True).T,
        precision=HIGHEST_PRECISION,
    )
    contribution = reached[:, :pivots]
    slot_index = (
        parent_index // parent_count // front_groups * parent_count + parent_index % parent_count
    )
    spread_rows = lax.axis_size("bulk") * parent_count
    routing = (slot_index[:, None] == jnp.arange(spread_rows)[None, :]).astype(jnp.float32)
    added = lax.psum_scatter(
        jnp.dot(routing.T, contribution, precision=HIGHEST_PRECISION),
        "bulk",
        scatter_dimension=0,
        tiled=True,
    )
    device_index = lax.axis_index("bulk") * front_groups + front_index
    first_row = device_index * parent_count
    block_rows = (first_row + jnp.arange(parent_count)) // BLOCK
    block_count = block_pattern.shape[0]
    picker = (block_rows[:, None] == jnp.arange(block_count)[None, :]).astype(jnp.float32)
    row_mask = jnp.dot(picker, block_pattern.astype(jnp.float32), precision=HIGHEST_PRECISION)
    full_mask = jnp.repeat(row_mask, BLOCK, axis=1)
    assembled = parent_arrow * full_mask + added
    parent_rows = parent_whole(assembled, first_row, pivots)
    return (lower_rows[None], coupling[None], parent_rows)


def solution(mesh):
    placed = (
        P("bulk", "front", None),
        P("bulk", "front", None),
        P(("bulk", "front"), None),
        P("bulk", "front"),
        P(),
    )
    return jax.shard_map(
        on_device,
        mesh=mesh,
        in_specs=placed,
        out_specs=(P("bulk", "front", None), P("bulk", "front", None), P(("bulk", "front"), None)),
        check_vma=False,
    )
```

profile of v0, /device:TPU:20, one launch (start us, length us, event | category | flops | bytes accessed | tf_op | source)
XLA Modules:
  0.0 1967.2 jit_solution(6807992179562077526)
XLA Ops:
  12.6 1061.5 %while.26 = (s32[]{:T(128)}, f32[256,2048]{1,0:T(8,128)}, f32[256,2048]{1,0:T(8,128)}, s32[]{:T(128)}, s32[]{:T(128)}, /*index=5*/s32[]{:T(128)}, s32[]{:T(128)}...) while((s32[]{:T(128)}, f32[256,2048]{1,0:T(8,128)}, f32[256,2048]{1,0:T(8,128)}, ...), condition=%wide.region_9.13_spmd.clone.clone, body=%wide.region_0.12_spmd.clone.clone.sunk | while | flops 11389736960 | bytes 145379760 | solution.py:56
  20.0 70.3 %all-gather.8.cloned.1.call-done = f32[2048,512]{1,0:T(8,128)} async-done(((f32[256,512]{1,0:T(8,128)}), f32[2048,512]{1,0:T(8,128)}) %all-gather.8.cloned.1.call-update) | async-done | bytes 4194320 | tf_op jit(solution)/shard_map/while/body/eval_jaxpr/all_gather | solution.py:37
  94.0 11.7 cholesky.1240
  116.4 11.7 cholesky.1243
  138.8 11.7 cholesky.1245
  161.0 11.9 cholesky.1246
  189.8 40.2 %custom-call.141 = f32[4,128,128]{1,2,0:T(8,128)S(1)} custom-call(f32[4,128,128]{2,1,0:T(8,128)} %get-tuple-element.441), custom_call_target="InvertDiagBlocksLowerTriangular" | custom-call | tf_op jit(solution)/shard_map/while/body/eval_jaxpr/jit(_solve_triangular)/triangular_solve | solution.py:23
  284.8 68.4 %all-gather.8.cloned.1.call-done = f32[2048,512]{1,0:T(8,128)} async-done(((f32[256,512]{1,0:T(8,128)}), f32[2048,512]{1,0:T(8,128)}) %all-gather.8.cloned.1.call-update) | async-done | bytes 4194320 | tf_op jit(solution)/shard_map/while/body/eval_jaxpr/all_gather | solution.py:37
  356.9 11.7 cholesky.1240
  379.3 11.7 cholesky.1243
  402.0 11.7 cholesky.1245
  424.1 11.9 cholesky.1246
  452.9 40.2 %custom-call.141 = f32[4,128,128]{1,2,0:T(8,128)S(1)} custom-call(f32[4,128,128]{2,1,0:T(8,128)} %get-tuple-element.441), custom_call_target="InvertDiagBlocksLowerTriangular" | custom-call | tf_op jit(solution)/shard_map/while/body/eval_jaxpr/jit(_solve_triangular)/triangular_solve | solution.py:23
  548.0 68.4 %all-gather.8.cloned.1.call-done = f32[2048,512]{1,0:T(8,128)} async-done(((f32[256,512]{1,0:T(8,128)}), f32[2048,512]{1,0:T(8,128)}) %all-gather.8.cloned.1.call-update) | async-done | bytes 4194320 | tf_op jit(solution)/shard_map/while/body/eval_jaxpr/all_gather | solution.py:37
  620.1 11.7 cholesky.1240
  642.4 11.7 cholesky.1243
  665.1 11.7 cholesky.1245
  687.2 11.9 cholesky.1246
  716.0 40.2 %custom-call.141 = f32[4,128,128]{1,2,0:T(8,128)S(1)} custom-call(f32[4,128,128]{2,1,0:T(8,128)} %get-tuple-element.441), custom_call_target="InvertDiagBlocksLowerTriangular" | custom-call | tf_op jit(solution)/shard_map/while/body/eval_jaxpr/jit(_solve_triangular)/triangular_solve | solution.py:23
  811.0 68.1 %all-gather.8.cloned.1.call-done = f32[2048,512]{1,0:T(8,128)} async-done(((f32[256,512]{1,0:T(8,128)}), f32[2048,512]{1,0:T(8,128)}) %all-gather.8.cloned.1.call-update) | async-done | bytes 4194320 | tf_op jit(solution)/shard_map/while/body/eval_jaxpr/all_gather | solution.py:37
  882.8 11.7 cholesky.1240
  950.0 11.9 cholesky.1246
  978.7 40.2 %custom-call.141 = f32[4,128,128]{1,2,0:T(8,128)S(1)} custom-call(f32[4,128,128]{2,1,0:T(8,128)} %get-tuple-element.441), custom_call_target="InvertDiagBlocksLowerTriangular" | custom-call | tf_op jit(solution)/shard_map/while/body/eval_jaxpr/jit(_solve_triangular)/triangular_solve | solution.py:23
  1078.5 225.6 %all-gather.4.cloned.1.call-done = f32[2048,2048]{1,0:T(8,128)} async-done(((f32[256,2048]{1,0:T(8,128)}), f32[2048,2048]{1,0:T(8,128)}) %all-gather.4.cloned.1.call-update) | async-done | bytes 16777232 | tf_op jit(solution)/shard_map/all_gather | solution.py:86
  1304.1 17.0 fusion.157
  1325.4 42.4 %reduce-scatter.2.cloned.1.call-done = f32[256,1024]{1,0:T(8,128)} async-done(((f32[1024,1024]{1,0:T(8,128)}), f32[256,1024]{1,0:T(8,128)}) %reduce-scatter.2.cloned.1.call-update) | async-done | bytes 1048592 | tf_op jit(solution)/shard_map/reduce_scatter | solution.py:95
  1370.8 124.6 %all-gather.6.cloned.1.call-done = f32[2048,1024]{1,0:T(8,128)} async-done(((f32[256,1024]{1,0:T(8,128)}), f32[2048,1024]{1,0:T(8,128)}) %all-gather.6.cloned.1.call-update) | async-done | bytes 8388624 | tf_op jit(solution)/shard_map/all_gather | solution.py:63
  1503.6 80.5 %all-reduce.4.cloned.1.call-done = f32[1024,1024]{1,0:T(8,128)} async-done(((f32[1024,1024]{1,0:T(8,128)}), f32[1024,1024]{1,0:T(8,128)}) %all-reduce.4.cloned.1.call-update) | async-done | bytes 4194320 | tf_op jit(solution)/shard_map/psum | solution.py:15
  1640.2 11.9 cholesky.368
  1691.6 11.9 cholesky.593
  1822.7 22.5 %while.24 = (s32[]{:T(128)}, f32[1024,1024]{1,0:T(8,128)}, s32[8,2]{0,1:T(2,128)S(1)}, f32[8,128,128]{2,1,0:T(8,128)S(1)}, s32[]{:T(128)}) while((s32[]{:T(128)}, f32[1024,1024]{1,0:T(8,128)}, s32[8,2]{0,1:T(2,128)S(1)}, f32[8,128,128]{2,1,0:T(8,128)S(1)}, s32[]{:T(128)}) %tuple.148), condition=%wide.while_cond.1, body=%wide.while_body.1.sunk | while | flops 2 | bytes 131189 | solution.py:23
  1845.2 78.8 %custom-call.110 = f32[8,128,128]{1,2,0:T(8,128)S(1)} custom-call(f32[8,128,128]{2,1,0:T(8,128)S(1)} %get-tuple-element.178), custom_call_target="InvertDiagBlocksLowerTriangular" | custom-call | tf_op jit(solution)/shard_map/jit(_solve_triangular)/triangular_solve | solution.py:23
  (500 shorter events, 775.4 us)
Async XLA Ops:
  8.0 3.3 copy-start.8
  8.0 4.6 copy-start.13
  13.2 77.2 %all-gather.8.cloned.1.call-start = ((), (), s32[]{:S(2)}) async-start(), calls=%async_computation.5 | async-start | bytes 4718592 | tf_op jit(solution)/shard_map/while/body/eval_jaxpr/all_gather | solution.py:37
  189.8 46.8 %copy-start.2 = (f32[512,512]{1,0:T(8,128)}, f32[512,512]{1,0:T(8,128)S(1)}, u32[]{:S(2)}) copy-start(f32[512,512]{1,0:T(8,128)S(1)} %get-tuple-element.519) | copy-start | bytes 3145732 | tf_op jit(solution)/shard_map/while
  229.9 6.6 copy-start
  252.5 7.8 copy-start.3
  261.7 6.3 copy-start.1
  274.8 2.0 copy-start.5
  278.0 75.3 %all-gather.8.cloned.1.call-start = ((), (), s32[]{:S(2)}) async-start(), calls=%async_computation.5 | async-start | bytes 4718592 | tf_op jit(solution)/shard_map/while/body/eval_jaxpr/all_gather | solution.py:37
  452.9 46.7 %copy-start.2 = (f32[512,512]{1,0:T(8,128)}, f32[512,512]{1,0:T(8,128)S(1)}, u32[]{:S(2)}) copy-start(f32[512,512]{1,0:T(8,128)S(1)} %get-tuple-element.519) | copy-start | bytes 3145732 | tf_op jit(solution)/shard_map/while
  493.1 6.6 copy-start
  515.5 7.8 copy-start.3
  524.6 6.6 copy-start.1
  541.1 75.3 %all-gather.8.cloned.1.call-start = ((), (), s32[]{:S(2)}) async-start(), calls=%async_computation.5 | async-start | bytes 4718592 | tf_op jit(solution)/shard_map/while/body/eval_jaxpr/all_gather | solution.py:37
  716.0 46.7 %copy-start.2 = (f32[512,512]{1,0:T(8,128)}, f32[512,512]{1,0:T(8,128)S(1)}, u32[]{:S(2)}) copy-start(f32[512,512]{1,0:T(8,128)S(1)} %get-tuple-element.519) | copy-start | bytes 3145732 | tf_op jit(solution)/shard_map/while
  756.2 6.6 copy-start
  778.5 7.8 copy-start.3
  787.7 6.6 copy-start.1
  801.0 2.0 copy-start.5
  804.2 74.9 %all-gather.8.cloned.1.call-start = ((), (), s32[]{:S(2)}) async-start(), calls=%async_computation.5 | async-start | bytes 4718592 | tf_op jit(solution)/shard_map/while/body/eval_jaxpr/all_gather | solution.py:37
  978.7 46.7 %copy-start.2 = (f32[512,512]{1,0:T(8,128)}, f32[512,512]{1,0:T(8,128)S(1)}, u32[]{:S(2)}) copy-start(f32[512,512]{1,0:T(8,128)S(1)} %get-tuple-element.519) | copy-start | bytes 3145732 | tf_op jit(solution)/shard_map/while
  1018.9 6.6 copy-start
  1041.3 7.8 copy-start.3
  1050.5 6.6 copy-start.1
  1063.8 2.0 copy-start.5
  1074.1 229.9 %all-gather.4.cloned.1.call-start = ((), (), s32[]{:S(2)}) async-start(), calls=%async_computation.1 | async-start | bytes 18874368 | tf_op jit(solution)/shard_map/all_gather | solution.py:86
  1078.5 289.3 %reduce-scatter.2.cloned.1.call-start = ((), (), s32[]{:S(2)}) async-start(), calls=%async_computation.2 | async-start | bytes 5242880 | tf_op jit(solution)/shard_map/reduce_scatter | solution.py:95
  1321.1 4.0 copy-start.12
  1321.1 47.0 %copy-start.10 = (f32[256,1024]{1,0:T(8,128)S(1)}, f32[256,1024]{1,0:T(8,128)}, u32[]{:S(2)}) copy-start(f32[256,1024]{1,0:T(8,128)} %param.15) | copy-start | bytes 3145732
  1325.0 170.4 %all-gather.6.cloned.1.call-start = ((), (), s32[]{:S(2)}) async-start(), calls=%async_computation.3 | async-start | bytes 9437184 | tf_op jit(solution)/shard_map/all_gather | solution.py:63
  1370.8 213.3 %all-reduce.4.cloned.1.call-start = ((), (), s32[]{:S(2)}) async-start(), calls=%async_computation.4 | async-start | bytes 8388608 | tf_op jit(solution)/shard_map/psum | solution.py:15
  1816.0 108.0 %copy-start.7 = (f32[256,1024]{1,0:T(8,128)S(1)}, f32[256,1024]{1,0:T(8,128)}, u32[]{:S(2)}) copy-start(f32[256,1024]{1,0:T(8,128)} %fusion.86) | copy-start | bytes 3145732
  (8 other events, 11.5 us)
Sparse Core Ops, SparseCore 0:
  16.7 73.5 all-gather.7
  281.5 71.6 all-gather.7
  544.7 71.6 all-gather.7
  807.4 71.6 all-gather.7
Sparse Core Ops, SparseCore 1:
  1078.5 225.5 all-gather.3
  1325.1 42.6 reduce-scatter.1
  1370.8 124.5 all-gather.5
  1500.5 83.5 all-reduce.3
where the time goes:
time: 1970 us
  other arithmetic  786 us (40%)
  waiting for transfers between devices  749 us (38%)
  matrix products  242 us (12%)
  local copies, waits for them, and re-layouts  148 us (8%)
  between operations  21.2 us (1%)
  loops' own time  20.9 us (1%)
    another operation x56, other arithmetic, advance(): factor = jnp.linalg.cholesky(mirror_lower(diag_block))  316 us
    all_gather x4, waiting for transfers between devices, advance(): gathered = lax.all_gather(column, 'front', axis=0, tiled=True)  275 us
    another operation x15, other arithmetic, solve_right(): jax.scipy.linalg.solve_triangular(lower_factor, matrix.T, lower=True)  251 us
    all_gather x1, waiting for transfers between devices, on_device(): lax.all_gather(landing_piece, 'front', axis=0, tiled=True)  226 us
    another operation x31, other arithmetic, parent_whole(): factor = jnp.linalg.cholesky(mirror_lower(pivot_block))  173 us
    another operation x71, matrix products, solve_right(): jax.scipy.linalg.solve_triangular(lower_factor, matrix.T, lower=True)  134 us
    all_gather x1, waiting for transfers between devices, parent_whole(): group_rows = lax.all_gather(assembled, 'front', axis=0, tiled=True)  125 us
    psum x1, waiting for transfers between devices, broadcast(): return lax.psum(kept, axis)  80.5 us
  transfers between devices with their start and end apart: 8, of which 8 were waited for; matrix products, arithmetic and copies ran while one was open for 1% of the time, Pallas kernels for 0%

commit v1 on v0

v1 whole, which is shorter than its diff:
```python
import functools

import jax
import jax.numpy as jnp
import numpy as np
from jax import lax
from jax.experimental import pallas as pl
from jax.experimental.pallas import tpu as pltpu
from jax.sharding import PartitionSpec as P

BLOCK = 128
STAGE = 512
CAP = 128
LANES = 128
SUB = 8
VMEM_LIMIT = 60 << 20

HIGHEST_PRECISION = lax.Precision.HIGHEST
NT = (((1,), (1,)), ((), ()))
NN = (((1,), (0,)), ((), ()))
F32 = jnp.float32
BF16 = jnp.bfloat16


def split(x):
    high = x.astype(BF16)
    return high, (x - high.astype(F32)).astype(BF16)


def dot(a, b, dims):
    return lax.dot_general(a, b, dims, preferred_element_type=F32)


def dot3(a, b, dims):
    return dot(a[0], b[0], dims) + (dot(a[0], b[1], dims) + dot(a[1], b[0], dims))


def ds(start, size):
    return pl.ds(pl.multiple_of(start, size), size)


def tiles(rows, cols, body, tile=256):
    tr, tc = min(tile, rows), min(tile, cols)
    nr, nc = rows // tr, cols // tc

    def step(t, carry):
        body((t // nc) * tr, tr, (t % nc) * tc, tc)
        return carry

    lax.fori_loop(0, nr * nc, step, 0)


def lane(x, c):
    return jnp.broadcast_to(x[:, c : c + 1], x.shape)


def sub(x, r):
    return jnp.broadcast_to(x[r : r + 1, :], x.shape)


def tree_sum(terms):
    terms = list(terms)
    while len(terms) > 1:
        terms = [
            terms[i] + terms[i + 1] if i + 1 < len(terms) else terms[i]
            for i in range(0, len(terms), 2)
        ]
    return terms[0]


def small_inverse_factor(s):
    n = len(s)
    s = [list(row) for row in s]
    low = [[None] * n for _ in range(n)]
    inv_diag = [None] * n
    for j in range(n):
        inv_diag[j] = lax.rsqrt(s[j][j])
        for i in range(j + 1, n):
            low[i][j] = s[i][j] * inv_diag[j]
        for i in range(j + 1, n):
            for k in range(j + 1, i + 1):
                s[i][k] = s[i][k] - low[i][j] * low[k][j]
    inv = [[None] * n for _ in range(n)]
    for j in range(n):
        inv[j][j] = inv_diag[j]
        for i in range(j + 1, n):
            inv[i][j] = -tree_sum(low[i][k] * inv[k][j] for k in range(j, i)) * inv_diag[i]
    return inv


def factor_block(rows):
    n = len(rows)
    row_id = lax.broadcasted_iota(jnp.int32, (SUB, LANES), 0)
    col_id = lax.broadcasted_iota(jnp.int32, (SUB, LANES), 1)
    a = list(rows)
    e = [jnp.where(row_id + SUB * s == col_id, 1.0, 0.0).astype(F32) for s in range(n)]
    out = []
    for s in range(n):
        cols = [lane(a[s], SUB * s + r) for r in range(SUB)]
        inv = small_inverse_factor([[sub(cols[j], i) for j in range(i + 1)] for i in range(SUB)])
        ra = [sub(a[s], r) for r in range(SUB)]
        re = [sub(e[s], r) for r in range(SUB)]
        ua = [tree_sum(inv[r][q] * ra[q] for q in range(r + 1)) for r in range(SUB)]
        ue = [tree_sum(inv[r][q] * re[q] for q in range(r + 1)) for r in range(SUB)]
        done = ue[0]
        for r in range(1, SUB):
            done = jnp.where(row_id == r, ue[r], done)
        out.append(done)
        if s + 1 == n:
            break
        ya = [tree_sum(inv[r][q] * ua[r] for r in range(q, SUB)) for q in range(SUB)]
        ye = [tree_sum(inv[r][q] * ue[r] for r in range(q, SUB)) for q in range(SUB)]
        for i in range(s + 1, n):
            w = [lane(a[i], SUB * s + r) for r in range(SUB)]
            a[i] = a[i] - tree_sum(w[r] * ya[r] for r in range(SUB))
            e[i] = e[i] - tree_sum(w[r] * ye[r] for r in range(SUB))
    return out


def subtract_products(dst, rows, cols, ah, al, bh, bl, depth):
    if depth == 0:
        return

    def body(r, nr, c, nc):
        a = (ah[ds(r, nr), :depth], al[ds(r, nr), :depth])
        b = (bh[ds(c, nc), :depth], bl[ds(c, nc), :depth])
        dst[ds(r, nr), ds(c, nc)] = dst[ds(r, nr), ds(c, nc)] - dot3(a, b, NT)

    tiles(rows, cols, body)


def times_inverse(src, outh, outl, out_at, rows, width, invh, invl):
    def body(r, nr, c, nc):
        a = split(src[ds(r, nr), :])
        b = (invh[ds(c, nc), :], invl[ds(c, nc), :])
        high, low = split(dot3(a, b, NT))
        outh[ds(r, nr), pl.ds(pl.multiple_of(out_at + c, nc), nc)] = high
        outl[ds(r, nr), pl.ds(pl.multiple_of(out_at + c, nc), nc)] = low

    tiles(rows, width, body)


def factor_diagonal(s_ref, at, width, lh, ll, invh, invl):
    invh[...] = jnp.zeros(invh.shape, BF16)
    invl[...] = jnp.zeros(invl.shape, BF16)
    row_id = lax.broadcasted_iota(jnp.int32, (width, LANES), 0)
    col_id = lax.broadcasted_iota(jnp.int32, (width, LANES), 1)
    wide_id = lax.broadcasted_iota(jnp.int32, (LANES, width), 1)

    def panel(p, carry):
        first = p * LANES
        here = ds(first, LANES)
        block = [
            s_ref[pl.ds(pl.multiple_of(first + SUB * i, SUB), SUB), here]
            for i in range(LANES // SUB)
        ]
        inv = jnp.concatenate(factor_block(block), axis=0)
        inv2 = split(inv)
        solved = dot3(split(s_ref[:, here]), inv2, NT)
        solved = jnp.where(row_id >= col_id + first, solved, 0.0)
        high, low = split(solved)
        lh[:, pl.ds(pl.multiple_of(at + first, LANES), LANES)] = high
        ll[:, pl.ds(pl.multiple_of(at + first, LANES), LANES)] = low
        below = row_id >= first + LANES
        bh = jnp.where(below, high, jnp.zeros_like(high))
        bl = jnp.where(below, low, jnp.zeros_like(low))

        def update(c, carry2):
            cols = ds(c * LANES, LANES)
            s_ref[:, cols] = s_ref[:, cols] - dot3(
                (bh, bl),
                (
                    jnp.where(c > p, lh[cols, pl.ds(pl.multiple_of(at + first, LANES), LANES)], 0),
                    jnp.where(c > p, ll[cols, pl.ds(pl.multiple_of(at + first, LANES), LANES)], 0),
                ),
                NT,
            )
            return carry2

        lax.fori_loop(p + 1, width // LANES, update, 0)
        left = wide_id < first
        rh = lh[here, at : at + width]
        rl = ll[here, at : at + width]
        rh = jnp.where(left, rh, jnp.zeros_like(rh))
        rl = jnp.where(left, rl, jnp.zeros_like(rl))
        mixed = dot3((rh, rl), (invh[...], invl[...]), NN)
        row = -dot3(inv2, split(mixed), NN)
        high, low = split(row)
        invh[here, :] = high
        invl[here, :] = low
        invh[here, here] = inv2[0]
        invl[here, here] = inv2[1]
        return carry

    lax.fori_loop(0, width // LANES, panel, 0)


def vmem_call(body, out_shapes, in_kinds, scratch, cost=None):
    specs = [pl.BlockSpec(memory_space=pltpu.SMEM if k else pltpu.VMEM) for k in in_kinds]
    return pl.pallas_call(
        body,
        out_shape=out_shapes,
        in_specs=specs,
        out_specs=[pl.BlockSpec(memory_space=pltpu.VMEM)] * len(out_shapes),
        scratch_shapes=scratch,
        compiler_params=pltpu.CompilerParams(vmem_limit_bytes=VMEM_LIMIT),
        cost_estimate=cost,
    )


def shaped(shape, dtype):
    return jax.ShapeDtypeStruct(shape, dtype)


def send_plan(groups, per_stage):
    pairs = [
        (j, i)
        for i in range(groups)
        for j in range(i)
        if not (i == j + 1 and j % 2 == 0)
    ]
    pairs.sort(key=lambda pair: (pair[1] // per_stage, pair))
    taken = {}

    def place(pair, limit, seen):
        for rnd in range(limit):
            for dev in (pair[1], pair[0]):
                slot = (rnd, dev)
                if slot in seen:
                    continue
                seen.add(slot)
                if slot not in taken or place(taken[slot], limit, seen):
                    taken[slot] = pair
                    return True
        return False

    limit = 1
    for pair in pairs:
        while not place(pair, limit, set()):
            limit += 1
    rounds = 1 + max((slot[0] for slot in taken), default=-1)
    table = np.full((max(rounds, 1), groups), -1, np.int32)
    for (rnd, dev), (j, i) in taken.items():
        table[rnd, dev] = j if dev == i else i
    return table[:rounds]


def ring_order(groups):
    return [i for i in range(0, groups, 2)] + [i for i in range(groups - 1, 0, -2)]


def ring_gather(chunk, axis, groups):
    order = ring_order(groups)
    ahead = [(order[i], order[(i + 1) % groups]) for i in range(groups)]
    back = [(b, a) for a, b in ahead]
    out = [chunk]
    going, coming = chunk, chunk
    steps_ahead = groups // 2
    steps_back = groups - 1 - steps_ahead
    aheads, backs = [], []
    for step in range(steps_ahead):
        going = lax.ppermute(going, axis, ahead)
        aheads.append(going)
        if step < steps_back:
            coming = lax.ppermute(coming, axis, back)
            backs.append(coming)
    return out + aheads + backs


def slot_owners(axis, groups):
    order = np.array(ring_order(groups), np.int32)
    place = np.argsort(order)
    me = jnp.asarray(place)[lax.axis_index(axis)]
    steps_ahead = groups // 2
    steps_back = groups - 1 - steps_ahead
    shifts = [0] + [-s for s in range(1, steps_ahead + 1)] + list(range(1, steps_back + 1))
    return jnp.asarray(order)[(me + jnp.asarray(shifts, jnp.int32)) % groups].astype(jnp.int32)


def bulk_gather(x, axis, size):
    me = lax.axis_index(axis)
    held = x[None]
    bits = size.bit_length() - 1
    for bit in range(bits - 1, -1, -1):
        step = 1 << bit
        other = lax.ppermute(held, axis, [(i, i ^ step) for i in range(size)])
        mine_high = (me >> bit) & 1
        held = jnp.where(
            mine_high == 1,
            jnp.concatenate([other, held], axis=0),
            jnp.concatenate([held, other], axis=0),
        )
    order = []
    for k in range(size):
        index = 0
        for bit in range(bits):
            if (k >> (bits - 1 - bit)) & 1:
                index |= 1 << bit
        order.append(index)
    back = np.argsort(np.array(order))
    return held, [int(v) for v in back]


def child_stage(q, width, own, groups, cap, chunk_counts, refs):
    per_stage = width // own
    refs = list(refs)

    def take(count):
        out, refs[:count] = refs[:count], []
        return out

    (owner_ref, table_ref, place_ref) = take(3)
    chunks = [take(count) for count in chunk_counts]
    prev_lh, prev_ll, prev_ih, prev_il, prev_xh, prev_xl = (take(q) for _ in range(6))
    (b_ref, pick_ref) = take(2)
    (lh, ll, invh, invl, xh, xl, top_ref, own_ref) = take(8)
    (a_ref, s_ref) = take(2)
    first_group = q * per_stage

    for k in range(groups):
        f = owner_ref[k]

        @pl.when(f // per_stage == q)
        def _(f=f, k=k):
            chunk = chunks[0][k]
            at = (f - first_group) * own
            a_ref[ds(at, own), ds(f * own, own)] = chunk[:, :own]
            half = own // 2
            odd = f % 2
            row = (f - odd + 1 - first_group) * own + odd * half
            a_ref[ds(row, half), ds((f - odd) * own, own)] = chunk[:, own:].T

    for rnd in range(1, len(chunks)):
        if not chunks[rnd]:
            continue
        for k in range(groups):
            f = owner_ref[k]
            c = table_ref[rnd - 1, f]
            high = jnp.maximum(f, c)
            low = jnp.minimum(f, c)
            mine = jnp.logical_and(c >= 0, high // per_stage == q)
            row = jnp.clip((high - first_group) * own, 0, width - own)
            col = jnp.clip(low * own, 0, (q + 1) * width - own)

            @pl.when(jnp.logical_and(mine, f > c))
            def _(rnd=rnd, k=k, row=row, col=col):
                a_ref[ds(row, own), ds(col, own)] = chunks[rnd][k][...]

            @pl.when(jnp.logical_and(mine, f < c))
            def _(rnd=rnd, k=k, row=row, col=col):
                a_ref[ds(row, own), ds(col, own)] = chunks[rnd][k][...].T

    for j in range(q):
        part = a_ref.at[:, j * width : (j + 1) * width]
        subtract_products(part, width, width, lh, ll, prev_lh[j], prev_ll[j], j * width)
        times_inverse(part, lh, ll, j * width, width, width, prev_ih[j], prev_il[j])
    s_ref[...] = a_ref[:, q * width : (q + 1) * width]
    subtract_products(s_ref, width, width, lh, ll, lh, ll, q * width)
    factor_diagonal(s_ref, q * width, width, lh, ll, invh, invl)

    rest = s_ref.at[:own, :]
    rest[...] = b_ref[...]
    for j in range(q):
        part = slice(j * width, (j + 1) * width)

        def body(r, nr, c, nc, j=j, part=part):
            a = (prev_xh[j][ds(r, nr), :], prev_xl[j][ds(r, nr), :])
            b = (lh[ds(c, nc), part], ll[ds(c, nc), part])
            rest[ds(r, nr), ds(c, nc)] = rest[ds(r, nr), ds(c, nc)] - dot3(a, b, NT)

        tiles(own, width, body)
    times_inverse(rest, xh, xl, 0, own, width, invh, invl)
    pick = pick_ref[...]
    top_ref[...] = dot(pick, xh[...], NN) + dot(pick, xl[...], NN)
    at = place_ref[0]
    own_ref[...] = lh[ds(at, own), :].astype(F32) + ll[ds(at, own), :].astype(F32)


def cross_kernel(stages, own, cap, sources, groups, refs):
    refs = list(refs)

    def take(count):
        out, refs[:count] = refs[:count], []
        return out

    (owner_ref,) = take(1)
    xh, xl = take(stages), take(stages)
    slots = [take(groups) for _ in range(stages)]
    con_ref, sq_ref = take(2)
    th, tl = take(2)
    width = xh[0].shape[1]
    total = sources * cap
    for k in range(groups):
        f = owner_ref[k]

        @pl.when(f < sources)
        def _(f=f, k=k):
            for q in range(stages):
                high, low = split(slots[q][k][...])
                th[ds(f * cap, cap), q * width : (q + 1) * width] = high
                tl[ds(f * cap, cap), q * width : (q + 1) * width] = low

    for c in range(total // LANES):
        rows = slice(c * LANES, (c + 1) * LANES)
        acc = jnp.zeros((own, LANES), F32)
        for q in range(stages):
            cols = slice(q * width, (q + 1) * width)
            acc = acc + dot3((xh[q][...], xl[q][...]), (th[rows, cols], tl[rows, cols]), NT)
        con_ref[:, rows] = acc

    def square(t, carry):
        i = carry[0]
        j = carry[1]
        a = (th[ds(i * LANES, LANES), :], tl[ds(i * LANES, LANES), :])
        b = (th[ds(j * LANES, LANES), :], tl[ds(j * LANES, LANES), :])
        sq_ref[t] = dot3(a, b, NT)
        end = j == i
        return (jnp.where(end, i + 1, i), jnp.where(end, 0, j + 1))

    blocks = total // LANES
    lax.fori_loop(0, blocks * (blocks + 1) // 2, square, (jnp.int32(0), jnp.int32(0)))


def parent_kernel(children, blocks, width, refs):
    top_ref, spread_ref, sq_ref, lh, ll, invh, invl, lower, s_ref = refs
    pivots = top_ref.shape[0]
    dense = pivots // blocks
    for i in range(blocks):
        for j in range(i + 1):
            at = i * (i + 1) // 2 + j
            parts = []
            for c in range(children):
                left = spread_ref[i, :, c * LANES : (c + 1) * LANES]
                high, low = split(sq_ref[c, at])
                parts.append(dot(left, high, NN) + dot(left, low, NN))
            high, low = split(jnp.concatenate(parts, axis=1))
            right = spread_ref[j]
            rows = slice(i * dense, (i + 1) * dense)
            cols = slice(j * dense, (j + 1) * dense)
            s_ref[rows, cols] = top_ref[rows, cols] - (
                dot(high, right, NT) + dot(low, right, NT)
            )
    for q in range(pivots // width):
        rows = slice(q * width, (q + 1) * width)
        lhq, llq = lh.at[rows, :], ll.at[rows, :]
        if q + 1 < pivots // width:
            lhq[:, (q + 1) * width :] = jnp.zeros((width, pivots - (q + 1) * width), BF16)
            llq[:, (q + 1) * width :] = jnp.zeros((width, pivots - (q + 1) * width), BF16)
        for j in range(q):
            part = s_ref.at[rows, j * width : (j + 1) * width]
            cut = slice(j * width, (j + 1) * width)
            subtract_products(part, width, width, lhq, llq, lh.at[cut, :], ll.at[cut, :], j * width)
            times_inverse(part, lhq, llq, j * width, width, width, invh.at[j], invl.at[j])
        part = s_ref.at[rows, q * width : (q + 1) * width]
        subtract_products(part, width, width, lhq, llq, lhq, llq, q * width)
        factor_diagonal(part, q * width, width, lhq, llq, invh.at[q], invl.at[q])
    lower[...] = lh[...].astype(F32) + ll[...].astype(F32)


def rest_kernel(children, blocks, width, refs):
    place_ref, rows_ref, route_ref, con_ref, spread_ref, lh, ll, invh, invl, out_ref, s_ref, xh, xl = refs
    pivots = lh.shape[0]
    own = con_ref.shape[1]
    count = rows_ref.shape[0]
    dense = pivots // blocks
    at = place_ref[1]

    @pl.when(at < pivots)
    def _():
        row = ds(jnp.minimum(at, pivots - count), count)
        out_ref[...] = lh[row, :].astype(F32) + ll[row, :].astype(F32)

    @pl.when(at >= pivots)
    def _():
        routed = []
        for c in range(children):
            high, low = split(con_ref[c])
            route = route_ref[c]
            routed.append(split(dot(route, high, NN) + dot(route, low, NN)))
        for b in range(blocks):
            lanes = slice(b * LANES, (b + 1) * LANES)
            high = jnp.concatenate([routed[c][0][:, lanes] for c in range(children)], axis=1)
            low = jnp.concatenate([routed[c][1][:, lanes] for c in range(children)], axis=1)
            right = spread_ref[b]
            cols = slice(b * dense, (b + 1) * dense)
            s_ref[:, cols] = rows_ref[:, cols] - (dot(high, right, NT) + dot(low, right, NT))
        for q in range(pivots // width):
            cut = slice(q * width, (q + 1) * width)
            part = s_ref.at[:, cut]
            subtract_products(part, count, width, xh, xl, lh.at[cut, :], ll.at[cut, :], q * width)
            times_inverse(part, xh, xl, q * width, count, width, invh.at[q], invl.at[q])
        out_ref[...] = xh[...].astype(F32) + xl[...].astype(F32)


def on_device(child_pivot, child_coupling, parent_arrow, row_map, block_pattern):
    front = lax.axis_size("front")
    bulk = lax.axis_size("bulk")
    me = lax.axis_index("front")
    mine = child_pivot[0]
    coupling = child_coupling[0]
    own, total = mine.shape
    count, pivots = parent_arrow.shape
    width = min(STAGE, total)
    stages = total // width
    per_stage = width // own
    first_row = (lax.axis_index("bulk") * front + me) * count
    sources = pivots // count
    cap = min(CAP, count, own)
    blocks = sources * cap // LANES

    maps = lax.all_gather(row_map[0], ("bulk", "front"), axis=0).reshape(bulk, front, own)
    lands = maps[:, :sources] < pivots
    rank = jnp.cumsum(lands.astype(jnp.int32), axis=2) - 1
    overflow = jnp.any(rank[:, :, -1] >= cap)
    chosen = jnp.where(lands[:, :, None, :], rank[:, :, None, :], -1) == jnp.arange(cap)[:, None]
    target = jnp.max(jnp.where(chosen, maps[:, :sources, None, :], -1), axis=3)
    target = jnp.where(overflow, -1, target).reshape(bulk, blocks, LANES)
    dense = pivots // blocks
    rows_of = (jnp.arange(blocks)[:, None] * dense + jnp.arange(dense)[None, :])[:, :, None, None]
    spread = (jnp.transpose(target, (1, 0, 2))[:, None] == rows_of).astype(BF16)
    spread = spread.reshape(blocks, dense, bulk * LANES)
    own_map = row_map[0]
    own_rank = jnp.where(own_map < pivots, jnp.cumsum((own_map < pivots).astype(jnp.int32)) - 1, -1)
    pick = (own_rank[None, :] == jnp.arange(cap)[:, None]).astype(BF16)
    route = (
        lax.dynamic_index_in_dim(maps, me, 1, False)[:, None, :]
        == (first_row + jnp.arange(count))[None, :, None]
    ).astype(BF16)

    table = send_plan(front, per_stage)
    half = own // 2
    own_block = lax.dynamic_slice_in_dim(mine, me * own, own, 1)
    even = lax.dynamic_slice_in_dim(mine, jnp.minimum(me + 1, front - 1) * own, half, 1)
    odd = lax.dynamic_slice_in_dim(mine[half:], jnp.maximum(me - 1, 0) * own, own, 1).T
    chunks = [jnp.concatenate([own_block, jnp.where(me % 2 == 0, even, odd)], axis=1)]
    for rnd in range(table.shape[0]):
        col = jnp.maximum(jnp.asarray(table[rnd])[me], 0)
        chunks.append(lax.dynamic_slice_in_dim(mine, col * own, own, 1))
    owners = slot_owners("front", front)
    gathered = [ring_gather(chunk, "front", front) for chunk in chunks]
    table_in = jnp.asarray(table if table.shape[0] else np.zeros((1, front), np.int32))
    place = jnp.stack([(me % per_stage) * own, first_row]).astype(jnp.int32)

    lh, ll, ih, il, xh, xl, tops, owned = ([] for _ in range(8))
    for q in range(stages):
        used = [gathered[0]]
        for rnd in range(table.shape[0]):
            needed = any(
                c >= 0 and max(f, c) // per_stage == q for f, c in enumerate(table[rnd])
            )
            used.append(gathered[rnd + 1] if needed else [])
        counts = [len(u) for u in used]
        flat = [x for u in used for x in u]
        operands = (
            [owners, table_in, place]
            + flat
            + lh + ll + ih + il + xh + xl
            + [coupling[:, q * width : (q + 1) * width], pick]
        )
        deep = (q + 1) * width
        out = vmem_call(
            functools.partial(
                lambda *refs, q, counts: child_stage(q, width, own, front, cap, counts, refs),
                q=q,
                counts=counts,
            ),
            [
                shaped((width, deep), BF16),
                shaped((width, deep), BF16),
                shaped((width, width), BF16),
                shaped((width, width), BF16),
                shaped((own, width), BF16),
                shaped((own, width), BF16),
                shaped((cap, width), F32),
                shaped((own, deep), F32),
            ],
            [True] * 3 + [False] * (len(operands) - 3),
            [pltpu.VMEM((width, deep), F32), pltpu.VMEM((width, width), F32)],
        )(*operands)
        for held, new in zip((lh, ll, ih, il, xh, xl, tops, owned), out, strict=True):
            held.append(new)

    x_own = jnp.concatenate([h.astype(F32) + l.astype(F32) for h, l in zip(xh, xl, strict=True)], axis=1)
    lower_rows = jnp.zeros((own, total), F32)
    for q in range(stages):
        padded = jnp.pad(owned[q], ((0, 0), (0, total - (q + 1) * width)))
        lower_rows = jnp.where(me // per_stage == q, padded, lower_rows)

    slots = [x for top in tops for x in ring_gather(top, "front", front)]
    con, squares = vmem_call(
        lambda *refs: cross_kernel(stages, own, cap, sources, front, refs),
        [
            shaped((own, sources * cap), F32),
            shaped((blocks * (blocks + 1) // 2, LANES, LANES), F32),
        ],
        [True] + [False] * (2 * stages + len(slots)),
        [pltpu.VMEM((sources * cap, total), BF16)] * 2,
    )(owners, *xh, *xl, *slots)

    block_rows = (first_row + jnp.arange(count)) // BLOCK
    row_mask = jnp.take(block_pattern, block_rows, axis=0).astype(F32)
    arrow = parent_arrow * jnp.repeat(row_mask, BLOCK, axis=1)
    piece = count // bulk
    part = arrow[:piece]
    for g in range(1, bulk):
        moved = lax.ppermute(arrow[g * piece : (g + 1) * piece], "bulk", [(0, g)])
        part = jnp.where(lax.axis_index("bulk") == g, moved, part)
    ring = ring_gather(part, "front", front)
    line = jnp.zeros((front, piece, pivots), F32)
    for k, value in enumerate(ring):
        line = lax.dynamic_update_index_in_dim(line, value, owners[k], 0)
    held, back = bulk_gather(line[:sources], "bulk", bulk)
    top = jnp.stack([held[b] for b in back], axis=1).reshape(pivots, pivots)

    def unchanged(top, arrow, x_own):
        return top, arrow

    def landing_whole(top, arrow, x_own):
        slot = own_map - me * count
        hits = (slot[:, None] == jnp.arange(count)[None, :]).astype(F32)
        piece_rows = jnp.dot(hits.T, x_own, precision=HIGHEST_PRECISION)
        whole = lax.all_gather(piece_rows, "front", axis=0, tiled=True)[:pivots]
        reached = jnp.dot(x_own, whole.T, precision=HIGHEST_PRECISION)
        slot_index = own_map // count // front * count + own_map % count
        routing = (slot_index[:, None] == jnp.arange(bulk * count)[None, :]).astype(F32)
        added = lax.psum_scatter(
            jnp.dot(routing.T, reached, precision=HIGHEST_PRECISION),
            "bulk",
            scatter_dimension=0,
            tiled=True,
        )
        whole_square = lax.psum(jnp.dot(whole, whole.T, precision=HIGHEST_PRECISION), "bulk")
        return top - whole_square, arrow - added

    top, arrow = lax.cond(overflow, landing_whole, unchanged, top, arrow, x_own)

    held, back = bulk_gather(squares, "bulk", bulk)
    sq_all = jnp.stack([held[b] for b in back], axis=0)
    plh, pll, pih, pil, plow = vmem_call(
        lambda *refs: parent_kernel(bulk, blocks, width, refs),
        [
            shaped((pivots, pivots), BF16),
            shaped((pivots, pivots), BF16),
            shaped((pivots // width, width, width), BF16),
            shaped((pivots // width, width, width), BF16),
            shaped((pivots, pivots), F32),
        ],
        [False] * 3,
        [pltpu.VMEM((pivots, pivots), F32)],
    )(top, spread, sq_all)

    held, back = bulk_gather(con, "bulk", bulk)
    con_all = jnp.stack([held[b] for b in back], axis=0)
    (parent_rows,) = vmem_call(
        lambda *refs: rest_kernel(bulk, blocks, width, refs),
        [shaped((count, pivots), F32)],
        [True] + [False] * 8,
        [
            pltpu.VMEM((count, pivots), F32),
            pltpu.VMEM((count, pivots), BF16),
            pltpu.VMEM((count, pivots), BF16),
        ],
    )(place, arrow, route, con_all, spread, plh, pll, pih, pil)
    return (lower_rows[None], x_own[None], parent_rows)


def solution(mesh):
    placed = (
        P("bulk", "front", None),
        P("bulk", "front", None),
        P(("bulk", "front"), None),
        P("bulk", "front"),
        P(),
    )
    return jax.shard_map(
        on_device,
        mesh=mesh,
        in_specs=placed,
        out_specs=(P("bulk", "front", None), P("bulk", "front", None), P(("bulk", "front"), None)),
        check_vma=False,
    )
```

time: 1970 us -> 611 us (0.31)
  other arithmetic: 786 us -> 36.9 us
  waiting for transfers between devices: 749 us -> 115 us
  Pallas kernels: 0 us -> 251 us
  matrix products: 242 us -> 0 us
  local copies, waits for them, and re-layouts: 148 us -> 32.2 us
  blocking collectives: 0 us -> 66.9 us
  starting transfers between devices: 0.35 us -> 63.2 us
    another operation x102 -> x9, other arithmetic: 740 us -> 11.3 us  [the longest x56 316 us: advance(): factor = jnp.linalg.cholesky(mirror_lower(diag_block))]
    all_gather x6 -> x0, waiting for transfers between devices: 625 us -> none  [the longest x4 275 us: advance(): gathered = lax.all_gather(column, 'front', axis=0, tiled=True)]
    pallas_call x0 -> x7, Pallas kernels: none -> 251 us  [the longest x4 164 us: on_device(): vmem_call(functools.partial(lambda *refs, q, counts: child_stage(q, width...]
    another operation x109 -> x0, matrix products: 164 us -> none  [the longest x71 134 us: solve_right(): jax.scipy.linalg.solve_triangular(lower_factor, matrix.T, lower=True)]
    ppermute x0 -> x72, waiting for transfers between devices: none -> 115 us  [the longest x36 72.7 us: ring_gather(): going = lax.ppermute(going, axis, ahead)]
    psum x1 -> x0, waiting for transfers between devices: 80.5 us -> none  [broadcast(): return lax.psum(kept, axis)]
    dot_general x12 -> x0, matrix products: 78.4 us -> none  [the longest x4 27 us: advance(): jnp.dot(own_factor, trailing.T, precision=HIGHEST_PRECISION)]
    another operation x108 -> x7, local copies, waits for them, and re-layouts: 72.4 us -> 1 us  [the longest x1 0.53 us: on_device(): top = jnp.stack([held[b] for b in back], axis=1).reshape(pivots, pivots)]
  transfers between devices with their start and end apart: 8 -> 72, of which waited for: 8 -> 32; matrix products, arithmetic and copies ran while one was open for 1% -> 9% of each run, Pallas kernels for 0% -> 30%
where the time goes in v1:
time: 611 us; the launch traced here: 601 us
  Pallas kernels  251 us (41%)
  waiting for transfers between devices  115 us (19%)
  blocking collectives  66.9 us (11%)
  starting transfers between devices  63.2 us (10%)
  other arithmetic  36.9 us (6%)
  between operations  32.7 us (5%)
  local copies, waits for them, and re-layouts  32.2 us (5%)
    pallas_call x4, Pallas kernels, on_device(): vmem_call(functools.partial(lambda *refs, q, counts: child_stage(q, width...  164 us
    ppermute x36, waiting for transfers between devices, ring_gather(): going = lax.ppermute(going, axis, ahead)  72.7 us
    all_gather x1, blocking collectives, on_device(): lax.all_gather(row_map[0], ('bulk', 'front'), axis=0)  66.9 us
    pallas_call x1, Pallas kernels, on_device(): vmem_call(lambda *refs: parent_kernel(bulk, blocks, width, refs), [shaped...  63.6 us
    ppermute x27, starting transfers between devices, ring_gather(): coming = lax.ppermute(coming, axis, back)  48.3 us
    ppermute x6, waiting for transfers between devices, bulk_gather(): other = lax.ppermute(held, axis, [(i, i ^ step) for i in range(size)])  19.3 us
    ppermute x27, waiting for transfers between devices, ring_gather(): coming = lax.ppermute(coming, axis, back)  19.2 us
    pallas_call x1, Pallas kernels, on_device(): vmem_call(lambda *refs: cross_kernel(stages, own, cap, sources, front, re...  14.8 us
  transfers between devices with their start and end apart: 72, of which 32 were waited for; matrix products, arithmetic and copies ran while one was open for 9% of the time, Pallas kernels for 30%

profile of v1, /device:TPU:20, one launch (start us, length us, event | category | flops | bytes accessed | tf_op | source)
XLA Modules:
  0.0 601.4 jit_solution(11619850310146783477)
XLA Ops:
  22.4 66.9 %all-gather = s32[32,1,256]{2,1,0:T(1,128)S(1)} all-gather(s32[1,1,256]{2,1,0:T(1,128)S(1)} %bitcast.105), channel_id=1, replica_groups=mesh['bulk'=4,'front'=8] {'bulk','front'}, dimensions={0}, use_global_device_ids=true | all-gather | bytes 33792 | tf_op jit(solution)/shard_map/all_gather | solution.py:511
  89.3 4.8 reduce-window.19
  100.4 3.3 collective-permute-start.25
  104.8 3.3 collective-permute-start.4
  114.0 3.3 collective-permute-done.29
  135.6 12.7 %collective-permute-done.22.refs_13_.refs_29_ = f32[256,256]{1,0:T(8,128)S(1)} collective-permute-done((f32[256,256]{1,0:T(8,128)}, f32[256,256]{1,0:T(8,128)S(1)}, u32[]{:S(2)}, u32[]{:S(2)}) %collective-permute-start.22) | collective-permute-done | bytes 262176 | tf_op jit(solution)/shard_map/ppermute | solution.py:262
  153.3 4.3 collective-permute-done.9.refs_14_
  159.7 3.5 collective-permute-done.16.refs_22_
  163.5 2.9 collective-permute-done.5.refs_9_
  168.2 3.4 collective-permute-done.2.refs_6_
  172.6 4.6 collective-permute-done.23.refs_14_.refs_30_
  179.9 2.9 collective-permute-done.32
  183.0 2.9 fusion.23
  187.8 9.0 %collective-permute-done.24.refs_15_.refs_31_ = f32[256,256]{1,0:T(8,128)S(1)} collective-permute-done((f32[256,256]{1,0:T(8,128)S(1)}, f32[256,256]{1,0:T(8,128)S(1)}, u32[]{:S(2)}, u32[]{:S(2)}) %collective-permute-start.24) | collective-permute-done | bytes 262176 | tf_op jit(solution)/shard_map/ppermute | solution.py:262
  197.1 5.5 collective-permute-done.33
  220.8 29.8 %shard_map.139 = (bf16[512,512]{1,0:T(8,128)(2,1)}, bf16[512,512]{1,0:T(8,128)(2,1)}, bf16[512,512]{1,0:T(8,128)(2,1)}, bf16[512,512]{1,0:T(8,128)(2,1)}, bf16[2...) custom-call(s32[8]{0:T(128)} %copy-done.62, ...), custom_call_target="tpu_custom_call" | custom-call | tf_op jit(solution)/shard_map/pallas_call | solution.py:561
  250.6 36.4 %shard_map.140 = (bf16[512,1024]{1,0:T(8,128)(2,1)}, bf16[512,1024]{1,0:T(8,128)(2,1)}, bf16[512,512]{1,0:T(8,128)(2,1)}, bf16[512,512]{1,0:T(8,128)(2,1)}, bf16...) custom-call(s32[8]{0:T(128)} %copy-done.62, ...), custom_call_target="tpu_custom_call" | custom-call | tf_op jit(solution)/shard_map/pallas_call | solution.py:561
  289.9 45.1 %shard_map.141 = (bf16[512,1536]{1,0:T(8,128)(2,1)}, bf16[512,1536]{1,0:T(8,128)(2,1)}, bf16[512,512]{1,0:T(8,128)(2,1)}, bf16[512,512]{1,0:T(8,128)(2,1)}, bf16...) custom-call(s32[8]{0:T(128)} %copy-done.62, ...), custom_call_target="tpu_custom_call" | custom-call | tf_op jit(solution)/shard_map/pallas_call | solution.py:561
  339.0 52.8 %shard_map.142 = (bf16[512,2048]{1,0:T(8,128)(2,1)}, bf16[512,2048]{1,0:T(8,128)(2,1)}, bf16[512,512]{1,0:T(8,128)(2,1)}, bf16[512,512]{1,0:T(8,128)(2,1)}, bf16...) custom-call(s32[8]{0:T(128)} %copy-done.62, ...), custom_call_target="tpu_custom_call" | custom-call | tf_op jit(solution)/shard_map/pallas_call | solution.py:561
  431.6 3.3 collective-permute-done.46.refs_16_
  437.2 3.3 collective-permute-done.53.refs_24_
  444.2 4.0 collective-permute-done.63.refs_36_
  453.8 5.1 collective-permute-done.50.refs_21_
  458.9 2.8 collective-permute-done.57.refs_29_
  461.8 2.8 collective-permute-done.64.refs_37_
  464.6 14.8 %shard_map.143 = (f32[256,512]{1,0:T(8,128)}, f32[10,128,128]{2,1,0:T(8,128)}) custom-call(s32[8]{0:T(128)} %copy-done.62, bf16[256,512]{1,0:T(8,128)(2,1)} %get-tuple-element.63.refs_23_.refs_43_.refs_47_.refs_1_, bf16[256,512]{1,0:T(8,128)(2,1)} %get-tuple-element.69.refs_44_.refs_48_.refs_2_, bf16[256,512]{1,0:T(8,128)(2,1)} %get-tuple-element.75.refs_49_.refs_3_, ...), custom_call_target="tpu_custom_call" | custom-call | tf_op jit(solution)/shard_map/pallas_call | solution.py:590
  481.8 7.1 %collective-permute-done.68 = f32[1,256,512]{2,1,0:T(8,128)S(1)} collective-permute-done((f32[1,256,512]{2,1,0:T(8,128)}, f32[1,256,512]{2,1,0:T(8,128)S(1)}, u32[]{:S(2)}, u32[]{:S(2)}) %collective-permute-start.68) | collective-permute-done | bytes 524320 | tf_op jit(solution)/shard_map/ppermute | solution.py:286
  494.2 12.2 %collective-permute-done.70 = f32[1,10,128,128]{3,2,1,0:T(8,128)S(1)} collective-permute-done((f32[1,10,128,128]{3,2,1,0:T(8,128)S(1)}, f32[1,10,128,128]{3,2,1,0:T(8,128)S(1)}, u32[]{:S(2)}, u32[]{:S(2)}) %collective-permute-start.70) | collective-permute-done | bytes 655392 | tf_op jit(solution)/shard_map/ppermute | solution.py:286
  513.3 3.6 conditional.1
  516.9 3.0 maximum_select_fusion.1
  521.9 63.6 %shard_map.144 = (bf16[1024,1024]{1,0:T(8,128)(2,1)}, bf16[1024,1024]{1,0:T(8,128)(2,1)}, bf16[2,512,512]{2,1,0:T(8,128)(2,1)}, bf16[2,512,512]{2,1,0:T(8,128)(2,1)}, f32[1024,1024]{1,0:T(8,128)}) custom-call(f32[1024,1024]{1,0:T(8,128)} %get-tuple-element.89.refs_0_, bf16[4,256,512]{2,1,0:T(8,128)(2,1)} %compare_convert_fusion.refs_1_.refs_4_, ...), custom_call_target="tpu_custom_call" | custom-call | tf_op jit(solution)/shard_map/pallas_call | solution.py:639
  585.5 8.8 %shard_map.145 = f32[256,1024]{1,0:T(8,128)} custom-call(s32[2]{0:T(128)} %pad_add_fusion.refs_2_.refs_0_, f32[256,1024]{1,0:T(8,128)S(1)} %get-tuple-element.83.refs_1_, bf16[4,256,256]{2,1,0:T(8,128)(2,1)} %compare_convert_fusion.1.refs_2_, f32[4,256,512]{2,1,0:T(8,128)} %pad_maximum_fusion.3.refs_3_, ...), custom_call_target="tpu_custom_call" | custom-call | tf_op jit(solution)/shard_map/pallas_call | solution.py:654
  (344 shorter events, 136.8 us)
Async XLA Ops:
  14.9 85.4 %collective-permute-start.7 = (f32[256,256]{1,0:T(8,128)S(1)}, f32[256,256]{1,0:T(8,128)S(1)}, u32[]{:S(2)}, u32[]{:S(2)}) collective-permute-start(f32[256,256]{1,0:T(8,128)S(1)} %get-tuple-element.120.refs_11_), channel_id=1, source_target_pairs={{0,2},{2,4},{4,6},{6,7},{7,5},{5,3},{3,1},{1,0},{8,10},{10,12},{12... | collective-permute-start | bytes 786440 | tf_op jit(solution)/shard_map/ppermute | solution.py:262
  16.5 88.2 %collective-permute-start.11 = (f32[256,256]{1,0:T(8,128)S(1)}, f32[256,256]{1,0:T(8,128)}, u32[]{:S(2)}, u32[]{:S(2)}) collective-permute-start(f32[256,256]{1,0:T(8,128)S(1)} %get-tuple-element.120.refs_11_), channel_id=1, source_target_pairs={{2,0},{4,2},{6,4},{7,6},{5,7},{3,5},{1,3},{0,1},{10,8},{12,10},{14... | collective-permute-start | bytes 786440 | tf_op jit(solution)/shard_map/ppermute | solution.py:265
  17.0 87.8 %collective-permute-start.14 = (f32[256,256]{1,0:T(8,128)}, f32[256,256]{1,0:T(8,128)}, u32[]{:S(2)}, u32[]{:S(2)}) collective-permute-start(f32[256,256]{1,0:T(8,128)} %get-tuple-element.122.refs_19_), channel_id=1, source_target_pairs={{0,2},{2,4},{4,6},{6,7},{7,5},{5,3},{3,1},{1,0},{8,10},{10,12},{12... | collective-permute-start | bytes 786440 | tf_op jit(solution)/shard_map/ppermute | solution.py:262
  18.5 89.6 %collective-permute-start.18 = (f32[256,256]{1,0:T(8,128)}, f32[256,256]{1,0:T(8,128)}, u32[]{:S(2)}, u32[]{:S(2)}) collective-permute-start(f32[256,256]{1,0:T(8,128)} %get-tuple-element.122.refs_19_), channel_id=1, source_target_pairs={{2,0},{4,2},{6,4},{7,6},{5,7},{3,5},{1,3},{0,1},{10,8},{12,10},{14... | collective-permute-start | bytes 786440 | tf_op jit(solution)/shard_map/ppermute | solution.py:265
  19.0 89.8 %collective-permute-start.21 = (f32[256,256]{1,0:T(8,128)S(1)}, f32[256,256]{1,0:T(8,128)}, u32[]{:S(2)}, u32[]{:S(2)}) collective-permute-start(f32[256,256]{1,0:T(8,128)S(1)} %get-tuple-element.119.refs_11_.refs_27_), channel_id=1, source_target_pairs={{0,2},{2,4},{4,6},{6,7},{7,5},{5,3},{3,1},{1,0},{8,10},{10,12},{12... | collective-permute-start | bytes 786440 | tf_op jit(solution)/shard_map/ppermute | solution.py:262
  104.7 18.7 %collective-permute-start = (f32[256,384]{1,0:T(8,128)S(1)}, f32[256,384]{1,0:T(8,128)S(1)}, u32[]{:S(2)}, u32[]{:S(2)}) collective-permute-start(f32[256,384]{1,0:T(8,128)S(1)} %pad_maximum_fusion.4.refs_3_), channel_id=1, source_target_pairs={{0,2},{2,4},{4,6},{6,7},{7,5},{5,3},{3,1},{1,0},{8,10},{10,12},{12... | collective-permute-start | bytes 1179656 | tf_op jit(solution)/shard_map/ppermute | solution.py:262
  104.8 20.7 %collective-permute-start.4 = (f32[256,384]{1,0:T(8,128)S(1)}, f32[256,384]{1,0:T(8,128)S(1)}, u32[]{:S(2)}, u32[]{:S(2)}) collective-permute-start(f32[256,384]{1,0:T(8,128)S(1)} %pad_maximum_fusion.4.refs_3_), channel_id=1, source_target_pairs={{2,0},{4,2},{6,4},{7,6},{5,7},{3,5},{1,3},{0,1},{10,8},{12,10},{14... | collective-permute-start | bytes 1179656 | tf_op jit(solution)/shard_map/ppermute | solution.py:265
  125.5 26.9 %collective-permute-start.1 = (f32[256,384]{1,0:T(8,128)S(1)}, f32[256,384]{1,0:T(8,128)S(1)}, u32[]{:S(2)}, u32[]{:S(2)}) collective-permute-start(f32[256,384]{1,0:T(8,128)S(1)} %collective-permute-done.refs_4_), channel_id=1, source_target_pairs={{0,2},{2,4},{4,6},{6,7},{7,5},{5,3},{3,1},{1,0},{8,10},{10,12},{12... | collective-permute-start | bytes 1179656 | tf_op jit(solution)/shard_map/ppermute | solution.py:262
  129.6 20.7 %collective-permute-start.31 = (f32[64,1024]{1,0:T(8,128)}, f32[64,1024]{1,0:T(8,128)}, u32[]{:S(2)}, u32[]{:S(2)}) collective-permute-start(f32[64,1024]{1,0:T(8,128)} %get-tuple-element.96), channel_id=1, source_target_pairs={{0,2},{2,4},{4,6},{6,7},{7,5},{5,3},{3,1},{1,0},{8,10},{10,12},{12... | collective-permute-start | bytes 786440 | tf_op jit(solution)/shard_map/ppermute | solution.py:262
  129.7 18.6 %collective-permute-start.22 = (f32[256,256]{1,0:T(8,128)}, f32[256,256]{1,0:T(8,128)S(1)}, u32[]{:S(2)}, u32[]{:S(2)}) collective-permute-start(f32[256,256]{1,0:T(8,128)} %collective-permute-done.21.refs_12_.refs_28_), channel_id=1, source_target_pairs={{0,2},{2,4},{4,6},{6,7},{7,5},{5,3},{3,1},{1,0},{8,10},{10,12},{12... | collective-permute-start | bytes 786440 | tf_op jit(solution)/shard_map/ppermute | solution.py:262
  130.4 18.1 %collective-permute-start.26 = (f32[256,256]{1,0:T(8,128)S(1)}, f32[256,256]{1,0:T(8,128)S(1)}, u32[]{:S(2)}, u32[]{:S(2)}) collective-permute-start(f32[256,256]{1,0:T(8,128)S(1)} %collective-permute-done.25.refs_16_.refs_32_), channel_id=1, source_target_pairs={{2,0},{4,2},{6,4},{7,6},{5,7},{3,5},{1,3},{0,1},{10,8},{12,10},{14... | collective-permute-start | bytes 786440 | tf_op jit(solution)/shard_map/ppermute | solution.py:265
  133.1 17.5 %collective-permute-start.35 = (f32[64,1024]{1,0:T(8,128)}, f32[64,1024]{1,0:T(8,128)}, u32[]{:S(2)}, u32[]{:S(2)}) collective-permute-start(f32[64,1024]{1,0:T(8,128)} %get-tuple-element.96), channel_id=1, source_target_pairs={{2,0},{4,2},{6,4},{7,6},{5,7},{3,5},{1,3},{0,1},{10,8},{12,10},{14... | collective-permute-start | bytes 786440 | tf_op jit(solution)/shard_map/ppermute | solution.py:265
  152.3 19.2 %collective-permute-start.2 = (f32[256,384]{1,0:T(8,128)S(1)}, f32[256,384]{1,0:T(8,128)S(1)}, u32[]{:S(2)}, u32[]{:S(2)}) collective-permute-start(f32[256,384]{1,0:T(8,128)S(1)} %collective-permute-done.1.refs_5_), channel_id=1, source_target_pairs={{0,2},{2,4},{4,6},{6,7},{7,5},{5,3},{3,1},{1,0},{8,10},{10,12},{12... | collective-permute-start | bytes 1179656 | tf_op jit(solution)/shard_map/ppermute | solution.py:262
  157.6 19.6 %collective-permute-start.23 = (f32[256,256]{1,0:T(8,128)S(1)}, f32[256,256]{1,0:T(8,128)S(1)}, u32[]{:S(2)}, u32[]{:S(2)}) collective-permute-start(f32[256,256]{1,0:T(8,128)S(1)} %collective-permute-done.22.refs_13_.refs_29_), channel_id=1, source_target_pairs={{0,2},{2,4},{4,6},{6,7},{7,5},{5,3},{3,1},{1,0},{8,10},{10,12},{12... | collective-permute-start | bytes 786440 | tf_op jit(solution)/shard_map/ppermute | solution.py:262
  158.0 20.8 %collective-permute-start.27 = (f32[256,256]{1,0:T(8,128)S(1)}, f32[256,256]{1,0:T(8,128)S(1)}, u32[]{:S(2)}, u32[]{:S(2)}) collective-permute-start(f32[256,256]{1,0:T(8,128)S(1)} %collective-permute-done.26.refs_17_.refs_33_), channel_id=1, source_target_pairs={{2,0},{4,2},{6,4},{7,6},{5,7},{3,5},{1,3},{0,1},{10,8},{12,10},{14... | collective-permute-start | bytes 786440 | tf_op jit(solution)/shard_map/ppermute | solution.py:265
  163.2 19.6 %collective-permute-start.32 = (f32[64,1024]{1,0:T(8,128)}, f32[64,1024]{1,0:T(8,128)S(1)}, u32[]{:S(2)}, u32[]{:S(2)}) collective-permute-start(f32[64,1024]{1,0:T(8,128)} %collective-permute-done.31), channel_id=1, source_target_pairs={{0,2},{2,4},{4,6},{6,7},{7,5},{5,3},{3,1},{1,0},{8,10},{10,12},{12... | collective-permute-start | bytes 786440 | tf_op jit(solution)/shard_map/ppermute | solution.py:262
  166.4 36.4 %collective-permute-start.6 = (f32[256,384]{1,0:T(8,128)S(1)}, f32[256,384]{1,0:T(8,128)S(1)}, u32[]{:S(2)}, u32[]{:S(2)}) collective-permute-start(f32[256,384]{1,0:T(8,128)S(1)} %collective-permute-done.5.refs_9_), channel_id=1, source_target_pairs={{2,0},{4,2},{6,4},{7,6},{5,7},{3,5},{1,3},{0,1},{10,8},{12,10},{14... | collective-permute-start | bytes 1179656 | tf_op jit(solution)/shard_map/ppermute | solution.py:265
  171.5 33.0 %collective-permute-start.3 = (f32[256,384]{1,0:T(8,128)S(1)}, f32[256,384]{1,0:T(8,128)S(1)}, u32[]{:S(2)}, u32[]{:S(2)}) collective-permute-start(f32[256,384]{1,0:T(8,128)S(1)} %collective-permute-done.2.refs_6_), channel_id=1, source_target_pairs={{0,2},{2,4},{4,6},{6,7},{7,5},{5,3},{3,1},{1,0},{8,10},{10,12},{12... | collective-permute-start | bytes 1179656 | tf_op jit(solution)/shard_map/ppermute | solution.py:262
  182.8 19.8 %collective-permute-start.33 = (f32[64,1024]{1,0:T(8,128)S(1)}, f32[64,1024]{1,0:T(8,128)}, u32[]{:S(2)}, u32[]{:S(2)}) collective-permute-start(f32[64,1024]{1,0:T(8,128)S(1)} %collective-permute-done.32), channel_id=1, source_target_pairs={{0,2},{2,4},{4,6},{6,7},{7,5},{5,3},{3,1},{1,0},{8,10},{10,12},{12... | collective-permute-start | bytes 786440 | tf_op jit(solution)/shard_map/ppermute | solution.py:262
  186.0 101.1 %collective-permute-start.20 = (f32[256,256]{1,0:T(8,128)}, f32[256,256]{1,0:T(8,128)S(1)}, u32[]{:S(2)}, u32[]{:S(2)}) collective-permute-start(f32[256,256]{1,0:T(8,128)} %collective-permute-done.19.refs_25_), channel_id=1, source_target_pairs={{2,0},{4,2},{6,4},{7,6},{5,7},{3,5},{1,3},{0,1},{10,8},{12,10},{14... | collective-permute-start | bytes 786440 | tf_op jit(solution)/shard_map/ppermute | solution.py:265
  196.8 90.4 %collective-permute-start.10 = (f32[256,256]{1,0:T(8,128)}, f32[256,256]{1,0:T(8,128)S(1)}, u32[]{:S(2)}, u32[]{:S(2)}) collective-permute-start(f32[256,256]{1,0:T(8,128)} %collective-permute-done.9.refs_14_), channel_id=1, source_target_pairs={{0,2},{2,4},{4,6},{6,7},{7,5},{5,3},{3,1},{1,0},{8,10},{10,12},{12... | collective-permute-start | bytes 786440 | tf_op jit(solution)/shard_map/ppermute | solution.py:262
  202.5 86.6 %collective-permute-start.17 = (f32[256,256]{1,0:T(8,128)}, f32[256,256]{1,0:T(8,128)S(1)}, u32[]{:S(2)}, u32[]{:S(2)}) collective-permute-start(f32[256,256]{1,0:T(8,128)} %collective-permute-done.16.refs_22_), channel_id=1, source_target_pairs={{0,2},{2,4},{4,6},{6,7},{7,5},{5,3},{3,1},{1,0},{8,10},{10,12},{12... | collective-permute-start | bytes 786440 | tf_op jit(solution)/shard_map/ppermute | solution.py:262
  202.8 132.2 %collective-permute-start.37 = (f32[64,1024]{1,0:T(8,128)}, f32[64,1024]{1,0:T(8,128)}, u32[]{:S(2)}, u32[]{:S(2)}) collective-permute-start(f32[64,1024]{1,0:T(8,128)} %collective-permute-done.36), channel_id=1, source_target_pairs={{2,0},{4,2},{6,4},{7,6},{5,7},{3,5},{1,3},{0,1},{10,8},{12,10},{14... | collective-permute-start | bytes 786440 | tf_op jit(solution)/shard_map/ppermute | solution.py:265
  205.3 131.5 %collective-permute-start.34 = (f32[64,1024]{1,0:T(8,128)}, f32[64,1024]{1,0:T(8,128)}, u32[]{:S(2)}, u32[]{:S(2)}) collective-permute-start(f32[64,1024]{1,0:T(8,128)} %collective-permute-done.33), channel_id=1, source_target_pairs={{0,2},{2,4},{4,6},{6,7},{7,5},{5,3},{3,1},{1,0},{8,10},{10,12},{12... | collective-permute-start | bytes 786440 | tf_op jit(solution)/shard_map/ppermute | solution.py:262
  287.1 104.8 %collective-permute-start.40 = (f32[128,512]{1,0:T(8,128)}, f32[128,512]{1,0:T(8,128)}, u32[]{:S(2)}, u32[]{:S(2)}) collective-permute-start(f32[128,512]{1,0:T(8,128)} %get-tuple-element.84.refs_9_), channel_id=1, source_target_pairs={{0,2},{2,4},{4,6},{6,7},{7,5},{5,3},{3,1},{1,0},{8,10},{10,12},{12... | collective-permute-start | bytes 786440 | tf_op jit(solution)/shard_map/ppermute | solution.py:262
  287.2 106.5 %collective-permute-start.44 = (f32[128,512]{1,0:T(8,128)}, f32[128,512]{1,0:T(8,128)}, u32[]{:S(2)}, u32[]{:S(2)}) collective-permute-start(f32[128,512]{1,0:T(8,128)} %get-tuple-element.84.refs_9_), channel_id=1, source_target_pairs={{2,0},{4,2},{6,4},{7,6},{5,7},{3,5},{1,3},{0,1},{10,8},{12,10},{14... | collective-permute-start | bytes 786440 | tf_op jit(solution)/shard_map/ppermute | solution.py:265
  289.2 104.8 %collective-permute-start.47 = (f32[128,512]{1,0:T(8,128)}, f32[128,512]{1,0:T(8,128)}, u32[]{:S(2)}, u32[]{:S(2)}) collective-permute-start(f32[128,512]{1,0:T(8,128)} %get-tuple-element.85.refs_17_), channel_id=1, source_target_pairs={{0,2},{2,4},{4,6},{6,7},{7,5},{5,3},{3,1},{1,0},{8,10},{10,12},{12... | collective-permute-start | bytes 786440 | tf_op jit(solution)/shard_map/ppermute | solution.py:262
  335.0 60.7 %collective-permute-start.51 = (f32[128,512]{1,0:T(8,128)}, f32[128,512]{1,0:T(8,128)}, u32[]{:S(2)}, u32[]{:S(2)}) collective-permute-start(f32[128,512]{1,0:T(8,128)} %get-tuple-element.85.refs_17_), channel_id=1, source_target_pairs={{2,0},{4,2},{6,4},{7,6},{5,7},{3,5},{1,3},{0,1},{10,8},{12,10},{14... | collective-permute-start | bytes 786440 | tf_op jit(solution)/shard_map/ppermute | solution.py:265
  336.8 59.2 %collective-permute-start.54 = (f32[128,512]{1,0:T(8,128)}, f32[128,512]{1,0:T(8,128)}, u32[]{:S(2)}, u32[]{:S(2)}) collective-permute-start(f32[128,512]{1,0:T(8,128)} %get-tuple-element.86.refs_25_), channel_id=1, source_target_pairs={{0,2},{2,4},{4,6},{6,7},{7,5},{5,3},{3,1},{1,0},{8,10},{10,12},{12... | collective-permute-start | bytes 786440 | tf_op jit(solution)/shard_map/ppermute | solution.py:262
  429.3 50.4 %collective-permute-start.38 = (f32[1,4,64,1024]{3,2,1,0:T(8,128)}, f32[1,4,64,1024]{3,2,1,0:T(8,128)S(1)}, u32[]{:S(2)}, u32[]{:S(2)}) collective-permute-start(f32[1,4,64,1024]{3,2,1,0:T(8,128)} %slice_bitcast_fusion.4), channel_id=1, source_target_pairs={{0,16},{8,24},{16,0},{24,8},{1,17},{9,25},{17,1},{25,9},{2,18},{10... | collective-permute-start | bytes 3145736 | tf_op jit(solution)/shard_map/ppermute | solution.py:286
  481.6 28.0 %collective-permute-start.39 = (f32[2,4,64,1024]{3,2,1,0:T(8,128)S(1)}, f32[2,4,64,1024]{3,2,1,0:T(8,128)S(1)}, u32[]{:S(2)}, u32[]{:S(2)}) collective-permute-start(f32[2,4,64,1024]{3,2,1,0:T(8,128)S(1)} %maximum_select_fusion.2), channel_id=1, source_target_pairs={{0,8},{8,0},{16,24},{24,16},{1,9},{9,1},{17,25},{25,17},{2,10},{10... | collective-permute-start | bytes 6291464 | tf_op jit(solution)/shard_map/ppermute | solution.py:286
  489.0 18.6 %collective-permute-start.69 = (f32[2,256,512]{2,1,0:T(8,128)S(1)}, f32[2,256,512]{2,1,0:T(8,128)S(1)}, u32[]{:S(2)}, u32[]{:S(2)}) collective-permute-start(f32[2,256,512]{2,1,0:T(8,128)S(1)} %maximum_select_fusion.5), channel_id=1, source_target_pairs={{0,8},{8,0},{16,24},{24,16},{1,9},{9,1},{17,25},{25,17},{2,10},{10... | collective-permute-start | bytes 3145736 | tf_op jit(solution)/shard_map/ppermute | solution.py:286
  (110 other events, 1833.1 us)

commit v2 on v1

--- a/solution.py
+++ b/solution.py
@@ -222,22 +222,26 @@
     pairs.sort(key=lambda pair: (pair[1] // per_stage, pair))
     taken = {}
 
-    def place(pair, limit, seen):
-        for rnd in range(limit):
+    last = {}
+
+    def place(pair, seen):
+        for rnd in range(last[pair]):
             for dev in (pair[1], pair[0]):
                 slot = (rnd, dev)
                 if slot in seen:
                     continue
                 seen.add(slot)
-                if slot not in taken or place(taken[slot], limit, seen):
+                if slot not in taken or place(taken[slot], seen):
                     taken[slot] = pair
                     return True
         return False
 
     limit = 1
     for pair in pairs:
-        while not place(pair, limit, set()):
+        last[pair] = limit
+        while not place(pair, set()):
             limit += 1
+            last[pair] = limit
     rounds = 1 + max((slot[0] for slot in taken), default=-1)
     table = np.full((max(rounds, 1), groups), -1, np.int32)
     for (rnd, dev), (j, i) in taken.items():
@@ -277,31 +281,29 @@
     return jnp.asarray(order)[(me + jnp.asarray(shifts, jnp.int32)) % groups].astype(jnp.int32)
 
 
+def direct_gather(x, axis, groups, sources):
+    moved = [
+        lax.ppermute(x, axis, [(s, (s + k) % groups) for s in range(sources)])
+        for k in range(1, groups)
+    ]
+    return [x] + moved
+
+
 def bulk_gather(x, axis, size):
-    me = lax.axis_index(axis)
-    held = x[None]
-    bits = size.bit_length() - 1
-    for bit in range(bits - 1, -1, -1):
-        step = 1 << bit
-        other = lax.ppermute(held, axis, [(i, i ^ step) for i in range(size)])
-        mine_high = (me >> bit) & 1
-        held = jnp.where(
-            mine_high == 1,
-            jnp.concatenate([other, held], axis=0),
-            jnp.concatenate([held, other], axis=0),
-        )
-    order = []
-    for k in range(size):
-        index = 0
-        for bit in range(bits):
-            if (k >> (bits - 1 - bit)) & 1:
-                index |= 1 << bit
-        order.append(index)
-    back = np.argsort(np.array(order))
-    return held, [int(v) for v in back]
-
-
-def child_stage(q, width, own, groups, cap, chunk_counts, refs):
+    held = {0: x}
+    step = size // 2
+    while step:
+        for mask in list(held):
+            held[mask | step] = lax.ppermute(held[mask], axis, [(i, i ^ step) for i in range(size)])
+        step //= 2
+    return [held[m] for m in range(size)]
+
+
+def after(x, dep):
+    return lax.optimization_barrier((x, dep))[0]
+
+
+def child_stage(q, width, own, groups, early, chunk_counts, refs):
     per_stage = width // own
     refs = list(refs)
 
@@ -312,10 +314,15 @@
     (owner_ref, table_ref, place_ref) = take(3)
     chunks = [take(count) for count in chunk_counts]
     prev_lh, prev_ll, prev_ih, prev_il, prev_xh, prev_xl = (take(q) for _ in range(6))
-    (b_ref, pick_ref) = take(2)
-    (lh, ll, invh, invl, xh, xl, top_ref, own_ref) = take(8)
+    (b_ref,) = take(1)
+    (lh, ll, invh, invl, xh, xl, own_ref) = take(7)
     (a_ref, s_ref) = take(2)
     first_group = q * per_stage
+
+    def block(rnd, k):
+        if rnd <= early:
+            return chunks[rnd][k][...]
+        return chunks[rnd][0][k * own : (k + 1) * own, :]
 
     for k in range(groups):
         f = owner_ref[k]
@@ -334,7 +341,7 @@
         if not chunks[rnd]:
             continue
         for k in range(groups):
-            f = owner_ref[k]
+            f = owner_ref[k] if rnd <= early else k
             c = table_ref[rnd - 1, f]
             high = jnp.maximum(f, c)
             low = jnp.minimum(f, c)
@@ -344,11 +351,11 @@
 
             @pl.when(jnp.logical_and(mine, f > c))
             def _(rnd=rnd, k=k, row=row, col=col):
-                a_ref[ds(row, own), ds(col, own)] = chunks[rnd][k][...]
+                a_ref[ds(row, own), ds(col, own)] = block(rnd, k)
 
             @pl.when(jnp.logical_and(mine, f < c))
             def _(rnd=rnd, k=k, row=row, col=col):
-                a_ref[ds(row, own), ds(col, own)] = chunks[rnd][k][...].T
+                a_ref[ds(row, own), ds(col, own)] = block(rnd, k).T
 
     for j in range(q):
         part = a_ref.at[:, j * width : (j + 1) * width]
@@ -370,35 +377,31 @@
 
         tiles(own, width, body)
     times_inverse(rest, xh, xl, 0, own, width, invh, invl)
-    pick = pick_ref[...]
-    top_ref[...] = dot(pick, xh[...], NN) + dot(pick, xl[...], NN)
     at = place_ref[0]
     own_ref[...] = lh[ds(at, own), :].astype(F32) + ll[ds(at, own), :].astype(F32)
 
 
-def cross_kernel(stages, own, cap, sources, groups, refs):
+def cross_kernel(stages, cap, sources, groups, refs):
     refs = list(refs)
 
     def take(count):
         out, refs[:count] = refs[:count], []
         return out
 
-    (owner_ref,) = take(1)
-    xh, xl = take(stages), take(stages)
-    slots = [take(groups) for _ in range(stages)]
+    (raw_ref,) = take(1)
+    lh, ll, ih, il, xh, xl = (take(stages) for _ in range(6))
     con_ref, sq_ref = take(2)
-    th, tl = take(2)
-    width = xh[0].shape[1]
+    t_ref, th, tl = take(3)
+    own, width = xh[0].shape
     total = sources * cap
-    for k in range(groups):
-        f = owner_ref[k]
-
-        @pl.when(f < sources)
-        def _(f=f, k=k):
-            for q in range(stages):
-                high, low = split(slots[q][k][...])
-                th[ds(f * cap, cap), q * width : (q + 1) * width] = high
-                tl[ds(f * cap, cap), q * width : (q + 1) * width] = low
+    share = raw_ref.shape[0] // groups
+    for f in range(groups):
+        at = (f % sources) * cap + (f // sources) * share
+        t_ref[at : at + share, :] = raw_ref[f * share : (f + 1) * share, :]
+    for q in range(stages):
+        part = t_ref.at[:, q * width : (q + 1) * width]
+        subtract_products(part, total, width, th, tl, lh[q], ll[q], q * width)
+        times_inverse(part, th, tl, q * width, total, width, ih[q], il[q])
 
     for c in range(total // LANES):
         rows = slice(c * LANES, (c + 1) * LANES)
@@ -409,8 +412,7 @@
         con_ref[:, rows] = acc
 
     def square(t, carry):
-        i = carry[0]
-        j = carry[1]
+        i, j = carry
         a = (th[ds(i * LANES, LANES), :], tl[ds(i * LANES, LANES), :])
         b = (th[ds(j * LANES, LANES), :], tl[ds(j * LANES, LANES), :])
         sq_ref[t] = dot3(a, b, NT)
@@ -422,16 +424,24 @@
 
 
 def parent_kernel(children, blocks, width, refs):
-    top_ref, spread_ref, sq_ref, lh, ll, invh, invl, lower, s_ref = refs
-    pivots = top_ref.shape[0]
+    refs = list(refs)
+    place_ref, spread_ref = refs[:2]
+    tops, squares = refs[2 : 2 + children], refs[2 + children : 2 + 2 * children]
+    lh, ll, invh, invl, lower, s_ref, top_ref = refs[2 + 2 * children :]
+    pivots = lh.shape[0]
     dense = pivots // blocks
+    sources, piece, _ = tops[0].shape
+    for m in range(children):
+        g = place_ref[2] ^ m
+        for s in range(sources):
+            top_ref[ds(s * (children * piece) + g * piece, piece), :] = tops[m][s]
     for i in range(blocks):
         for j in range(i + 1):
             at = i * (i + 1) // 2 + j
             parts = []
             for c in range(children):
                 left = spread_ref[i, :, c * LANES : (c + 1) * LANES]
-                high, low = split(sq_ref[c, at])
+                high, low = split(squares[c][at])
                 parts.append(dot(left, high, NN) + dot(left, low, NN))
             high, low = split(jnp.concatenate(parts, axis=1))
             right = spread_ref[j]
@@ -458,9 +468,11 @@
 
 
 def rest_kernel(children, blocks, width, refs):
-    place_ref, rows_ref, route_ref, con_ref, spread_ref, lh, ll, invh, invl, out_ref, s_ref, xh, xl = refs
+    refs = list(refs)
+    place_ref, rows_ref, route_ref, spread_ref = refs[:4]
+    con_refs = refs[4 : 4 + children]
+    lh, ll, invh, invl, out_ref, s_ref, xh, xl = refs[4 + children :]
     pivots = lh.shape[0]
-    own = con_ref.shape[1]
     count = rows_ref.shape[0]
     dense = pivots // blocks
     at = place_ref[1]
@@ -474,7 +486,7 @@
     def _():
         routed = []
         for c in range(children):
-            high, low = split(con_ref[c])
+            high, low = split(con_refs[c][...])
             route = route_ref[c]
             routed.append(split(dot(route, high, NN) + dot(route, low, NN)))
         for b in range(blocks):
@@ -508,43 +520,91 @@
     cap = min(CAP, count, own)
     blocks = sources * cap // LANES
 
-    maps = lax.all_gather(row_map[0], ("bulk", "front"), axis=0).reshape(bulk, front, own)
+    table = send_plan(front, per_stage)
+    rounds = table.shape[0]
+    early = max(
+        (r + 1 for r in range(rounds) for f, c in enumerate(table[r]) if c >= 0 and max(f, c) // per_stage == 1),
+        default=0,
+    )
+    half = own // 2
+    own_block = lax.dynamic_slice_in_dim(mine, me * own, own, 1)
+    even = lax.dynamic_slice_in_dim(mine, jnp.minimum(me + 1, front - 1) * own, half, 1)
+    odd = lax.dynamic_slice_in_dim(mine[half:], jnp.maximum(me - 1, 0) * own, own, 1).T
+    chunks = [jnp.concatenate([own_block, jnp.where(me % 2 == 0, even, odd)], axis=1)]
+    for rnd in range(rounds):
+        col = jnp.maximum(jnp.asarray(table[rnd])[me], 0)
+        chunks.append(lax.dynamic_slice_in_dim(mine, col * own, own, 1))
+    owners = slot_owners("front", front)
+    gathered = []
+    for rnd in range(early + 1):
+        chunk = chunks[rnd] if rnd == 0 else after(chunks[rnd], gathered[-1][-1])
+        gathered.append(ring_gather(chunk, "front", front))
+    started = gathered[0][-1]
+    late = started
+    if early < rounds:
+        late = after(jnp.concatenate(chunks[early + 1 :], axis=1), started)
+        late = lax.all_gather(late, "front", axis=0, tiled=True)
+        for rnd in range(rounds - early):
+            gathered.append([late[:, rnd * own : (rnd + 1) * own]])
+    table_in = jnp.asarray(table if rounds else np.zeros((1, front), np.int32))
+    bulk_me = lax.axis_index("bulk")
+    place = jnp.stack([(me % per_stage) * own, first_row, bulk_me]).astype(jnp.int32)
+
+    own_map = row_map[0]
+    own_lands = own_map < pivots
+    own_rank = jnp.where(own_lands, jnp.cumsum(own_lands.astype(jnp.int32)) - 1, -1)
+    pick = (own_rank[None, :] == jnp.arange(cap)[:, None]).astype(F32)
+    compact = jnp.dot(pick, coupling, precision=HIGHEST_PRECISION)
+    spreads = front // sources
+    share = cap // spreads
+    part = compact[:share]
+    for k in range(1, spreads):
+        moved = lax.ppermute(
+            compact[k * share : (k + 1) * share],
+            "front",
+            [(s, s + k * sources) for s in range(sources)],
+        )
+        part = jnp.where(me // sources == k, moved, part)
+    raw_landing = lax.all_gather(after(part, late), "front", axis=0, tiled=True)
+
+    block_rows = (first_row + jnp.arange(count)) // BLOCK
+    row_mask = jnp.take(block_pattern, block_rows, axis=0).astype(F32)
+    arrow = parent_arrow * jnp.repeat(row_mask, BLOCK, axis=1)
+    piece = count // bulk
+    part = arrow[:piece]
+    for g in range(1, bulk):
+        moved = lax.ppermute(arrow[g * piece : (g + 1) * piece], "bulk", [(0, g)])
+        part = jnp.where(bulk_me == g, moved, part)
+    slots = direct_gather(after(part, gathered[early][-1]), "front", front, sources)
+    stacked = jnp.stack(slots)
+    line = jnp.stack(
+        [lax.dynamic_index_in_dim(stacked, (me - s) % front, 0, False) for s in range(sources)]
+    )
+
+    my_maps = jnp.stack(ring_gather(after(own_map, started), "front", front))
+    ordered = jnp.zeros((front, own), jnp.int32)
+    for k in range(front):
+        ordered = lax.dynamic_update_index_in_dim(ordered, my_maps[k], owners[k], 0)
+    maps = jnp.stack(bulk_gather(ordered, "bulk", bulk))
     lands = maps[:, :sources] < pivots
     rank = jnp.cumsum(lands.astype(jnp.int32), axis=2) - 1
     overflow = jnp.any(rank[:, :, -1] >= cap)
-    chosen = jnp.where(lands[:, :, None, :], rank[:, :, None, :], -1) == jnp.arange(cap)[:, None]
+    chosen = jnp.where(lands, rank, -1)[:, :, None, :] == jnp.arange(cap)[:, None]
     target = jnp.max(jnp.where(chosen, maps[:, :sources, None, :], -1), axis=3)
     target = jnp.where(overflow, -1, target).reshape(bulk, blocks, LANES)
     dense = pivots // blocks
     rows_of = (jnp.arange(blocks)[:, None] * dense + jnp.arange(dense)[None, :])[:, :, None, None]
     spread = (jnp.transpose(target, (1, 0, 2))[:, None] == rows_of).astype(BF16)
     spread = spread.reshape(blocks, dense, bulk * LANES)
-    own_map = row_map[0]
-    own_rank = jnp.where(own_map < pivots, jnp.cumsum((own_map < pivots).astype(jnp.int32)) - 1, -1)
-    pick = (own_rank[None, :] == jnp.arange(cap)[:, None]).astype(BF16)
     route = (
         lax.dynamic_index_in_dim(maps, me, 1, False)[:, None, :]
         == (first_row + jnp.arange(count))[None, :, None]
     ).astype(BF16)
 
-    table = send_plan(front, per_stage)
-    half = own // 2
-    own_block = lax.dynamic_slice_in_dim(mine, me * own, own, 1)
-    even = lax.dynamic_slice_in_dim(mine, jnp.minimum(me + 1, front - 1) * own, half, 1)
-    odd = lax.dynamic_slice_in_dim(mine[half:], jnp.maximum(me - 1, 0) * own, own, 1).T
-    chunks = [jnp.concatenate([own_block, jnp.where(me % 2 == 0, even, odd)], axis=1)]
-    for rnd in range(table.shape[0]):
-        col = jnp.maximum(jnp.asarray(table[rnd])[me], 0)
-        chunks.append(lax.dynamic_slice_in_dim(mine, col * own, own, 1))
-    owners = slot_owners("front", front)
-    gathered = [ring_gather(chunk, "front", front) for chunk in chunks]
-    table_in = jnp.asarray(table if table.shape[0] else np.zeros((1, front), np.int32))
-    place = jnp.stack([(me % per_stage) * own, first_row]).astype(jnp.int32)
-
-    lh, ll, ih, il, xh, xl, tops, owned = ([] for _ in range(8))
+    lh, ll, ih, il, xh, xl, owned = ([] for _ in range(7))
     for q in range(stages):
         used = [gathered[0]]
-        for rnd in range(table.shape[0]):
+        for rnd in range(rounds):
             needed = any(
                 c >= 0 and max(f, c) // per_stage == q for f, c in enumerate(table[rnd])
             )
@@ -555,12 +615,12 @@
             [owners, table_in, place]
             + flat
             + lh + ll + ih + il + xh + xl
-            + [coupling[:, q * width : (q + 1) * width], pick]
+            + [coupling[:, q * width : (q + 1) * width]]
         )
         deep = (q + 1) * width
         out = vmem_call(
             functools.partial(
-                lambda *refs, q, counts: child_stage(q, width, own, front, cap, counts, refs),
+                lambda *refs, q, counts: child_stage(q, width, own, front, early, counts, refs),
                 q=q,
                 counts=counts,
             ),
@@ -571,13 +631,13 @@
                 shaped((width, width), BF16),
                 shaped((own, width), BF16),
                 shaped((own, width), BF16),
-                shaped((cap, width), F32),
                 shaped((own, deep), F32),
             ],
             [True] * 3 + [False] * (len(operands) - 3),
             [pltpu.VMEM((width, deep), F32), pltpu.VMEM((width, width), F32)],
+            pl.CostEstimate(flops=30_000_000_000, bytes_accessed=1 << 24, transcendentals=0),
         )(*operands)
-        for held, new in zip((lh, ll, ih, il, xh, xl, tops, owned), out, strict=True):
+        for held, new in zip((lh, ll, ih, il, xh, xl, owned), out, strict=True):
             held.append(new)
 
     x_own = jnp.concatenate([h.astype(F32) + l.astype(F32) for h, l in zip(xh, xl, strict=True)], axis=1)
@@ -586,36 +646,20 @@
         padded = jnp.pad(owned[q], ((0, 0), (0, total - (q + 1) * width)))
         lower_rows = jnp.where(me // per_stage == q, padded, lower_rows)
 
-    slots = [x for top in tops for x in ring_gather(top, "front", front)]
     con, squares = vmem_call(
-        lambda *refs: cross_kernel(stages, own, cap, sources, front, refs),
+        lambda *refs: cross_kernel(stages, cap, sources, front, refs),
         [
             shaped((own, sources * cap), F32),
             shaped((blocks * (blocks + 1) // 2, LANES, LANES), F32),
         ],
-        [True] + [False] * (2 * stages + len(slots)),
-        [pltpu.VMEM((sources * cap, total), BF16)] * 2,
-    )(owners, *xh, *xl, *slots)
-
-    block_rows = (first_row + jnp.arange(count)) // BLOCK
-    row_mask = jnp.take(block_pattern, block_rows, axis=0).astype(F32)
-    arrow = parent_arrow * jnp.repeat(row_mask, BLOCK, axis=1)
-    piece = count // bulk
-    part = arrow[:piece]
-    for g in range(1, bulk):
-        moved = lax.ppermute(arrow[g * piece : (g + 1) * piece], "bulk", [(0, g)])
-        part = jnp.where(lax.axis_index("bulk") == g, moved, part)
-    ring = ring_gather(part, "front", front)
-    line = jnp.zeros((front, piece, pivots), F32)
-    for k, value in enumerate(ring):
-        line = lax.dynamic_update_index_in_dim(line, value, owners[k], 0)
-    held, back = bulk_gather(line[:sources], "bulk", bulk)
-    top = jnp.stack([held[b] for b in back], axis=1).reshape(pivots, pivots)
-
-    def unchanged(top, arrow, x_own):
-        return top, arrow
-
-    def landing_whole(top, arrow, x_own):
+        [False] * (1 + 6 * stages),
+        [pltpu.VMEM((sources * cap, total), F32)] + [pltpu.VMEM((sources * cap, total), BF16)] * 2,
+    )(raw_landing, *lh, *ll, *ih, *il, *xh, *xl)
+
+    def unchanged(lines, arrow, x_own):
+        return lines, arrow
+
+    def landing_whole(lines, arrow, x_own):
         slot = own_map - me * count
         hits = (slot[:, None] == jnp.arange(count)[None, :]).astype(F32)
         piece_rows = jnp.dot(hits.T, x_own, precision=HIGHEST_PRECISION)
@@ -629,13 +673,18 @@
             scatter_dimension=0,
             tiled=True,
         )
-        whole_square = lax.psum(jnp.dot(whole, whole.T, precision=HIGHEST_PRECISION), "bulk")
-        return top - whole_square, arrow - added
-
-    top, arrow = lax.cond(overflow, landing_whole, unchanged, top, arrow, x_own)
-
-    held, back = bulk_gather(squares, "bulk", bulk)
-    sq_all = jnp.stack([held[b] for b in back], axis=0)
+        square = lax.psum(jnp.dot(whole, whole.T, precision=HIGHEST_PRECISION), "bulk")
+        square = square.reshape(sources, bulk, piece, pivots)
+        changed = [
+            lines[m] - lax.dynamic_index_in_dim(square, bulk_me ^ m, 1, False) for m in range(bulk)
+        ]
+        return changed, arrow - added
+
+    lines = bulk_gather(line, "bulk", bulk)
+    lines, arrow = lax.cond(overflow, landing_whole, unchanged, lines, arrow, x_own)
+
+    all_squares = bulk_gather(squares, "bulk", bulk)
+    all_con = bulk_gather(after(con, all_squares[-1]), "bulk", bulk)
     plh, pll, pih, pil, plow = vmem_call(
         lambda *refs: parent_kernel(bulk, blocks, width, refs),
         [
@@ -645,22 +694,21 @@
             shaped((pivots // width, width, width), BF16),
             shaped((pivots, pivots), F32),
         ],
-        [False] * 3,
-        [pltpu.VMEM((pivots, pivots), F32)],
-    )(top, spread, sq_all)
-
-    held, back = bulk_gather(con, "bulk", bulk)
-    con_all = jnp.stack([held[b] for b in back], axis=0)
+        [True] + [False] * (1 + 2 * bulk),
+        [pltpu.VMEM((pivots, pivots), F32)] * 2,
+        pl.CostEstimate(flops=60_000_000_000, bytes_accessed=1 << 24, transcendentals=0),
+    )(place, spread, *lines, *all_squares)
+
     (parent_rows,) = vmem_call(
         lambda *refs: rest_kernel(bulk, blocks, width, refs),
         [shaped((count, pivots), F32)],
-        [True] + [False] * 8,
+        [True] + [False] * (7 + bulk),
         [
             pltpu.VMEM((count, pivots), F32),
             pltpu.VMEM((count, pivots), BF16),
             pltpu.VMEM((count, pivots), BF16),
         ],
-    )(place, arrow, route, con_all, spread, plh, pll, pih, pil)
+    )(place, arrow, route, spread, *all_con, plh, pll, pih, pil)
     return (lower_rows[None], x_own[None], parent_rows)
 
 

time: 611 us -> 550 us (0.900)
  blocking collectives: 66.9 us -> 0 us
  waiting for transfers between devices: 115 us -> 149 us
  starting transfers between devices: 63.2 us -> 42.9 us
  Pallas kernels: 251 us -> 267 us
  other arithmetic: 36.9 us -> 22.9 us
  local copies, waits for them, and re-layouts: 32.2 us -> 20.5 us
    all_gather x1 -> x0, blocking collectives: 66.9 us -> none  [on_device(): lax.all_gather(row_map[0], ('bulk', 'front'), axis=0)]
    ppermute x27 -> x9, starting transfers between devices: 48.3 us -> 5.06 us  [ring_gather(): coming = lax.ppermute(coming, axis, back)]
    ppermute x6 -> x20, waiting for transfers between devices: 19.3 us -> 47.8 us  [the longest x7 24.9 us: direct_gather(): lax.ppermute(x, axis, [(s, (s + k) % groups) for s in range(sources)])]
    pallas_call x1, Pallas kernels: 14.8 us -> 31.6 us  [on_device(): vmem_call(lambda *refs: cross_kernel(stages, cap, sources, front, refs),...]
    ppermute x6 -> x20, starting transfers between devices: 0.29 us -> 15.5 us  [the longest x7 7.18 us: direct_gather(): lax.ppermute(x, axis, [(s, (s + k) % groups) for s in range(sources)])]
    ppermute x27 -> x9, waiting for transfers between devices: 19.2 us -> 28.5 us  [ring_gather(): coming = lax.ppermute(coming, axis, back)]
    dynamic_update_slice x7 -> x8, local copies, waits for them, and re-layouts: 7.57 us -> 0.33 us  [on_device(): ordered = lax.dynamic_update_index_in_dim(ordered, my_maps[k], owners[k], 0)]
    ppermute x36 -> x12, starting transfers between devices: 11.3 us -> 18.3 us  [ring_gather(): going = lax.ppermute(going, axis, ahead)]
  transfers between devices with their start and end apart: 72 -> 46, of which waited for: 32 -> 15; matrix products, arithmetic and copies ran while one was open for 9% -> 7% of each run, Pallas kernels for 30% -> 48%
where the time goes in v2:
time: 550 us; the launch traced here: 542 us
  Pallas kernels  267 us (49%)
  waiting for transfers between devices  149 us (27%)
  starting transfers between devices  42.9 us (8%)
  between operations  33.6 us (6%)
  other arithmetic  22.9 us (4%)
  local copies, waits for them, and re-layouts  20.5 us (4%)
    pallas_call x4, Pallas kernels, on_device(): vmem_call(functools.partial(lambda *refs, q, counts: child_stage(q, width...  163 us
    ppermute x12, waiting for transfers between devices, ring_gather(): going = lax.ppermute(going, axis, ahead)  72.8 us
    pallas_call x1, Pallas kernels, on_device(): vmem_call(lambda *refs: parent_kernel(bulk, blocks, width, refs), [shaped...  63.6 us
    pallas_call x1, Pallas kernels, on_device(): vmem_call(lambda *refs: cross_kernel(stages, cap, sources, front, refs),...  31.6 us
    ppermute x9, waiting for transfers between devices, ring_gather(): coming = lax.ppermute(coming, axis, back)  28.5 us
    ppermute x7, waiting for transfers between devices, direct_gather(): lax.ppermute(x, axis, [(s, (s + k) % groups) for s in range(sources)])  24.9 us
    ppermute x12, waiting for transfers between devices, bulk_gather(): lax.ppermute(held[mask], axis, [(i, i ^ step) for i in range(size)])  22.9 us
    ppermute x12, starting transfers between devices, ring_gather(): going = lax.ppermute(going, axis, ahead)  18.3 us
  transfers between devices with their start and end apart: 46, of which 15 were waited for; matrix products, arithmetic and copies ran while one was open for 7% of the time, Pallas kernels for 48%

profile of v2, /device:TPU:20, one launch (start us, length us, event | category | flops | bytes accessed | tf_op | source)
XLA Modules:
  0.0 541.9 jit_solution(8515913351045776142)
XLA Ops:
  14.1 2.1 dynamic-slice_bitcast_fusion.1
  26.2 1.9 collective-permute-done.4.refs_8_
  30.1 8.3 %collective-permute-done.5.refs_9_ = f32[256,384]{1,0:T(8,128)S(1)} collective-permute-done((f32[256,384]{1,0:T(8,128)}, f32[256,384]{1,0:T(8,128)S(1)}, u32[]{:S(2)}, u32[]{:S(2)}) %collective-permute-start.5) | collective-permute-done | bytes 393248 | tf_op jit(solution)/shard_map/ppermute | solution.py:269
  39.4 1.8 fusion.13
  41.3 6.1 %collective-permute-done.6.refs_10_ = f32[256,384]{1,0:T(8,128)S(1)} collective-permute-done((f32[256,384]{1,0:T(8,128)S(1)}, f32[256,384]{1,0:T(8,128)S(1)}, u32[]{:S(2)}, u32[]{:S(2)}) %collective-permute-start.6) | collective-permute-done | bytes 393248 | tf_op jit(solution)/shard_map/ppermute | solution.py:269
  63.4 34.4 %collective-permute-done.17 = s32[256]{0:T(256)S(1)} collective-permute-done((s32[256]{0:T(256)S(1)}, s32[256]{0:T(256)S(1)}, u32[]{:S(2)}, u32[]{:S(2)}) %collective-permute-start.17) | collective-permute-done | bytes 1056 | tf_op jit(solution)/shard_map/ppermute | solution.py:266
  119.0 2.0 collective-permute-start.11
  121.0 24.0 %collective-permute-done.2.refs_6_ = f32[256,384]{1,0:T(8,128)} collective-permute-done((f32[256,384]{1,0:T(8,128)}, f32[256,384]{1,0:T(8,128)}, u32[]{:S(2)}, u32[]{:S(2)}) %collective-permute-start.2) | collective-permute-done | bytes 393248 | tf_op jit(solution)/shard_map/ppermute | solution.py:266
  145.0 3.7 collective-permute-start.3
  148.7 4.8 reduce-window.15
  154.1 8.0 %collective-permute-done.12.refs_17_ = f32[256,256]{1,0:T(8,128)S(1)} collective-permute-done((f32[256,256]{1,0:T(8,128)S(1)}, f32[256,256]{1,0:T(8,128)S(1)}, u32[]{:S(2)}, u32[]{:S(2)}) %collective-permute-start.12) | collective-permute-done | bytes 262176 | tf_op jit(solution)/shard_map/ppermute | solution.py:269
  164.2 1.8 collective-permute-start.8
  166.0 2.5 collective-permute-done.13.refs_18_
  170.6 29.7 %shard_map.139 = (bf16[512,512]{1,0:T(8,128)(2,1)}, bf16[512,512]{1,0:T(8,128)(2,1)}, bf16[512,512]{1,0:T(8,128)(2,1)}, bf16[512,512]{1,0:T(8,128)(2,1)}, bf16[2...) custom-call(s32[8]{0:T(128)} %copy-done.20, s32[3,8]{1,0:T(4,128)} %constant.265.clone.refs_1_, ...), custom_call_target="tpu_custom_call" | custom-call | flops 30000001024 | bytes 16777216 | tf_op jit(solution)/shard_map/pallas_call | solution.py:621
  204.5 22.5 %collective-permute-done.28 = f32[64,1024]{1,0:T(8,128)S(1)} collective-permute-done((f32[64,1024]{1,0:T(8,128)S(1)}, f32[64,1024]{1,0:T(8,128)S(1)}, u32[]{:S(2)}, u32[]{:S(2)}) %collective-permute-start.28) | collective-permute-done | bytes 262176 | tf_op jit(solution)/shard_map/ppermute | solution.py:286
  228.9 4.8 collective-permute-start.10
  233.7 2.4 collective-permute-done.30
  238.2 14.4 %collective-permute-done.10.refs_15_ = f32[256,256]{1,0:T(8,128)S(1)} collective-permute-done((f32[256,256]{1,0:T(8,128)S(1)}, f32[256,256]{1,0:T(8,128)S(1)}, u32[]{:S(2)}, u32[]{:S(2)}) %collective-permute-start.10) | collective-permute-done | bytes 262176 | tf_op jit(solution)/shard_map/ppermute | solution.py:266
  253.3 36.3 %shard_map.140 = (bf16[512,1024]{1,0:T(8,128)(2,1)}, bf16[512,1024]{1,0:T(8,128)(2,1)}, bf16[512,512]{1,0:T(8,128)(2,1)}, bf16[512,512]{1,0:T(8,128)(2,1)}, bf16...) custom-call(s32[8]{0:T(128)} %copy-done.20, s32[3,8]{1,0:T(4,128)} %constant.265.clone.refs_1_, ...), custom_call_target="tpu_custom_call" | custom-call | flops 30000001024 | bytes 16777216 | tf_op jit(solution)/shard_map/pallas_call | solution.py:621
  289.8 4.5 fusion.22
  294.3 44.5 %shard_map.141 = (bf16[512,1536]{1,0:T(8,128)(2,1)}, bf16[512,1536]{1,0:T(8,128)(2,1)}, bf16[512,512]{1,0:T(8,128)(2,1)}, bf16[512,512]{1,0:T(8,128)(2,1)}, bf16...) custom-call(s32[8]{0:T(128)} %copy-done.20, s32[3,8]{1,0:T(4,128)} %constant.265.clone.refs_1_, ...), custom_call_target="tpu_custom_call" | custom-call | flops 30000001024 | bytes 16777216 | tf_op jit(solution)/shard_map/pallas_call | solution.py:621
  338.7 52.8 %shard_map.142 = (bf16[512,2048]{1,0:T(8,128)(2,1)}, bf16[512,2048]{1,0:T(8,128)(2,1)}, bf16[512,512]{1,0:T(8,128)(2,1)}, bf16[512,512]{1,0:T(8,128)(2,1)}, bf16...) custom-call(s32[8]{0:T(128)} %copy-done.20, s32[3,8]{1,0:T(4,128)} %constant.265.clone.refs_1_, ...), custom_call_target="tpu_custom_call" | custom-call | flops 30000001024 | bytes 16777216 | tf_op jit(solution)/shard_map/pallas_call | solution.py:621
  391.6 31.6 %shard_map.143 = (f32[256,512]{1,0:T(8,128)}, f32[10,128,128]{2,1,0:T(8,128)}) custom-call(f32[512,2048]{1,0:T(8,128)} %all-gather.8.cloned.1.call-done.refs_0_, bf16[512,512]{1,0:T(8,128)(2,1)} %get-tuple-element.87.refs_19_.refs_21_.refs_1_, bf16[512,1024]{1,0:T(8,128)(2,1)} %get-tuple-element.93.refs_22_.refs_2_, ...), custom_call_target="tpu_custom_call" | custom-call | tf_op jit(solution)/shard_map/pallas_call | solution.py:649
  423.3 1.9 collective-permute-start.38
  428.0 12.9 %collective-permute-done.38.refs_8_ = f32[10,128,128]{2,1,0:T(8,128)} collective-permute-done((f32[10,128,128]{2,1,0:T(8,128)}, f32[10,128,128]{2,1,0:T(8,128)}, u32[]{:S(2)}, u32[]{:S(2)}) %collective-permute-start.38) | collective-permute-done | bytes 655392 | tf_op jit(solution)/shard_map/ppermute | solution.py:297
  441.8 1.8 pad_maximum_fusion
  443.7 3.5 conditional.1
  447.2 1.8 collective-permute-start.41
  449.0 3.8 select_bitcast_fusion
  452.9 8.5 %collective-permute-done.41.refs_6_ = f32[256,512]{1,0:T(8,128)S(1)} collective-permute-done((f32[256,512]{1,0:T(8,128)}, f32[256,512]{1,0:T(8,128)S(1)}, u32[]{:S(2)}, u32[]{:S(2)}) %collective-permute-start.41) | collective-permute-done | bytes 524320 | tf_op jit(solution)/shard_map/ppermute | solution.py:297
  461.3 63.6 %shard_map.144 = (bf16[1024,1024]{1,0:T(8,128)(2,1)}, bf16[1024,1024]{1,0:T(8,128)(2,1)}, bf16[2,512,512]{2,1,0:T(8,128)(2,1)}, bf16[2,512,512]{2,1,0:T(8,128)(2,1)}, f32[1024,1024]{1,0:T(8,128)}) custom-call(s32[3]{0:T(128)} %pad_add_fusion.1.refs_2_.refs_0_, bf16[4,256,512]{2,1,0:T(8,128)(2,1)} %compare_convert_fusion.refs_1_.refs_3_, ...), custom_call_target="tpu_custom_call" | custom-call | flops 60000002048 | bytes 16777216 | tf_op jit(solution)/shard_map/pallas_call | solution.py:688
  525.8 8.7 %shard_map.145 = f32[256,1024]{1,0:T(8,128)} custom-call(s32[3]{0:T(128)} %pad_add_fusion.1.refs_2_.refs_0_, f32[256,1024]{1,0:T(8,128)S(1)} %get-tuple-element.113.refs_1_, bf16[4,256,256]{2,1,0:T(8,128)(2,1)} %compare_convert_fusion.1.refs_2_, bf16[4,256,512]{2,1,0:T(8,128)(2,1)} %compare_convert_fusion.refs_1_.refs_3_, ...), custom_call_target="tpu_custom_call" | custom-call | tf_op jit(solution)/shard_map/pallas_call | solution.py:702
  (221 shorter events, 56.6 us)
Async XLA Ops:
  7.2 231.0 %all-gather.6.cloned.1.call-start = ((), (), s32[]{:S(2)}) async-start(), calls=%async_computation.4 | async-start | bytes 4718592 | tf_op jit(solution)/shard_map/all_gather | solution.py:546
  17.0 11.2 %collective-permute-start.4 = (f32[256,384]{1,0:T(8,128)}, f32[256,384]{1,0:T(8,128)}, u32[]{:S(2)}, u32[]{:S(2)}) collective-permute-start(f32[256,384]{1,0:T(8,128)} %pad_maximum_fusion.3.refs_3_), channel_id=1, source_target_pairs={{2,0},{4,2},{6,4},{7,6},{5,7},{3,5},{1,3},{0,1},{10,8},{12,10},{14... | collective-permute-start | bytes 1179656 | tf_op jit(solution)/shard_map/ppermute | solution.py:269
  17.4 40.9 %collective-permute-start = (f32[256,384]{1,0:T(8,128)}, f32[256,384]{1,0:T(8,128)}, u32[]{:S(2)}, u32[]{:S(2)}) collective-permute-start(f32[256,384]{1,0:T(8,128)} %pad_maximum_fusion.3.refs_3_), channel_id=1, source_target_pairs={{0,2},{2,4},{4,6},{6,7},{7,5},{5,3},{3,1},{1,0},{8,10},{10,12},{12... | collective-permute-start | bytes 1179656 | tf_op jit(solution)/shard_map/ppermute | solution.py:266
  22.9 91.4 %collective-permute-start.26 = (f32[64,1024]{1,0:T(8,128)}, f32[64,1024]{1,0:T(8,128)}, u32[]{:S(2)}, u32[]{:S(2)}) collective-permute-start(f32[64,1024]{1,0:T(8,128)} %get-tuple-element.154), channel_id=1, source_target_pairs={{0,8},{1,9},{2,10},{3,11},{4,12},{5,13},{6,14},{7,15}} | collective-permute-start | bytes 786440 | tf_op jit(solution)/shard_map/ppermute | solution.py:576
  24.3 91.1 %collective-permute-start.25 = (f32[64,1024]{1,0:T(8,128)}, f32[64,1024]{1,0:T(8,128)}, u32[]{:S(2)}, u32[]{:S(2)}) collective-permute-start(f32[64,1024]{1,0:T(8,128)} %get-tuple-element.155), channel_id=1, source_target_pairs={{0,16},{1,17},{2,18},{3,19},{4,20},{5,21},{6,22},{7,23}} | collective-permute-start | bytes 786440 | tf_op jit(solution)/shard_map/ppermute | solution.py:576
  58.4 57.0 %collective-permute-start.24 = (f32[64,1024]{1,0:T(8,128)S(1)}, f32[64,1024]{1,0:T(8,128)}, u32[]{:S(2)}, u32[]{:S(2)}) collective-permute-start(f32[64,1024]{1,0:T(8,128)S(1)} %copy-done.19), channel_id=1, source_target_pairs={{0,24},{1,25},{2,26},{3,27},{4,28},{5,29},{6,30},{7,31}} | collective-permute-start | bytes 786440 | tf_op jit(solution)/shard_map/ppermute | solution.py:576
  59.7 58.3 %collective-permute-start.37 = (f32[64,2048]{1,0:T(8,128)S(1)}, f32[64,2048]{1,0:T(8,128)S(1)}, u32[]{:S(2)}, u32[]{:S(2)}) collective-permute-start(f32[64,2048]{1,0:T(8,128)S(1)} %slice.133), channel_id=1, source_target_pairs={{0,4},{1,5},{2,6},{3,7},{8,12},{9,13},{10,14},{11,15},{16,20},{17,... | collective-permute-start | bytes 1572872 | tf_op jit(solution)/shard_map/ppermute | solution.py:562
  61.0 36.8 %collective-permute-start.17 = (s32[256]{0:T(256)S(1)}, s32[256]{0:T(256)S(1)}, u32[]{:S(2)}, u32[]{:S(2)}) collective-permute-start(s32[256]{0:T(256)S(1)} %collective-permute-done.16), channel_id=1, source_target_pairs={{0,2},{2,4},{4,6},{6,7},{7,5},{5,3},{3,1},{1,0},{8,10},{10,12},{12... | collective-permute-start | bytes 3080 | tf_op jit(solution)/shard_map/ppermute | solution.py:266
  63.4 328.2 %all-gather.8.cloned.1.call-start = ((), (), s32[]{:S(2)}) async-start(), calls=%async_computation.5 | async-start | bytes 4718592 | tf_op jit(solution)/shard_map/all_gather | solution.py:568
  97.8 18.5 %collective-permute-start.1 = (f32[256,384]{1,0:T(8,128)}, f32[256,384]{1,0:T(8,128)}, u32[]{:S(2)}, u32[]{:S(2)}) collective-permute-start(f32[256,384]{1,0:T(8,128)} %collective-permute-done.refs_4_), channel_id=1, source_target_pairs={{0,2},{2,4},{4,6},{6,7},{7,5},{5,3},{3,1},{1,0},{8,10},{10,12},{12... | collective-permute-start | bytes 1179656 | tf_op jit(solution)/shard_map/ppermute | solution.py:266
  116.4 28.6 %collective-permute-start.2 = (f32[256,384]{1,0:T(8,128)}, f32[256,384]{1,0:T(8,128)}, u32[]{:S(2)}, u32[]{:S(2)}) collective-permute-start(f32[256,384]{1,0:T(8,128)} %collective-permute-done.1.refs_5_), channel_id=1, source_target_pairs={{0,2},{2,4},{4,6},{6,7},{7,5},{5,3},{3,1},{1,0},{8,10},{10,12},{12... | collective-permute-start | bytes 1179656 | tf_op jit(solution)/shard_map/ppermute | solution.py:266
  116.5 32.2 %collective-permute-start.21 = (s32[8,256]{1,0:T(8,128)S(1)}, s32[8,256]{1,0:T(8,128)S(1)}, u32[]{:S(2)}, u32[]{:S(2)}) collective-permute-start(s32[8,256]{1,0:T(8,128)S(1)} %dynamic_update_slice.32), channel_id=1, source_target_pairs={{0,8},{8,0},{16,24},{24,16},{1,9},{9,1},{17,25},{25,17},{2,10},{10... | collective-permute-start | bytes 24584 | tf_op jit(solution)/shard_map/ppermute | solution.py:297
  118.1 30.6 %collective-permute-start.23 = (s32[8,256]{1,0:T(8,128)S(1)}, s32[8,256]{1,0:T(8,128)S(1)}, u32[]{:S(2)}, u32[]{:S(2)}) collective-permute-start(s32[8,256]{1,0:T(8,128)S(1)} %collective-permute-done.22), channel_id=1, source_target_pairs={{0,8},{8,0},{16,24},{24,16},{1,9},{9,1},{17,25},{25,17},{2,10},{10... | collective-permute-start | bytes 24584 | tf_op jit(solution)/shard_map/ppermute | solution.py:297
  119.0 35.0 %collective-permute-start.11 = (f32[256,256]{1,0:T(8,128)}, f32[256,256]{1,0:T(8,128)S(1)}, u32[]{:S(2)}, u32[]{:S(2)}) collective-permute-start(f32[256,256]{1,0:T(8,128)} %get-tuple-element.85.refs_11_), channel_id=1, source_target_pairs={{2,0},{4,2},{6,4},{7,6},{5,7},{3,5},{1,3},{0,1},{10,8},{12,10},{14... | collective-permute-start | bytes 786440 | tf_op jit(solution)/shard_map/ppermute | solution.py:269
  121.0 43.2 %collective-permute-start.7 = (f32[256,256]{1,0:T(8,128)}, f32[256,256]{1,0:T(8,128)S(1)}, u32[]{:S(2)}, u32[]{:S(2)}) collective-permute-start(f32[256,256]{1,0:T(8,128)} %get-tuple-element.85.refs_11_), channel_id=1, source_target_pairs={{0,2},{2,4},{4,6},{6,7},{7,5},{5,3},{3,1},{1,0},{8,10},{10,12},{12... | collective-permute-start | bytes 786440 | tf_op jit(solution)/shard_map/ppermute | solution.py:266
  145.0 24.9 %collective-permute-start.3 = (f32[256,384]{1,0:T(8,128)}, f32[256,384]{1,0:T(8,128)S(1)}, u32[]{:S(2)}, u32[]{:S(2)}) collective-permute-start(f32[256,384]{1,0:T(8,128)} %collective-permute-done.2.refs_6_), channel_id=1, source_target_pairs={{0,2},{2,4},{4,6},{6,7},{7,5},{5,3},{3,1},{1,0},{8,10},{10,12},{12... | collective-permute-start | bytes 1179656 | tf_op jit(solution)/shard_map/ppermute | solution.py:266
  164.2 36.1 %collective-permute-start.8 = (f32[256,256]{1,0:T(8,128)S(1)}, f32[256,256]{1,0:T(8,128)S(1)}, u32[]{:S(2)}, u32[]{:S(2)}) collective-permute-start(f32[256,256]{1,0:T(8,128)S(1)} %collective-permute-done.7.refs_12_), channel_id=1, source_target_pairs={{0,2},{2,4},{4,6},{6,7},{7,5},{5,3},{3,1},{1,0},{8,10},{10,12},{12... | collective-permute-start | bytes 786440 | tf_op jit(solution)/shard_map/ppermute | solution.py:266
  168.6 34.6 %collective-permute-start.27 = (f32[64,1024]{1,0:T(8,128)S(1)}, f32[64,1024]{1,0:T(8,128)S(1)}, u32[]{:S(2)}, u32[]{:S(2)}) collective-permute-start(f32[64,1024]{1,0:T(8,128)S(1)} %fusion.12), channel_id=1, source_target_pairs={{0,1},{1,2},{2,3},{3,4},{8,9},{9,10},{10,11},{11,12},{16,17},{17,1... | collective-permute-start | bytes 786440 | tf_op jit(solution)/shard_map/ppermute | solution.py:286
  200.4 27.9 %collective-permute-start.9 = (f32[256,256]{1,0:T(8,128)S(1)}, f32[256,256]{1,0:T(8,128)S(1)}, u32[]{:S(2)}, u32[]{:S(2)}) collective-permute-start(f32[256,256]{1,0:T(8,128)S(1)} %collective-permute-done.8.refs_13_), channel_id=1, source_target_pairs={{0,2},{2,4},{4,6},{6,7},{7,5},{5,3},{3,1},{1,0},{8,10},{10,12},{12... | collective-permute-start | bytes 786440 | tf_op jit(solution)/shard_map/ppermute | solution.py:266
  200.4 35.8 %collective-permute-start.33 = (f32[64,1024]{1,0:T(8,128)S(1)}, f32[64,1024]{1,0:T(8,128)S(1)}, u32[]{:S(2)}, u32[]{:S(2)}) collective-permute-start(f32[64,1024]{1,0:T(8,128)S(1)} %fusion.12), channel_id=1, source_target_pairs={{0,7},{1,0},{2,1},{3,2},{8,15},{9,8},{10,9},{11,10},{16,23},{17,16... | collective-permute-start | bytes 786440 | tf_op jit(solution)/shard_map/ppermute | solution.py:286
  201.1 35.1 %collective-permute-start.32 = (f32[64,1024]{1,0:T(8,128)S(1)}, f32[64,1024]{1,0:T(8,128)S(1)}, u32[]{:S(2)}, u32[]{:S(2)}) collective-permute-start(f32[64,1024]{1,0:T(8,128)S(1)} %fusion.12), channel_id=1, source_target_pairs={{0,6},{1,7},{2,0},{3,1},{8,14},{9,15},{10,8},{11,9},{16,22},{17,23... | collective-permute-start | bytes 786440 | tf_op jit(solution)/shard_map/ppermute | solution.py:286
  201.8 25.1 %collective-permute-start.28 = (f32[64,1024]{1,0:T(8,128)S(1)}, f32[64,1024]{1,0:T(8,128)S(1)}, u32[]{:S(2)}, u32[]{:S(2)}) collective-permute-start(f32[64,1024]{1,0:T(8,128)S(1)} %fusion.12), channel_id=1, source_target_pairs={{0,2},{1,3},{2,4},{3,5},{8,10},{9,11},{10,12},{11,13},{16,18},{17,... | collective-permute-start | bytes 786440 | tf_op jit(solution)/shard_map/ppermute | solution.py:286
  203.1 25.8 %collective-permute-start.29 = (f32[64,1024]{1,0:T(8,128)S(1)}, f32[64,1024]{1,0:T(8,128)S(1)}, u32[]{:S(2)}, u32[]{:S(2)}) collective-permute-start(f32[64,1024]{1,0:T(8,128)S(1)} %fusion.12), channel_id=1, source_target_pairs={{0,3},{1,4},{2,5},{3,6},{8,11},{9,12},{10,13},{11,14},{16,19},{17,... | collective-permute-start | bytes 786440 | tf_op jit(solution)/shard_map/ppermute | solution.py:286
  228.9 23.7 %collective-permute-start.10 = (f32[256,256]{1,0:T(8,128)S(1)}, f32[256,256]{1,0:T(8,128)S(1)}, u32[]{:S(2)}, u32[]{:S(2)}) collective-permute-start(f32[256,256]{1,0:T(8,128)S(1)} %collective-permute-done.9.refs_14_), channel_id=1, source_target_pairs={{0,2},{2,4},{4,6},{6,7},{7,5},{5,3},{3,1},{1,0},{8,10},{10,12},{12... | collective-permute-start | bytes 786440 | tf_op jit(solution)/shard_map/ppermute | solution.py:266
  236.5 53.1 %collective-permute-start.35 = (f32[4,64,1024]{2,1,0:T(8,128)S(1)}, f32[4,64,1024]{2,1,0:T(8,128)}, u32[]{:S(2)}, u32[]{:S(2)}) collective-permute-start(f32[4,64,1024]{2,1,0:T(8,128)S(1)} %pad_maximum_fusion.1), channel_id=1, source_target_pairs={{0,16},{8,24},{16,0},{24,8},{1,17},{9,25},{17,1},{25,9},{2,18},{10... | collective-permute-start | bytes 3145736 | tf_op jit(solution)/shard_map/ppermute | solution.py:297
  238.2 202.9 %collective-permute-start.34 = (f32[4,64,1024]{2,1,0:T(8,128)S(1)}, f32[4,64,1024]{2,1,0:T(8,128)}, u32[]{:S(2)}, u32[]{:S(2)}) collective-permute-start(f32[4,64,1024]{2,1,0:T(8,128)S(1)} %pad_maximum_fusion.1), channel_id=1, source_target_pairs={{0,8},{8,0},{16,24},{24,16},{1,9},{9,1},{17,25},{25,17},{2,10},{10... | collective-permute-start | bytes 3145736 | tf_op jit(solution)/shard_map/ppermute | solution.py:297
  289.7 151.4 %collective-permute-start.36 = (f32[4,64,1024]{2,1,0:T(8,128)}, f32[4,64,1024]{2,1,0:T(8,128)}, u32[]{:S(2)}, u32[]{:S(2)}) collective-permute-start(f32[4,64,1024]{2,1,0:T(8,128)} %collective-permute-done.35), channel_id=1, source_target_pairs={{0,8},{8,0},{16,24},{24,16},{1,9},{9,1},{17,25},{25,17},{2,10},{10... | collective-permute-start | bytes 3145736 | tf_op jit(solution)/shard_map/ppermute | solution.py:297
  423.3 17.6 %collective-permute-start.38 = (f32[10,128,128]{2,1,0:T(8,128)}, f32[10,128,128]{2,1,0:T(8,128)}, u32[]{:S(2)}, u32[]{:S(2)}) collective-permute-start(f32[10,128,128]{2,1,0:T(8,128)} %get-tuple-element.120.refs_6_), channel_id=1, source_target_pairs={{0,16},{8,24},{16,0},{24,8},{1,17},{9,25},{17,1},{25,9},{2,18},{10... | collective-permute-start | bytes 1966088 | tf_op jit(solution)/shard_map/ppermute | solution.py:297
  441.3 20.0 %collective-permute-start.43 = (f32[10,128,128]{2,1,0:T(8,128)}, f32[10,128,128]{2,1,0:T(8,128)}, u32[]{:S(2)}, u32[]{:S(2)}) collective-permute-start(f32[10,128,128]{2,1,0:T(8,128)} %get-tuple-element.120.refs_6_), channel_id=1, source_target_pairs={{0,8},{8,0},{16,24},{24,16},{1,9},{9,1},{17,25},{25,17},{2,10},{10... | collective-permute-start | bytes 1966088 | tf_op jit(solution)/shard_map/ppermute | solution.py:297
  447.2 14.1 %collective-permute-start.41 = (f32[256,512]{1,0:T(8,128)}, f32[256,512]{1,0:T(8,128)S(1)}, u32[]{:S(2)}, u32[]{:S(2)}) collective-permute-start(f32[256,512]{1,0:T(8,128)} %get-tuple-element.121.refs_4_), channel_id=1, source_target_pairs={{0,16},{8,24},{16,0},{24,8},{1,17},{9,25},{17,1},{25,9},{2,18},{10... | collective-permute-start | bytes 1572872 | tf_op jit(solution)/shard_map/ppermute | solution.py:297
  452.9 72.1 %collective-permute-start.40 = (f32[256,512]{1,0:T(8,128)S(1)}, f32[256,512]{1,0:T(8,128)S(1)}, u32[]{:S(2)}, u32[]{:S(2)}) collective-permute-start(f32[256,512]{1,0:T(8,128)S(1)} %copy-done.16), channel_id=1, source_target_pairs={{0,8},{8,0},{16,24},{24,16},{1,9},{9,1},{17,25},{25,17},{2,10},{10... | collective-permute-start | bytes 1572872 | tf_op jit(solution)/shard_map/ppermute | solution.py:297
  461.3 63.7 %collective-permute-start.42 = (f32[256,512]{1,0:T(8,128)S(1)}, f32[256,512]{1,0:T(8,128)}, u32[]{:S(2)}, u32[]{:S(2)}) collective-permute-start(f32[256,512]{1,0:T(8,128)S(1)} %collective-permute-done.41.refs_6_), channel_id=1, source_target_pairs={{0,8},{8,0},{16,24},{24,16},{1,9},{9,1},{17,25},{25,17},{2,10},{10... | collective-permute-start | bytes 1572872 | tf_op jit(solution)/shard_map/ppermute | solution.py:297
  (48 other events, 990.4 us)
Sparse Core Ops, SparseCore 0:
  63.5 102.6 all-gather.5
  238.3 87.4 all-gather.7

commit v3 on v2

v3 whole, which is shorter than its diff:
```python
import functools

import jax
import jax.numpy as jnp
import numpy as np
from jax import lax
from jax.experimental import pallas as pl
from jax.experimental.pallas import tpu as pltpu
from jax.sharding import PartitionSpec as P

BLOCK = 128
STAGE = 512
CAP = 128
LANES = 128
SUB = 8
VMEM_LIMIT = 60 << 20

HIGHEST_PRECISION = lax.Precision.HIGHEST
NT = (((1,), (1,)), ((), ()))
NN = (((1,), (0,)), ((), ()))
F32 = jnp.float32
BF16 = jnp.bfloat16


def split(x):
    high = x.astype(BF16)
    return high, (x - high.astype(F32)).astype(BF16)


def dot(a, b, dims):
    return lax.dot_general(a, b, dims, preferred_element_type=F32)


def dot3(a, b, dims):
    return dot(a[0], b[0], dims) + (dot(a[0], b[1], dims) + dot(a[1], b[0], dims))


def ds(start, size):
    return pl.ds(pl.multiple_of(start, size), size)


def tiles(rows, cols, body, tile=256):
    tr, tc = min(tile, rows), min(tile, cols)
    nr, nc = rows // tr, cols // tc

    def step(t, carry):
        body((t // nc) * tr, tr, (t % nc) * tc, tc)
        return carry

    lax.fori_loop(0, nr * nc, step, 0)


def lane(x, c):
    return jnp.broadcast_to(x[:, c : c + 1], x.shape)


def sub(x, r):
    return jnp.broadcast_to(x[r : r + 1, :], x.shape)


def tree_sum(terms):
    terms = list(terms)
    while len(terms) > 1:
        terms = [
            terms[i] + terms[i + 1] if i + 1 < len(terms) else terms[i]
            for i in range(0, len(terms), 2)
        ]
    return terms[0]


def invert_small(s):
    n = len(s)
    s = list(s)
    row_id = lax.broadcasted_iota(jnp.int32, (SUB, LANES), 0)
    m = [None] * n
    for p in range(0, n, 2):
        q = p + 1
        a, b, d = sub(s[p], p), sub(s[q], p), sub(s[q], q)
        det = a * d - b * b
        scale = 1.0 / det
        ra = lax.rsqrt(a)
        rq = lax.rsqrt(det) * (a * ra)
        ba = b * ra * ra
        at_p, at_q = row_id == p, row_id == q
        sp, sq = s[p], s[q]
        fp, fq = (sp * d - sq * b) * scale, (sq * a - sp * b) * scale
        for k in range(n):
            if k in (p, q):
                continue
            u, v = sub(s[k], p), sub(s[k], q)
            if k < p:
                m[k] = jnp.where(at_p, -(u * ra), jnp.where(at_q, (u * ba - v) * rq, m[k]))
            s[k] = jnp.where(at_p, sub(fp, k), jnp.where(at_q, sub(fq, k), s[k] - (fp * u + fq * v)))
        s[p] = jnp.where(at_p, -(d * scale), jnp.where(at_q, b * scale, fp))
        s[q] = jnp.where(at_q, -(a * scale), jnp.where(at_p, b * scale, fq))
        m[p] = jnp.where(at_p, ra, jnp.where(at_q, -(ba * rq), 0.0))
        m[q] = jnp.where(at_q, rq, 0.0)
    return s, m


def factor_block(rows):
    n = len(rows)
    row_id = lax.broadcasted_iota(jnp.int32, (SUB, LANES), 0)
    lane_id = lax.broadcasted_iota(jnp.int32, (SUB, LANES), 1)
    a = list(rows)
    out = []
    for s in range(n):
        here = jnp.logical_and(lane_id >= SUB * s, lane_id < SUB * (s + 1))
        cols = [lane(a[s], SUB * s + r) for r in range(SUB)]
        r = jnp.where(here, jnp.where(row_id + SUB * s == lane_id, 1.0, 0.0), a[s])
        rb = [sub(r, q) for q in range(SUB)]
        t, m = invert_small(cols)
        v = tree_sum(m[q] * rb[q] for q in range(SUB))
        out.append(jnp.where(lane_id < SUB * (s + 1), v, 0.0))
        if s + 1 == n:
            break
        y = tree_sum(t[q] * rb[q] for q in range(SUB))
        yb = [sub(y, q) for q in range(SUB)]
        for i in range(s + 1, n):
            w = [lane(a[i], SUB * s + q) for q in range(SUB)]
            a[i] = jnp.where(here, 0.0, a[i]) + tree_sum(w[q] * yb[q] for q in range(SUB))
    return out


def subtract_products(dst, rows, cols, ah, al, bh, bl, depth):
    if depth == 0:
        return

    def body(r, nr, c, nc):
        a = (ah[ds(r, nr), :depth], al[ds(r, nr), :depth])
        b = (bh[ds(c, nc), :depth], bl[ds(c, nc), :depth])
        dst[ds(r, nr), ds(c, nc)] = dst[ds(r, nr), ds(c, nc)] - dot3(a, b, NT)

    tiles(rows, cols, body)


def times_inverse(src, outh, outl, out_at, rows, width, invh, invl):
    def body(r, nr, c, nc):
        a = split(src[ds(r, nr), :])
        b = (invh[ds(c, nc), :], invl[ds(c, nc), :])
        high, low = split(dot3(a, b, NT))
        outh[ds(r, nr), pl.ds(pl.multiple_of(out_at + c, nc), nc)] = high
        outl[ds(r, nr), pl.ds(pl.multiple_of(out_at + c, nc), nc)] = low

    tiles(rows, width, body)


def clear_inverse(invh, invl):
    invh[...] = jnp.zeros(invh.shape, BF16)
    invl[...] = jnp.zeros(invl.shape, BF16)


def inverse_row(r, at, width, lh, ll, invh, invl):
    here = ds(r * LANES, LANES)
    left = lax.broadcasted_iota(jnp.int32, (LANES, width), 1) < r * LANES
    none = jnp.zeros((LANES, width), BF16)
    low = tuple(jnp.where(left, ref[here, at : at + width], none) for ref in (lh, ll))
    mixed = split(dot3(low, (invh[...], invl[...]), NN))
    high, low = split(-dot3((invh[here, here], invl[here, here]), mixed, NN))
    invh[here, :] = jnp.where(left, high, invh[here, :])
    invl[here, :] = jnp.where(left, low, invl[here, :])


def factor_panels(start, stop, s_ref, at, width, lh, ll, invh, invl, job=None):
    row_id = lax.broadcasted_iota(jnp.int32, (width, LANES), 0)
    col_id = lax.broadcasted_iota(jnp.int32, (width, LANES), 1)
    none = jnp.zeros((width, LANES), BF16)
    last = width // LANES - 1

    def panel(p, carry):
        first = p * LANES
        here = ds(first, LANES)
        block = [
            s_ref[pl.ds(pl.multiple_of(first + SUB * i, SUB), SUB), here]
            for i in range(LANES // SUB)
        ]
        before = jnp.maximum(p - 1, 0)
        done = ds(at + before * LANES, LANES)
        later = jnp.logical_and(row_id >= first + LANES, p > 0)
        old = tuple(jnp.where(later, ref[:, done], none) for ref in (lh, ll))
        for c in range(1, last + 1):
            cols = slice(c * LANES, (c + 1) * LANES)
            some = (old[0][cols], old[1][cols])
            s_ref[c * LANES :, cols] = s_ref[c * LANES :, cols] - dot3(
                (old[0][c * LANES :], old[1][c * LANES :]), some, NT
            )
        inverse_row(before, at, width, lh, ll, invh, invl)
        if job is not None:
            job(p)

        inv = split(jnp.concatenate(factor_block(block), axis=0))
        invh[here, here] = inv[0]
        invl[here, here] = inv[1]
        solved = dot3(split(s_ref[:, here]), inv, NT)
        high, low = split(jnp.where(row_id >= col_id + first, solved, 0.0))
        lh[:, ds(at + first, LANES)] = high
        ll[:, ds(at + first, LANES)] = low
        below = row_id >= first + LANES
        following = ds(jnp.minimum(p + 1, last) * LANES, LANES)
        some = (lh[following, ds(at + first, LANES)], ll[following, ds(at + first, LANES)])
        s_ref[:, following] = s_ref[:, following] - dot3(
            (jnp.where(below, high, none), jnp.where(below, low, none)), some, NT
        )
        return carry

    lax.fori_loop(start, stop, panel, 0)
    if stop == last + 1:
        inverse_row(last, at, width, lh, ll, invh, invl)


def solve_some(rows, src, q, width, xh, xl, l_rows, inv):
    part = src
    if q > 0:
        deep = q * width
        part = part - dot3(
            (xh[rows, :deep], xl[rows, :deep]), (l_rows[0][:, :deep], l_rows[1][:, :deep]), NT
        )
    high, low = split(dot3(split(part), (inv[0][...], inv[1][...]), NT))
    xh[rows, q * width : (q + 1) * width] = high
    xl[rows, q * width : (q + 1) * width] = low


def vmem_call(body, out_shapes, in_kinds, scratch, cost=None, aliases=None):
    specs = [pl.BlockSpec(memory_space=pltpu.SMEM if k else pltpu.VMEM) for k in in_kinds]
    return pl.pallas_call(
        body,
        out_shape=out_shapes,
        in_specs=specs,
        out_specs=[pl.BlockSpec(memory_space=pltpu.VMEM)] * len(out_shapes),
        scratch_shapes=scratch,
        compiler_params=pltpu.CompilerParams(vmem_limit_bytes=VMEM_LIMIT),
        cost_estimate=cost,
        input_output_aliases=aliases or {},
    )


def shaped(shape, dtype):
    return jax.ShapeDtypeStruct(shape, dtype)


def send_plan(groups, per_stage):
    pairs = [
        (j, i)
        for i in range(groups)
        for j in range(i)
        if not (i == j + 1 and j % 2 == 0)
    ]
    pairs.sort(key=lambda pair: (pair[1] // per_stage, pair))
    taken = {}

    last = {}

    def place(pair, seen):
        for rnd in range(last[pair]):
            for dev in (pair[1], pair[0]):
                slot = (rnd, dev)
                if slot in seen:
                    continue
                seen.add(slot)
                if slot not in taken or place(taken[slot], seen):
                    taken[slot] = pair
                    return True
        return False

    limit = 1
    for pair in pairs:
        last[pair] = limit
        while not place(pair, set()):
            limit += 1
            last[pair] = limit
    rounds = 1 + max((slot[0] for slot in taken), default=-1)
    table = np.full((max(rounds, 1), groups), -1, np.int32)
    for (rnd, dev), (j, i) in taken.items():
        table[rnd, dev] = j if dev == i else i
    return table[:rounds]


def ring_order(groups):
    return [i for i in range(0, groups, 2)] + [i for i in range(groups - 1, 0, -2)]


def ring_gather(chunk, axis, groups):
    order = ring_order(groups)
    ahead = [(order[i], order[(i + 1) % groups]) for i in range(groups)]
    back = [(b, a) for a, b in ahead]
    out = [chunk]
    going, coming = chunk, chunk
    steps_ahead = groups // 2
    steps_back = groups - 1 - steps_ahead
    aheads, backs = [], []
    for step in range(steps_ahead):
        going = lax.ppermute(going, axis, ahead)
        aheads.append(going)
        if step < steps_back:
            coming = lax.ppermute(coming, axis, back)
            backs.append(coming)
    return out + aheads + backs


class Ring:
    def __init__(self, chunk, axis, groups):
        order = ring_order(groups)
        self.axis = axis
        self.ahead = [(order[i], order[(i + 1) % groups]) for i in range(groups)]
        self.back = [(b, a) for a, b in self.ahead]
        self.steps = groups // 2
        self.steps_back = groups - 1 - self.steps
        self.own = chunk
        self.aheads, self.backs = [], []
        self.going = self.coming = chunk

    def advance(self, token):
        if len(self.aheads) < self.steps:
            self.going = lax.ppermute(self.going, self.axis, self.ahead)
            self.aheads.append(self.going)
            if len(self.backs) < self.steps_back:
                self.coming = lax.ppermute(self.coming, self.axis, self.back)
                self.backs.append(self.coming)
        return token

    def arrive(self, token, beside):
        token, self.going, self.coming, _ = lax.optimization_barrier((token, self.going, self.coming, beside))
        return token

    def finish(self):
        while len(self.aheads) < self.steps:
            self.advance(None)

    def slots(self):
        return [self.own] + self.aheads + self.backs


def slot_owners(axis, groups):
    order = np.array(ring_order(groups), np.int32)
    place = np.argsort(order)
    me = jnp.asarray(place)[lax.axis_index(axis)]
    steps_ahead = groups // 2
    steps_back = groups - 1 - steps_ahead
    shifts = [0] + [-s for s in range(1, steps_ahead + 1)] + list(range(1, steps_back + 1))
    return jnp.asarray(order)[(me + jnp.asarray(shifts, jnp.int32)) % groups].astype(jnp.int32)


def direct_gather(x, axis, groups, sources):
    moved = [
        lax.ppermute(x, axis, [(s, (s + k) % groups) for s in range(sources)])
        for k in range(1, groups)
    ]
    return [x] + moved


def bulk_gather(x, axis, size):
    held = {0: x}
    step = size // 2
    while step:
        for mask in list(held):
            held[mask | step] = lax.ppermute(held[mask], axis, [(i, i ^ step) for i in range(size)])
        step //= 2
    return [held[m] for m in range(size)]


def after(x, dep):
    return lax.optimization_barrier((x, dep))[0]


def assemble_rows(q, width, own, groups, owner_ref, table_ref, chunks, late_rounds, a_ref):
    per_stage = width // own
    first_group = q * per_stage
    for k in range(groups):
        f = owner_ref[k]

        @pl.when(f // per_stage == q)
        def _(f=f, k=k):
            chunk = chunks[0][k]
            at = (f - first_group) * own
            a_ref[ds(at, own), ds(f * own, own)] = chunk[:own, :own]
            half = own // 2
            odd = f % 2
            row = (f - odd + 1 - first_group) * own + odd * half
            a_ref[ds(row, half), ds((f - odd) * own, own)] = chunk[:own, own:].T

    sent = [(rnd, chunk, 0) for rnd, chunk in enumerate(chunks[1:-1]) if chunk]
    sent += [(rnd, chunks[-1], at * own) for at, rnd in late_rounds]
    for rnd, chunk, cut in sent:
        for k in range(groups):
            f = owner_ref[k]
            c = table_ref[rnd, f]
            high = jnp.maximum(f, c)
            low = jnp.minimum(f, c)
            mine = jnp.logical_and(c >= 0, high // per_stage == q)
            row = jnp.clip((high - first_group) * own, 0, width - own)
            col = jnp.clip(low * own, 0, (q + 1) * width - own)

            @pl.when(jnp.logical_and(mine, f > c))
            def _(chunk=chunk, cut=cut, k=k, row=row, col=col):
                a_ref[ds(row, own), ds(col, own)] = chunk[k][:, cut : cut + own]

            @pl.when(jnp.logical_and(mine, f < c))
            def _(chunk=chunk, cut=cut, k=k, row=row, col=col):
                a_ref[ds(row, own), ds(col, own)] = chunk[k][:, cut : cut + own].T


def child_stage(q, width, own, groups, late_rounds, counts, span, shapes, couples, landing, refs):
    start, stop = span
    panels = width // LANES
    refs = list(refs)

    def take(count):
        out, refs[:count] = refs[:count], []
        return out

    (place_ref,) = take(1)
    if start == 0:
        owner_ref, table_ref = take(2)
        chunks = [take(count) for count in counts]
    else:
        state = take(5)
    prev_lh, prev_ll, prev_ih, prev_il = (take(q) for _ in range(4))
    if couples:
        b_ref = take(1)[0]
        old_x = take(2) if q > 1 else None
    if landing:
        raw_ref = take(1)[0]
    s_out, lh, ll, invh, invl = take(5)
    if couples:
        xh, xl = take(2)
    if stop == panels:
        own_ref = take(1)[0]
    if landing:
        th, tl, sq_ref = take(3)
    if start == 0:
        a_ref = take(1)[0]
    if landing:
        t_ref = take(1)[0]

    if start == 0:
        assemble_rows(q, width, own, groups, owner_ref, table_ref, chunks, late_rounds, a_ref)
        for j in range(q):
            part = a_ref.at[:, j * width : (j + 1) * width]
            subtract_products(part, width, width, lh, ll, prev_lh[j], prev_ll[j], j * width)
            times_inverse(part, lh, ll, j * width, width, width, prev_ih[j], prev_il[j])
        s_out[...] = a_ref[:, q * width : (q + 1) * width]
        subtract_products(s_out, width, width, lh, ll, lh, ll, q * width)
        clear_inverse(invh, invl)
    else:
        for new, held in zip((s_out, lh, ll, invh, invl), state, strict=True):
            new[...] = held[...]
    if couples and q > 1:
        xh[:, : (q - 1) * width] = old_x[0][...]
        xl[:, : (q - 1) * width] = old_x[1][...]
    if landing:
        total, front, sources, cap = shapes
        share = cap * sources // front
        for f in range(front):
            at = (f % sources) * cap + (f // sources) * share
            t_ref[at : at + share, :] = raw_ref[f * share : (f + 1) * share, :]

    def job(p):
        if couples:
            some = own // (stop - start)
            rows = ds((p - start) * some, some)
            solve_some(
                rows, b_ref[rows, :], q - 1, width, xh, xl,
                (prev_lh[q - 1], prev_ll[q - 1]), (prev_ih[q - 1], prev_il[q - 1]),
            )
        if landing:
            some = total // (stop - start)
            rows = ds((p - start) * some, some)
            for j in range(q):
                solve_some(
                    rows, t_ref[rows, j * width : (j + 1) * width], j, width, th, tl,
                    (prev_lh[j], prev_ll[j]), (prev_ih[j], prev_il[j]),
                )

    factor_panels(start, stop, s_out, q * width, width, lh, ll, invh, invl, job)
    if stop == panels:
        at = place_ref[0]
        own_ref[...] = lh[ds(at, own), :].astype(F32) + ll[ds(at, own), :].astype(F32)
    if landing:
        part = t_ref.at[:, q * width : (q + 1) * width]
        subtract_products(part, total, width, th, tl, lh, ll, q * width)
        times_inverse(part, th, tl, q * width, total, width, invh, invl)

        def square(t, carry):
            i, j = carry
            a = (th[ds(i * LANES, LANES), :], tl[ds(i * LANES, LANES), :])
            b = (th[ds(j * LANES, LANES), :], tl[ds(j * LANES, LANES), :])
            sq_ref[t] = dot3(a, b, NT)
            end = j == i
            return (jnp.where(end, i + 1, i), jnp.where(end, 0, j + 1))

        blocks = total // LANES
        lax.fori_loop(0, blocks * (blocks + 1) // 2, square, (jnp.int32(0), jnp.int32(0)))


def own_kernel(first, stages, width, refs):
    refs = list(refs)

    def take(count):
        out, refs[:count] = refs[:count], []
        return out

    (b_ref,) = take(1)
    old_h, old_l = take(2) if first > 0 else (None, None)
    left = stages - first
    lh, ll, ih, il = (take(left) for _ in range(4))
    th, tl = take(2)
    x_ref, con_ref = take(2)
    xh, xl = take(2)
    own = b_ref.shape[0]
    if first > 0:
        xh[:, : first * width] = old_h[...]
        xl[:, : first * width] = old_l[...]
    for k in range(left):
        q = first + k
        for c in range(1):
            part = b_ref.at[:, k * width : (k + 1) * width]
            x_ref[:, q * width : (q + 1) * width] = part[...]
            part = x_ref.at[:, q * width : (q + 1) * width]
            subtract_products(part, own, width, xh, xl, lh[k], ll[k], q * width)
            times_inverse(part, xh, xl, q * width, own, width, ih[k], il[k])
    x_ref[...] = xh[...].astype(F32) + xl[...].astype(F32)

    def body(r, nr, c, nc):
        a = (xh[ds(r, nr), :], xl[ds(r, nr), :])
        b = (th[ds(c, nc), :], tl[ds(c, nc), :])
        con_ref[ds(r, nr), ds(c, nc)] = dot3(a, b, NT)

    tiles(own, con_ref.shape[1], body)


def parent_kernel(children, blocks, width, sources, refs):
    refs = list(refs)
    place_ref, spread_ref = refs[:2]
    tops, squares = refs[2 : 2 + children], refs[2 + children : 2 + 2 * children]
    lh, ll, invh, invl, lower, s_ref, top_ref = refs[2 + 2 * children :]
    pivots = lh.shape[0]
    dense = pivots // blocks
    groups, part_rows, _ = tops[0].shape
    spreads = groups // sources
    piece = part_rows * spreads
    for m in range(children):
        g = place_ref[2] ^ m
        for f in range(groups):
            at = (f % sources) * (children * piece) + g * piece + (f // sources) * part_rows
            top_ref[ds(at, part_rows), :] = tops[m][f]
    for i in range(blocks):
        for j in range(i + 1):
            at = i * (i + 1) // 2 + j
            parts = []
            for c in range(children):
                left = spread_ref[i, :, c * LANES : (c + 1) * LANES]
                high, low = split(squares[c][at])
                parts.append(dot(left, high, NN) + dot(left, low, NN))
            high, low = split(jnp.concatenate(parts, axis=1))
            right = spread_ref[j]
            rows = slice(i * dense, (i + 1) * dense)
            cols = slice(j * dense, (j + 1) * dense)
            s_ref[rows, cols] = top_ref[rows, cols] - (
                dot(high, right, NT) + dot(low, right, NT)
            )
    for q in range(pivots // width):
        rows = slice(q * width, (q + 1) * width)
        lhq, llq = lh.at[rows, :], ll.at[rows, :]
        if q + 1 < pivots // width:
            lhq[:, (q + 1) * width :] = jnp.zeros((width, pivots - (q + 1) * width), BF16)
            llq[:, (q + 1) * width :] = jnp.zeros((width, pivots - (q + 1) * width), BF16)
        for j in range(q):
            part = s_ref.at[rows, j * width : (j + 1) * width]
            cut = slice(j * width, (j + 1) * width)
            subtract_products(part, width, width, lhq, llq, lh.at[cut, :], ll.at[cut, :], j * width)
            times_inverse(part, lhq, llq, j * width, width, width, invh.at[j], invl.at[j])
        part = s_ref.at[rows, q * width : (q + 1) * width]
        subtract_products(part, width, width, lhq, llq, lhq, llq, q * width)
        clear_inverse(invh.at[q], invl.at[q])
        factor_panels(0, width // LANES, part, q * width, width, lhq, llq, invh.at[q], invl.at[q])
    lower[...] = lh[...].astype(F32) + ll[...].astype(F32)


def rest_kernel(children, blocks, width, refs):
    refs = list(refs)
    place_ref, rows_ref, route_ref, spread_ref = refs[:4]
    con_refs = refs[4 : 4 + children]
    lh, ll, invh, invl, out_ref, s_ref, xh, xl = refs[4 + children :]
    pivots = lh.shape[0]
    count = rows_ref.shape[0]
    dense = pivots // blocks
    at = place_ref[1]

    @pl.when(at < pivots)
    def _():
        row = ds(jnp.minimum(at, pivots - count), count)
        out_ref[...] = lh[row, :].astype(F32) + ll[row, :].astype(F32)

    @pl.when(at >= pivots)
    def _():
        routed = []
        for c in range(children):
            high, low = split(con_refs[c][...])
            route = route_ref[c]
            routed.append(split(dot(route, high, NN) + dot(route, low, NN)))
        for b in range(blocks):
            lanes = slice(b * LANES, (b + 1) * LANES)
            high = jnp.concatenate([routed[c][0][:, lanes] for c in range(children)], axis=1)
            low = jnp.concatenate([routed[c][1][:, lanes] for c in range(children)], axis=1)
            right = spread_ref[b]
            cols = slice(b * dense, (b + 1) * dense)
            s_ref[:, cols] = rows_ref[:, cols] - (dot(high, right, NT) + dot(low, right, NT))
        for q in range(pivots // width):
            cut = slice(q * width, (q + 1) * width)
            part = s_ref.at[:, cut]
            subtract_products(part, count, width, xh, xl, lh.at[cut, :], ll.at[cut, :], q * width)
            times_inverse(part, xh, xl, q * width, count, width, invh.at[q], invl.at[q])
        out_ref[...] = xh[...].astype(F32) + xl[...].astype(F32)


def on_device(child_pivot, child_coupling, parent_arrow, row_map, block_pattern):
    front = lax.axis_size("front")
    bulk = lax.axis_size("bulk")
    me = lax.axis_index("front")
    mine = child_pivot[0]
    coupling = child_coupling[0]
    own, total = mine.shape
    count, pivots = parent_arrow.shape
    width = min(STAGE, total)
    stages = total // width
    per_stage = width // own
    first_row = (lax.axis_index("bulk") * front + me) * count
    sources = pivots // count
    cap = min(CAP, count, own)
    blocks = sources * cap // LANES

    table = send_plan(front, per_stage)
    rounds = table.shape[0]
    bulk_me = lax.axis_index("bulk")
    early = max(
        (r + 1 for r in range(rounds) for f, c in enumerate(table[r]) if c >= 0 and max(f, c) // per_stage <= 1),
        default=0,
    )
    half = own // 2
    own_map = row_map[0]
    own_block = lax.dynamic_slice_in_dim(mine, me * own, own, 1)
    even = lax.dynamic_slice_in_dim(mine, jnp.minimum(me + 1, front - 1) * own, half, 1)
    odd = lax.dynamic_slice_in_dim(mine[half:], jnp.maximum(me - 1, 0) * own, own, 1).T
    head = jnp.concatenate([own_block, jnp.where(me % 2 == 0, even, odd)], axis=1)
    tail = jnp.pad(own_map.astype(F32)[None], ((0, SUB - 1), (0, half)))
    chunks = [jnp.concatenate([head, tail], axis=0)]
    for rnd in range(rounds):
        col = jnp.maximum(jnp.asarray(table[rnd])[me], 0)
        chunks.append(lax.dynamic_slice_in_dim(mine, col * own, own, 1))
    owners = slot_owners("front", front)
    gathered = [ring_gather(chunks[0], "front", front)]
    started = gathered[0][-1]
    for rnd in range(1, early + 1):
        gathered.append(ring_gather(after(chunks[rnd], gathered[-1][-1]), "front", front))
    late = Ring(after(jnp.concatenate(chunks[early + 1 :], axis=1), gathered[-1][-1]), "front", front)
    table_in = jnp.asarray(table)
    place = jnp.stack([(me % per_stage) * own, first_row, bulk_me]).astype(jnp.int32)

    own_lands = own_map < pivots
    own_rank = jnp.where(own_lands, jnp.cumsum(own_lands.astype(jnp.int32)) - 1, -1)
    pick = (own_rank[None, :] == jnp.arange(cap)[:, None]).astype(F32)
    spreads = front // sources

    def spread_out(x):
        rows = x.shape[0] // spreads
        part = x[:rows]
        for k in range(1, spreads):
            moved = lax.ppermute(
                x[k * rows : (k + 1) * rows],
                "front",
                [(s, s + k * sources) for s in range(sources)],
            )
            part = jnp.where(me // sources == k, moved, part)
        return part

    compact = jnp.dot(pick, coupling, precision=HIGHEST_PRECISION)
    raw_landing = lax.all_gather(spread_out(after(compact, started)), "front", axis=0, tiled=True)

    block_rows = (first_row + jnp.arange(count)) // BLOCK
    row_mask = jnp.take(block_pattern, block_rows, axis=0).astype(F32)
    arrow = parent_arrow * jnp.repeat(row_mask, BLOCK, axis=1)
    piece = count // bulk
    part = after(arrow, gathered[early][-1])
    pieces = part[:piece]
    for g in range(1, bulk):
        moved = lax.ppermute(part[g * piece : (g + 1) * piece], "bulk", [(0, g)])
        pieces = jnp.where(bulk_me == g, moved, pieces)
    line = lax.all_gather(after(spread_out(pieces), raw_landing), "front", axis=0, tiled=False)

    my_maps = jnp.stack([slot[own, :own] for slot in gathered[0]])
    ordered = jnp.sum(
        jnp.where(owners[None, :, None] == jnp.arange(front)[:, None, None], my_maps[None], 0.0), axis=1
    )
    maps = jnp.stack(bulk_gather(ordered, "bulk", bulk)).astype(jnp.int32)
    lands = maps[:, :sources] < pivots
    rank = jnp.cumsum(lands.astype(jnp.int32), axis=2) - 1
    overflow = jnp.any(rank[:, :, -1] >= cap)
    chosen = jnp.where(lands, rank, -1)[:, :, None, :] == jnp.arange(cap)[:, None]
    target = jnp.max(jnp.where(chosen, maps[:, :sources, None, :], -1), axis=3)
    target = jnp.where(overflow, -1, target).reshape(bulk, blocks, LANES)
    dense = pivots // blocks
    rows_of = (jnp.arange(blocks)[:, None] * dense + jnp.arange(dense)[None, :])[:, :, None, None]
    spread = (jnp.transpose(target, (1, 0, 2))[:, None] == rows_of).astype(BF16)
    spread = spread.reshape(blocks, dense, bulk * LANES)
    route = (
        lax.dynamic_index_in_dim(maps, me, 1, False)[:, None, :]
        == (first_row + jnp.arange(count))[None, :, None]
    ).astype(BF16)

    panels = width // LANES
    total_landing = sources * cap
    lh, ll, ih, il, owned = ([] for _ in range(5))
    xs = None
    for q in range(stages):
        final = q == stages - 1
        if q == 2 or (q < 2 and final):
            late.finish()
        split_at = [0, panels // 2, panels] if q < 2 and not final else [0, panels]
        needed = [
            any(c >= 0 and max(f, c) // per_stage == q for f, c in enumerate(row)) for row in table
        ]
        used = [gathered[0]] + [gathered[rnd + 1] if needed[rnd] else [] for rnd in range(early)]
        late_rounds = [(rnd - early, rnd) for rnd in range(early, rounds) if needed[rnd]]
        used.append(late.slots() if late_rounds else [])
        counts = [len(u) for u in used]
        deep = (q + 1) * width
        state = None
        for start, stop in zip(split_at[:-1], split_at[1:], strict=True):
            couples = 0 < q < stages - 1 and stop == panels
            landing = final
            if q < 2 and not final:
                place = late.advance(place)
            operands = [place]
            smem = 1
            aliases = {}
            if start == 0:
                operands += [owners, table_in] + [x for u in used for x in u]
                smem = 3
            else:
                operands += state
                aliases = {1 + k: k for k in range(5)}
            operands += lh + ll + ih + il
            if couples:
                operands.append(coupling[:, (q - 1) * width : q * width])
                if q > 1:
                    operands += xs
            if landing:
                operands.append(raw_landing)
            outs = [
                shaped((width, width), F32),
                shaped((width, deep), BF16),
                shaped((width, deep), BF16),
                shaped((width, width), BF16),
                shaped((width, width), BF16),
            ]
            scratch = []
            if couples:
                outs += [shaped((own, q * width), BF16)] * 2
            if stop == panels:
                outs.append(shaped((own, deep), F32))
            if landing:
                outs += [shaped((total_landing, total), BF16)] * 2
                outs.append(shaped((blocks * (blocks + 1) // 2, LANES, LANES), F32))
            if start == 0:
                scratch.append(pltpu.VMEM((width, deep), F32))
            if landing:
                scratch.append(pltpu.VMEM((total_landing, total), F32))
            out = list(
                vmem_call(
                    functools.partial(
                        lambda *refs, args: child_stage(*args, refs),
                        args=(
                            q, width, own, front, late_rounds, counts, (start, stop),
                            (total_landing, front, sources, cap), couples, landing,
                        ),
                    ),
                    outs,
                    [True] * smem + [False] * (len(operands) - smem),
                    scratch,
                    pl.CostEstimate(
                        flops=6_000_000_000 * (stop - start), bytes_accessed=1 << 20, transcendentals=0
                    ),
                    aliases,
                )(*operands)
            )
            state = out[:5]
            rest = out[5:]
            if couples:
                xs, rest = rest[:2], rest[2:]
            if stop == panels:
                owned.append(rest[0])
                rest = rest[1:]
            if landing:
                th, tl, squares = rest
            if q < 2 and not final:
                place = late.arrive(place, state[0])
        for held, new in zip((lh, ll, ih, il), state[1:], strict=True):
            held.append(new)

    lower_rows = jnp.zeros((own, total), F32)
    for q in range(stages):
        padded = jnp.pad(owned[q], ((0, 0), (0, total - (q + 1) * width)))
        lower_rows = jnp.where(me // per_stage == q, padded, lower_rows)

    all_squares = bulk_gather(squares, "bulk", bulk)
    solved = max(stages - 2, 0)
    operands = [coupling[:, solved * width :]] + (xs if solved > 0 else [])
    operands += lh[solved:] + ll[solved:] + ih[solved:] + il[solved:] + [th, tl]
    x_own, con = vmem_call(
        lambda *refs: own_kernel(solved, stages, width, refs),
        [shaped((own, total), F32), shaped((own, total_landing), F32)],
        [False] * len(operands),
        [pltpu.VMEM((own, total), BF16)] * 2,
        pl.CostEstimate(flops=10_000_000_000, bytes_accessed=1 << 20, transcendentals=0),
    )(*operands)

    def unchanged(lines, arrow, x_own):
        return lines, arrow

    def landing_whole(lines, arrow, x_own):
        slot = own_map - me * count
        hits = (slot[:, None] == jnp.arange(count)[None, :]).astype(F32)
        piece_rows = jnp.dot(hits.T, x_own, precision=HIGHEST_PRECISION)
        whole = lax.all_gather(piece_rows, "front", axis=0, tiled=True)[:pivots]
        reached = jnp.dot(x_own, whole.T, precision=HIGHEST_PRECISION)
        slot_index = own_map // count // front * count + own_map % count
        routing = (slot_index[:, None] == jnp.arange(bulk * count)[None, :]).astype(F32)
        added = lax.psum_scatter(
            jnp.dot(routing.T, reached, precision=HIGHEST_PRECISION),
            "bulk",
            scatter_dimension=0,
            tiled=True,
        )
        square = lax.psum(jnp.dot(whole, whole.T, precision=HIGHEST_PRECISION), "bulk")
        square = square.reshape(sources, bulk, spreads, piece // spreads, pivots)
        square = jnp.transpose(square, (1, 2, 0, 3, 4)).reshape(bulk, front, piece // spreads, pivots)
        changed = [
            lines[m] - lax.dynamic_index_in_dim(square, bulk_me ^ m, 0, False) for m in range(bulk)
        ]
        return changed, arrow - added

    lines = bulk_gather(line, "bulk", bulk)
    lines, arrow = lax.cond(overflow, landing_whole, unchanged, lines, arrow, x_own)

    all_con = bulk_gather(after(con, all_squares[-1]), "bulk", bulk)
    plh, pll, pih, pil, plow = vmem_call(
        lambda *refs: parent_kernel(bulk, blocks, width, sources, refs),
        [
            shaped((pivots, pivots), BF16),
            shaped((pivots, pivots), BF16),
            shaped((pivots // width, width, width), BF16),
            shaped((pivots // width, width, width), BF16),
            shaped((pivots, pivots), F32),
        ],
        [True] + [False] * (1 + 2 * bulk),
        [pltpu.VMEM((pivots, pivots), F32)] * 2,
        pl.CostEstimate(flops=60_000_000_000, bytes_accessed=1 << 24, transcendentals=0),
    )(place, spread, *lines, *all_squares)

    (parent_rows,) = vmem_call(
        lambda *refs: rest_kernel(bulk, blocks, width, refs),
        [shaped((count, pivots), F32)],
        [True] + [False] * (7 + bulk),
        [
            pltpu.VMEM((count, pivots), F32),
            pltpu.VMEM((count, pivots), BF16),
            pltpu.VMEM((count, pivots), BF16),
        ],
    )(place, arrow, route, spread, *all_con, plh, pll, pih, pil)
    return (lower_rows[None], x_own[None], parent_rows)


def solution(mesh):
    placed = (
        P("bulk", "front", None),
        P("bulk", "front", None),
        P(("bulk", "front"), None),
        P("bulk", "front"),
        P(),
    )
    return jax.shard_map(
        on_device,
        mesh=mesh,
        in_specs=placed,
        out_specs=(P("bulk", "front", None), P("bulk", "front", None), P(("bulk", "front"), None)),
        check_vma=False,
    )
```

time: 550 us -> 487 us (0.89)
  the two profiles are of different devices: /device:TPU:20 before, /device:TPU:1 now
where the time goes in v3:
time: 487 us; the launch traced here: 479 us
  Pallas kernels  247 us (51%)
  waiting for transfers between devices  114 us (23%)
  starting transfers between devices  58.1 us (12%)
  other arithmetic  22.9 us (5%)
  local copies, waits for them, and re-layouts  18.7 us (4%)
  between operations  17.5 us (4%)
    pallas_call x6, Pallas kernels, on_device(): vmem_call(functools.partial(lambda *refs, args: child_stage(*args, refs),...  168 us
    pallas_call x1, Pallas kernels, on_device(): vmem_call(lambda *refs: parent_kernel(bulk, blocks, width, sources, refs)...  56.5 us
    ppermute x6, waiting for transfers between devices, ring_gather(): coming = lax.ppermute(coming, axis, back)  43.2 us
    ppermute x8, waiting for transfers between devices, ring_gather(): going = lax.ppermute(going, axis, ahead)  33.8 us
    ppermute x8, starting transfers between devices, ring_gather(): going = lax.ppermute(going, axis, ahead)  25.5 us
    ppermute x12, waiting for transfers between devices, bulk_gather(): lax.ppermute(held[mask], axis, [(i, i ^ step) for i in range(size)])  17.9 us
    pallas_call x1, Pallas kernels, on_device(): vmem_call(lambda *refs: own_kernel(solved, stages, width, refs), [shaped(...  13.5 us
    ppermute x12, starting transfers between devices, bulk_gather(): lax.ppermute(held[mask], axis, [(i, i ^ step) for i in range(size)])  13.1 us
  transfers between devices with their start and end apart: 40, of which 15 were waited for; matrix products, arithmetic and copies ran while one was open for 6% of the time, Pallas kernels for 50%

profile of v3, /device:TPU:1, one launch (start us, length us, event | category | flops | bytes accessed | tf_op | source)
XLA Modules:
  0.0 478.5 jit_solution(17088734017186787248)
XLA Ops:
  16.2 2.3 dynamic-slice_bitcast_fusion
  22.8 8.0 %collective-permute-done.refs_8_ = f32[264,384]{1,0:T(8,128)S(1)} collective-permute-done((f32[264,384]{1,0:T(8,128)}, f32[264,384]{1,0:T(8,128)S(1)}, u32[]{:S(2)}, u32[]{:S(2)}) %collective-permute-start) | collective-permute-done | bytes 405536 | tf_op jit(solution)/shard_map/ppermute | solution.py:295
  32.0 8.5 %collective-permute-done.1.refs_9_ = f32[264,384]{1,0:T(8,128)S(1)} collective-permute-done((f32[264,384]{1,0:T(8,128)S(1)}, f32[264,384]{1,0:T(8,128)S(1)}, u32[]{:S(2)}, u32[]{:S(2)}) %collective-permute-start.1) | collective-permute-done | bytes 405536 | tf_op jit(solution)/shard_map/ppermute | solution.py:295
  42.9 6.5 %collective-permute-done.2.refs_10_ = f32[264,384]{1,0:T(8,128)S(1)} collective-permute-done((f32[264,384]{1,0:T(8,128)S(1)}, f32[264,384]{1,0:T(8,128)S(1)}, u32[]{:S(2)}, u32[]{:S(2)}) %collective-permute-start.2) | collective-permute-done | bytes 405536 | tf_op jit(solution)/shard_map/ppermute | solution.py:295
  50.3 4.2 collective-permute-start.21
  57.6 13.1 %collective-permute-done.9.refs_5_ = f32[264,384]{1,0:T(8,128)} collective-permute-done((f32[264,384]{1,0:T(8,128)}, f32[264,384]{1,0:T(8,128)}, u32[]{:S(2)}, u32[]{:S(2)}) %collective-permute-start.9) | collective-permute-done | bytes 405536 | tf_op jit(solution)/shard_map/ppermute | solution.py:292
  70.7 16.0 %collective-permute-start.10 = (f32[264,384]{1,0:T(8,128)}, f32[264,384]{1,0:T(8,128)}, u32[]{:S(2)}, u32[]{:S(2)}) collective-permute-start(f32[264,384]{1,0:T(8,128)} %collective-permute-done.9.refs_5_), channel_id=1, source_target_pairs={{0,2},{2,4},{4,6},{6,7},{7,5},{5,3},{3,1},{1,0},{8,10},{10,12},{12... | collective-permute-start | bytes 1216520 | tf_op jit(solution)/shard_map/ppermute | solution.py:292
  89.5 5.8 %collective-permute-done.10.refs_6_ = f32[264,384]{1,0:T(8,128)} collective-permute-done((f32[264,384]{1,0:T(8,128)}, f32[264,384]{1,0:T(8,128)}, u32[]{:S(2)}, u32[]{:S(2)}) %collective-permute-start.10) | collective-permute-done | bytes 405536 | tf_op jit(solution)/shard_map/ppermute | solution.py:292
  99.5 2.3 collective-permute-start.16
  105.9 8.7 %collective-permute-done.11.refs_7_ = f32[264,384]{1,0:T(8,128)} collective-permute-done((f32[264,384]{1,0:T(8,128)}, f32[264,384]{1,0:T(8,128)}, u32[]{:S(2)}, u32[]{:S(2)}) %collective-permute-start.11) | collective-permute-done | bytes 405536 | tf_op jit(solution)/shard_map/ppermute | solution.py:292
  119.6 6.2 %collective-permute-done.16.refs_12_ = f32[256,256]{1,0:T(8,128)} collective-permute-done((f32[256,256]{1,0:T(8,128)S(1)}, f32[256,256]{1,0:T(8,128)}, u32[]{:S(2)}, u32[]{:S(2)}) %collective-permute-start.16) | collective-permute-done | bytes 262176 | tf_op jit(solution)/shard_map/ppermute | solution.py:292
  125.8 2.8 collective-permute-start.17
  128.7 2.3 collective-permute-start.22
  131.0 13.9 %shard_map.139 = (f32[512,512]{1,0:T(8,128)}, bf16[512,512]{1,0:T(8,128)(2,1)}, bf16[512,512]{1,0:T(8,128)(2,1)}, bf16[512,512]{1,0:T(8,128)(2,1)}, bf16[512,512]{1,0:T(8,128)(2,1)}) custom-call(s32[3]{0:T(128)} %pad_add_fusion.refs_0_, s32[8]{0:T(128)} %copy-done.10, s32[3,8]{1,0:T(4,128)} %constant.219.clone.refs_2_, ...), custom_call_target="tpu_custom_call" | custom-call | flops 12000000000 | bytes 1048576 | tf_op jit(solution)/shard_map/pallas_call | solution.py:769
  144.9 4.8 %reduce-window.19 = s32[4,4,2,128]{3,2,1,0:T(2,128)S(1)} reduce-window(s32[4,4,2,128]{3,2,1,0:T(2,128)S(1)} %reshape.220, s32[]{:T(128)} %constant.194.clone.1), window={size=1x1x1x128 pad=0_0x0_0x0_0x127_0}, to_apply=%region_3.4 | reduce-window | flops 520192 | bytes 32772 | tf_op jit(solution)/shard_map/reduce-window.2
  151.0 19.2 %collective-permute-done.5.refs_18_ = f32[256,256]{1,0:T(8,128)} collective-permute-done((f32[256,256]{1,0:T(8,128)S(1)}, f32[256,256]{1,0:T(8,128)}, u32[]{:S(2)}, u32[]{:S(2)}) %collective-permute-start.5) | collective-permute-done | bytes 262176 | tf_op jit(solution)/shard_map/ppermute | solution.py:295
  175.1 2.3 collective-permute-done.27
  179.9 10.3 %collective-permute-done.28 = f32[32,1024]{1,0:T(8,128)S(1)} collective-permute-done((f32[32,1024]{1,0:T(8,128)S(1)}, f32[32,1024]{1,0:T(8,128)S(1)}, u32[]{:S(2)}, u32[]{:S(2)}) %collective-permute-start.28) | collective-permute-done | bytes 131104 | tf_op jit(solution)/shard_map/ppermute | solution.py:668
  192.5 14.2 %shard_map.140 = (f32[512,512]{1,0:T(8,128)}, bf16[512,512]{1,0:T(8,128)(2,1)}, bf16[512,512]{1,0:T(8,128)(2,1)}, bf16[512,512]{1,0:T(8,128)(2,1)}, bf16[512,512]{1,0:T(8,128)(2,1)}, /*index=5*/f32[256,512]{1,0:T(8,128)}) custom-call(s32[3]{0:T(128)} %pad_add_fusion.refs_0_, ...), custom_call_target="tpu_custom_call", output_to_operand_aliasing={{0}: (1, {}), {1}: (2, {}), {2}: (3, {}), {3}: (4, {}), {4}... | custom-call | flops 12000000000 | bytes 1048576 | tf_op jit(solution)/shard_map/pallas_call | solution.py:769
  210.0 19.4 %shard_map.141 = (f32[512,512]{1,0:T(8,128)}, bf16[512,1024]{1,0:T(8,128)(2,1)}, bf16[512,1024]{1,0:T(8,128)(2,1)}, bf16[512,512]{1,0:T(8,128)(2,1)}, bf16[512,512]{1,0:T(8,128)(2,1)}) custom-call(s32[3]{0:T(128)} %pad_add_fusion.refs_0_, s32[8]{0:T(128)} %copy-done.10, s32[3,8]{1,0:T(4,128)} %constant.219.clone.refs_2_, ...), custom_call_target="tpu_custom_call" | custom-call | flops 12000000000 | bytes 1048576 | tf_op jit(solution)/shard_map/pallas_call | solution.py:769
  231.4 16.4 %shard_map.142 = (f32[512,512]{1,0:T(8,128)}, bf16[512,1024]{1,0:T(8,128)(2,1)}, bf16[512,1024]{1,0:T(8,128)(2,1)}, bf16[512,512]{1,0:T(8,128)(2,1)}, bf16[512,5...) custom-call(s32[3]{0:T(128)} %pad_add_fusion.refs_0_, ...), custom_call_target="tpu_custom_call", output_to_operand_aliasing={{0}: (1, {}), {1}: (2, {}), {2}: (3, {}), {3}: (4, {}), {4}... | custom-call | flops 12000000000 | bytes 1048576 | tf_op jit(solution)/shard_map/pallas_call | solution.py:769
  248.6 39.5 %shard_map.143 = (f32[512,512]{1,0:T(8,128)}, bf16[512,1536]{1,0:T(8,128)(2,1)}, bf16[512,1536]{1,0:T(8,128)(2,1)}, bf16[512,512]{1,0:T(8,128)(2,1)}, bf16[512,5...) custom-call(s32[3]{0:T(128)} %pad_add_fusion.refs_0_, ...), custom_call_target="tpu_custom_call" | custom-call | flops 24000000000 | bytes 1048576 | tf_op jit(solution)/shard_map/pallas_call | solution.py:769
  288.1 5.9 %all-gather.9.cloned.1.call-done = f32[256,1024]{1,0:T(8,128)} async-done(((f32[32,1024]{1,0:T(8,128)}), f32[256,1024]{1,0:T(8,128)}) %all-gather.9.cloned.1.call-update) | async-done | bytes 1048592 | tf_op jit(solution)/shard_map/all_gather | solution.py:688
  295.3 64.4 %shard_map.144 = (f32[512,512]{1,0:T(8,128)}, bf16[512,2048]{1,0:T(8,128)(2,1)}, bf16[512,2048]{1,0:T(8,128)(2,1)}, bf16[512,512]{1,0:T(8,128)(2,1)}, bf16[512,5...) custom-call(s32[3]{0:T(128)} %pad_add_fusion.refs_0_, ...), custom_call_target="tpu_custom_call" | custom-call | flops 24000000000 | bytes 1048576 | tf_op jit(solution)/shard_map/pallas_call | solution.py:769
  362.7 3.4 collective-permute-start.37
  366.1 8.3 %collective-permute-done.32.refs_8_ = f32[10,128,128]{2,1,0:T(8,128)} collective-permute-done((f32[10,128,128]{2,1,0:T(8,128)}, f32[10,128,128]{2,1,0:T(8,128)}, u32[]{:S(2)}, u32[]{:S(2)}) %collective-permute-start.32) | collective-permute-done | bytes 655392 | tf_op jit(solution)/shard_map/ppermute | solution.py:356
  374.4 2.9 collective-permute-start.33
  377.7 13.5 %shard_map.145 = (f32[256,2048]{1,0:T(8,128)S(1)}, f32[256,512]{1,0:T(8,128)}) custom-call(f32[256,1024]{1,0:T(8,128)} %slice.114.refs_0_, bf16[256,1024]{1,0:T(8,128)(2,1)} %get-tuple-element.144.refs_1_, bf16[256,1024]{1,0:T(8,128)(2,1)} %get-tuple-element.145.refs_2_, bf16[512,1536]{1,0:T(8,128)(2,1)} %get-tuple-element.135.refs_29_.refs_3_, ...), custom_call_target="tpu_custom_call" | custom-call | flops 10000000000 | bytes 1048576 | tf_op jit(solution)/shard_map/pallas_call | solution.py:809
  391.5 4.1 select_bitcast_fusion
  395.6 9.6 %collective-permute-done.35.refs_6_ = f32[256,512]{1,0:T(8,128)} collective-permute-done((f32[256,512]{1,0:T(8,128)}, f32[256,512]{1,0:T(8,128)}, u32[]{:S(2)}, u32[]{:S(2)}) %collective-permute-start.35) | collective-permute-done | bytes 524320 | tf_op jit(solution)/shard_map/ppermute | solution.py:356
  406.0 56.5 %shard_map.146 = (bf16[1024,1024]{1,0:T(8,128)(2,1)}, bf16[1024,1024]{1,0:T(8,128)(2,1)}, bf16[2,512,512]{2,1,0:T(8,128)(2,1)}, bf16[2,512,512]{2,1,0:T(8,128)(2,1)}, f32[1024,1024]{1,0:T(8,128)}) custom-call(s32[3]{0:T(128)} %pad_add_fusion.refs_0_, bf16[4,256,512]{2,1,0:T(8,128)(2,1)} %compare_convert_fusion.refs_1_.refs_3_, ...), custom_call_target="tpu_custom_call" | custom-call | flops 60000002048 | bytes 16777216 | tf_op jit(solution)/shard_map/pallas_call | solution.py:846
  462.6 8.8 %shard_map.147 = f32[256,1024]{1,0:T(8,128)} custom-call(s32[3]{0:T(128)} %pad_add_fusion.refs_0_, f32[256,1024]{1,0:T(8,128)S(1)} %get-tuple-element.155.refs_1_, bf16[4,256,256]{2,1,0:T(8,128)(2,1)} %compare_convert_fusion.1.refs_2_, bf16[4,256,512]{2,1,0:T(8,128)(2,1)} %compare_convert_fusion.refs_1_.refs_3_, f32[256,512]{1,0:T(8,128)} %get-tuple-element.158.refs_4_, ...), custom_call_target="tpu_custom_call" | custom-call | tf_op jit(solution)/shard_map/pallas_call | solution.py:860
  (180 shorter events, 56.9 us)
Async XLA Ops:
  7.2 240.7 %all-gather.7.cloned.1.call-start = ((), (), s32[]{:S(2)}) async-start(), calls=%async_computation.4 | async-start | bytes 4718592 | tf_op jit(solution)/shard_map/all_gather | solution.py:677
  21.3 33.9 %collective-permute-start.8 = (f32[264,384]{1,0:T(8,128)}, f32[264,384]{1,0:T(8,128)}, u32[]{:S(2)}, u32[]{:S(2)}) collective-permute-start(f32[264,384]{1,0:T(8,128)} %select_maximum_fusion.refs_3_), channel_id=1, source_target_pairs={{0,2},{2,4},{4,6},{6,7},{7,5},{5,3},{3,1},{1,0},{8,10},{10,12},{12... | collective-permute-start | bytes 1216520 | tf_op jit(solution)/shard_map/ppermute | solution.py:292
  50.3 36.5 %collective-permute-start.21 = (f32[64,2048]{1,0:T(8,128)}, f32[64,2048]{1,0:T(8,128)}, u32[]{:S(2)}, u32[]{:S(2)}) collective-permute-start(f32[64,2048]{1,0:T(8,128)} %slice.87), channel_id=1, source_target_pairs={{0,4},{1,5},{2,6},{3,7},{8,12},{9,13},{10,14},{11,15},{16,20},{17,... | collective-permute-start | bytes 1572872 | tf_op jit(solution)/shard_map/ppermute | solution.py:668
  55.2 15.5 %collective-permute-start.9 = (f32[264,384]{1,0:T(8,128)}, f32[264,384]{1,0:T(8,128)}, u32[]{:S(2)}, u32[]{:S(2)}) collective-permute-start(f32[264,384]{1,0:T(8,128)} %collective-permute-done.8.refs_4_), channel_id=1, source_target_pairs={{0,2},{2,4},{4,6},{6,7},{7,5},{5,3},{3,1},{1,0},{8,10},{10,12},{12... | collective-permute-start | bytes 1216520 | tf_op jit(solution)/shard_map/ppermute | solution.py:292
  70.7 24.6 %collective-permute-start.10 = (f32[264,384]{1,0:T(8,128)}, f32[264,384]{1,0:T(8,128)}, u32[]{:S(2)}, u32[]{:S(2)}) collective-permute-start(f32[264,384]{1,0:T(8,128)} %collective-permute-done.9.refs_5_), channel_id=1, source_target_pairs={{0,2},{2,4},{4,6},{6,7},{7,5},{5,3},{3,1},{1,0},{8,10},{10,12},{12... | collective-permute-start | bytes 1216520 | tf_op jit(solution)/shard_map/ppermute | solution.py:292
  87.7 206.3 %all-gather.9.cloned.1.call-start = ((), (), s32[]{:S(2)}) async-start(), calls=%async_computation.5 | async-start | bytes 1179648 | tf_op jit(solution)/shard_map/all_gather | solution.py:688
  95.4 19.3 %collective-permute-start.11 = (f32[264,384]{1,0:T(8,128)}, f32[264,384]{1,0:T(8,128)}, u32[]{:S(2)}, u32[]{:S(2)}) collective-permute-start(f32[264,384]{1,0:T(8,128)} %collective-permute-done.10.refs_6_), channel_id=1, source_target_pairs={{0,2},{2,4},{4,6},{6,7},{7,5},{5,3},{3,1},{1,0},{8,10},{10,12},{12... | collective-permute-start | bytes 1216520 | tf_op jit(solution)/shard_map/ppermute | solution.py:292
  99.4 20.2 %collective-permute-start.3 = (f32[256,256]{1,0:T(8,128)S(1)}, f32[256,256]{1,0:T(8,128)}, u32[]{:S(2)}, u32[]{:S(2)}) collective-permute-start(f32[256,256]{1,0:T(8,128)S(1)} %copy-done.7), channel_id=1, source_target_pairs={{2,0},{4,2},{6,4},{7,6},{5,7},{3,5},{1,3},{0,1},{10,8},{12,10},{14... | collective-permute-start | bytes 786440 | tf_op jit(solution)/shard_map/ppermute | solution.py:295
  99.5 26.3 %collective-permute-start.16 = (f32[256,256]{1,0:T(8,128)S(1)}, f32[256,256]{1,0:T(8,128)}, u32[]{:S(2)}, u32[]{:S(2)}) collective-permute-start(f32[256,256]{1,0:T(8,128)S(1)} %copy-done.7), channel_id=1, source_target_pairs={{0,2},{2,4},{4,6},{6,7},{7,5},{5,3},{3,1},{1,0},{8,10},{10,12},{12... | collective-permute-start | bytes 786440 | tf_op jit(solution)/shard_map/ppermute | solution.py:292
  115.5 15.4 %collective-permute-start.23 = (f32[8,256]{1,0:T(8,128)S(1)}, f32[8,256]{1,0:T(8,128)S(1)}, u32[]{:S(2)}, u32[]{:S(2)}) collective-permute-start(f32[8,256]{1,0:T(8,128)S(1)} %select_reduce_fusion.1), channel_id=1, source_target_pairs={{0,16},{8,24},{16,0},{24,8},{1,17},{9,25},{17,1},{25,9},{2,18},{10... | collective-permute-start | bytes 24584 | tf_op jit(solution)/shard_map/ppermute | solution.py:356
  119.6 30.5 %collective-permute-start.4 = (f32[256,256]{1,0:T(8,128)}, f32[256,256]{1,0:T(8,128)S(1)}, u32[]{:S(2)}, u32[]{:S(2)}) collective-permute-start(f32[256,256]{1,0:T(8,128)} %collective-permute-done.3.refs_16_), channel_id=1, source_target_pairs={{2,0},{4,2},{6,4},{7,6},{5,7},{3,5},{1,3},{0,1},{10,8},{12,10},{14... | collective-permute-start | bytes 786440 | tf_op jit(solution)/shard_map/ppermute | solution.py:295
  125.8 47.7 %collective-permute-start.17 = (f32[256,256]{1,0:T(8,128)}, f32[256,256]{1,0:T(8,128)}, u32[]{:S(2)}, u32[]{:S(2)}) collective-permute-start(f32[256,256]{1,0:T(8,128)} %collective-permute-done.16.refs_12_), channel_id=1, source_target_pairs={{0,2},{2,4},{4,6},{6,7},{7,5},{5,3},{3,1},{1,0},{8,10},{10,12},{12... | collective-permute-start | bytes 786440 | tf_op jit(solution)/shard_map/ppermute | solution.py:292
  128.7 16.2 %collective-permute-start.22 = (f32[8,256]{1,0:T(8,128)S(1)}, f32[8,256]{1,0:T(8,128)S(1)}, u32[]{:S(2)}, u32[]{:S(2)}) collective-permute-start(f32[8,256]{1,0:T(8,128)S(1)} %select_reduce_fusion.1), channel_id=1, source_target_pairs={{0,8},{8,0},{16,24},{24,16},{1,9},{9,1},{17,25},{25,17},{2,10},{10... | collective-permute-start | bytes 24584 | tf_op jit(solution)/shard_map/ppermute | solution.py:356
  131.0 13.9 %collective-permute-start.24 = (f32[8,256]{1,0:T(8,128)S(1)}, f32[8,256]{1,0:T(8,128)S(1)}, u32[]{:S(2)}, u32[]{:S(2)}) collective-permute-start(f32[8,256]{1,0:T(8,128)S(1)} %collective-permute-done.23), channel_id=1, source_target_pairs={{0,8},{8,0},{16,24},{24,16},{1,9},{9,1},{17,25},{25,17},{2,10},{10... | collective-permute-start | bytes 24584 | tf_op jit(solution)/shard_map/ppermute | solution.py:356
  150.1 20.1 %collective-permute-start.5 = (f32[256,256]{1,0:T(8,128)S(1)}, f32[256,256]{1,0:T(8,128)}, u32[]{:S(2)}, u32[]{:S(2)}) collective-permute-start(f32[256,256]{1,0:T(8,128)S(1)} %collective-permute-done.4.refs_17_), channel_id=1, source_target_pairs={{2,0},{4,2},{6,4},{7,6},{5,7},{3,5},{1,3},{0,1},{10,8},{12,10},{14... | collective-permute-start | bytes 786440 | tf_op jit(solution)/shard_map/ppermute | solution.py:295
  173.6 17.2 %collective-permute-start.6 = (f32[256,512]{1,0:T(8,128)S(1)}, f32[256,512]{1,0:T(8,128)}, u32[]{:S(2)}, u32[]{:S(2)}) collective-permute-start(f32[256,512]{1,0:T(8,128)S(1)} %copy-done.5), channel_id=1, source_target_pairs={{0,2},{2,4},{4,6},{6,7},{7,5},{5,3},{3,1},{1,0},{8,10},{10,12},{12... | collective-permute-start | bytes 1572872 | tf_op jit(solution)/shard_map/ppermute | solution.py:314
  173.7 17.1 %collective-permute-start.7 = (f32[256,512]{1,0:T(8,128)S(1)}, f32[256,512]{1,0:T(8,128)}, u32[]{:S(2)}, u32[]{:S(2)}) collective-permute-start(f32[256,512]{1,0:T(8,128)S(1)} %copy-done.5), channel_id=1, source_target_pairs={{2,0},{4,2},{6,4},{7,6},{5,7},{3,5},{1,3},{0,1},{10,8},{12,10},{14... | collective-permute-start | bytes 1572872 | tf_op jit(solution)/shard_map/ppermute | solution.py:317
  179.2 30.0 %collective-permute-start.19 = (f32[256,256]{1,0:T(8,128)}, f32[256,256]{1,0:T(8,128)S(1)}, u32[]{:S(2)}, u32[]{:S(2)}) collective-permute-start(f32[256,256]{1,0:T(8,128)} %collective-permute-done.18.refs_14_), channel_id=1, source_target_pairs={{0,2},{2,4},{4,6},{6,7},{7,5},{5,3},{3,1},{1,0},{8,10},{10,12},{12... | collective-permute-start | bytes 786440 | tf_op jit(solution)/shard_map/ppermute | solution.py:292
  190.8 16.3 %collective-permute-start.12 = (f32[256,512]{1,0:T(8,128)}, f32[256,512]{1,0:T(8,128)S(1)}, u32[]{:S(2)}, u32[]{:S(2)}) collective-permute-start(f32[256,512]{1,0:T(8,128)} %collective-permute-done.6.refs_20_), channel_id=1, source_target_pairs={{0,2},{2,4},{4,6},{6,7},{7,5},{5,3},{3,1},{1,0},{8,10},{10,12},{12... | collective-permute-start | bytes 1572872 | tf_op jit(solution)/shard_map/ppermute | solution.py:314
  190.8 16.3 %collective-permute-start.13 = (f32[256,512]{1,0:T(8,128)}, f32[256,512]{1,0:T(8,128)S(1)}, u32[]{:S(2)}, u32[]{:S(2)}) collective-permute-start(f32[256,512]{1,0:T(8,128)} %collective-permute-done.7.refs_24_), channel_id=1, source_target_pairs={{2,0},{4,2},{6,4},{7,6},{5,7},{3,5},{1,3},{0,1},{10,8},{12,10},{14... | collective-permute-start | bytes 1572872 | tf_op jit(solution)/shard_map/ppermute | solution.py:317
  207.1 22.3 %collective-permute-start.14 = (f32[256,512]{1,0:T(8,128)S(1)}, f32[256,512]{1,0:T(8,128)S(1)}, u32[]{:S(2)}, u32[]{:S(2)}) collective-permute-start(f32[256,512]{1,0:T(8,128)S(1)} %collective-permute-done.12.refs_21_), channel_id=1, source_target_pairs={{0,2},{2,4},{4,6},{6,7},{7,5},{5,3},{3,1},{1,0},{8,10},{10,12},{12... | collective-permute-start | bytes 1572872 | tf_op jit(solution)/shard_map/ppermute | solution.py:314
  209.3 20.2 %collective-permute-start.15 = (f32[256,512]{1,0:T(8,128)S(1)}, f32[256,512]{1,0:T(8,128)S(1)}, u32[]{:S(2)}, u32[]{:S(2)}) collective-permute-start(f32[256,512]{1,0:T(8,128)S(1)} %collective-permute-done.13.refs_25_), channel_id=1, source_target_pairs={{2,0},{4,2},{6,4},{7,6},{5,7},{3,5},{1,3},{0,1},{10,8},{12,10},{14... | collective-permute-start | bytes 1572872 | tf_op jit(solution)/shard_map/ppermute | solution.py:317
  229.5 18.3 %collective-permute-start.20 = (f32[256,512]{1,0:T(8,128)S(1)}, f32[256,512]{1,0:T(8,128)S(1)}, u32[]{:S(2)}, u32[]{:S(2)}) collective-permute-start(f32[256,512]{1,0:T(8,128)S(1)} %collective-permute-done.14.refs_22_), channel_id=1, source_target_pairs={{0,2},{2,4},{4,6},{6,7},{7,5},{5,3},{3,1},{1,0},{8,10},{10,12},{12... | collective-permute-start | bytes 1572872 | tf_op jit(solution)/shard_map/ppermute | solution.py:314
  294.0 83.2 %collective-permute-start.30 = (f32[8,32,1024]{2,1,0:T(8,128)}, f32[8,32,1024]{2,1,0:T(8,128)}, u32[]{:S(2)}, u32[]{:S(2)}) collective-permute-start(f32[8,32,1024]{2,1,0:T(8,128)} %bitcast.34), channel_id=1, source_target_pairs={{0,16},{8,24},{16,0},{24,8},{1,17},{9,25},{17,1},{25,9},{2,18},{10... | collective-permute-start | bytes 3145736 | tf_op jit(solution)/shard_map/ppermute | solution.py:356
  359.7 14.7 %collective-permute-start.32 = (f32[10,128,128]{2,1,0:T(8,128)}, f32[10,128,128]{2,1,0:T(8,128)}, u32[]{:S(2)}, u32[]{:S(2)}) collective-permute-start(f32[10,128,128]{2,1,0:T(8,128)} %get-tuple-element.157.refs_6_), channel_id=1, source_target_pairs={{0,16},{8,24},{16,0},{24,8},{1,17},{9,25},{17,1},{25,9},{2,18},{10... | collective-permute-start | bytes 1966088 | tf_op jit(solution)/shard_map/ppermute | solution.py:356
  362.7 43.4 %collective-permute-start.37 = (f32[10,128,128]{2,1,0:T(8,128)}, f32[10,128,128]{2,1,0:T(8,128)}, u32[]{:S(2)}, u32[]{:S(2)}) collective-permute-start(f32[10,128,128]{2,1,0:T(8,128)} %get-tuple-element.157.refs_6_), channel_id=1, source_target_pairs={{0,8},{8,0},{16,24},{24,16},{1,9},{9,1},{17,25},{25,17},{2,10},{10... | collective-permute-start | bytes 1966088 | tf_op jit(solution)/shard_map/ppermute | solution.py:356
  374.4 16.9 %collective-permute-start.33 = (f32[10,128,128]{2,1,0:T(8,128)}, f32[10,128,128]{2,1,0:T(8,128)}, u32[]{:S(2)}, u32[]{:S(2)}) collective-permute-start(f32[10,128,128]{2,1,0:T(8,128)} %collective-permute-done.32.refs_8_), channel_id=1, source_target_pairs={{0,8},{8,0},{16,24},{24,16},{1,9},{9,1},{17,25},{25,17},{2,10},{10... | collective-permute-start | bytes 1966088 | tf_op jit(solution)/shard_map/ppermute | solution.py:356
  377.2 28.8 %collective-permute-start.29 = (f32[8,32,1024]{2,1,0:T(8,128)}, f32[8,32,1024]{2,1,0:T(8,128)}, u32[]{:S(2)}, u32[]{:S(2)}) collective-permute-start(f32[8,32,1024]{2,1,0:T(8,128)} %bitcast.34), channel_id=1, source_target_pairs={{0,8},{8,0},{16,24},{24,16},{1,9},{9,1},{17,25},{25,17},{2,10},{10... | collective-permute-start | bytes 3145736 | tf_op jit(solution)/shard_map/ppermute | solution.py:356
  377.2 28.7 %collective-permute-start.31 = (f32[8,32,1024]{2,1,0:T(8,128)}, f32[8,32,1024]{2,1,0:T(8,128)}, u32[]{:S(2)}, u32[]{:S(2)}) collective-permute-start(f32[8,32,1024]{2,1,0:T(8,128)} %collective-permute-done.30), channel_id=1, source_target_pairs={{0,8},{8,0},{16,24},{24,16},{1,9},{9,1},{17,25},{25,17},{2,10},{10... | collective-permute-start | bytes 3145736 | tf_op jit(solution)/shard_map/ppermute | solution.py:356
  391.3 13.9 %collective-permute-start.35 = (f32[256,512]{1,0:T(8,128)}, f32[256,512]{1,0:T(8,128)}, u32[]{:S(2)}, u32[]{:S(2)}) collective-permute-start(f32[256,512]{1,0:T(8,128)} %get-tuple-element.158.refs_4_), channel_id=1, source_target_pairs={{0,16},{8,24},{16,0},{24,8},{1,17},{9,25},{17,1},{25,9},{2,18},{10... | collective-permute-start | bytes 1572872 | tf_op jit(solution)/shard_map/ppermute | solution.py:356
  395.6 67.0 %collective-permute-start.34 = (f32[256,512]{1,0:T(8,128)}, f32[256,512]{1,0:T(8,128)}, u32[]{:S(2)}, u32[]{:S(2)}) collective-permute-start(f32[256,512]{1,0:T(8,128)} %get-tuple-element.158.refs_4_), channel_id=1, source_target_pairs={{0,8},{8,0},{16,24},{24,16},{1,9},{9,1},{17,25},{25,17},{2,10},{10... | collective-permute-start | bytes 1572872 | tf_op jit(solution)/shard_map/ppermute | solution.py:356
  405.2 57.4 %collective-permute-start.36 = (f32[256,512]{1,0:T(8,128)}, f32[256,512]{1,0:T(8,128)}, u32[]{:S(2)}, u32[]{:S(2)}) collective-permute-start(f32[256,512]{1,0:T(8,128)} %collective-permute-done.35.refs_6_), channel_id=1, source_target_pairs={{0,8},{8,0},{16,24},{24,16},{1,9},{9,1},{17,25},{25,17},{2,10},{10... | collective-permute-start | bytes 1572872 | tf_op jit(solution)/shard_map/ppermute | solution.py:356
  (32 other events, 462.3 us)
Sparse Core Ops, SparseCore 0:
  87.8 87.3 all-gather.6
  248.0 45.9 all-gather.8

commit v4 on v3

--- a/solution.py
+++ b/solution.py
@@ -122,27 +122,26 @@
     return out
 
 
-def subtract_products(dst, rows, cols, ah, al, bh, bl, depth):
+def subtract_products(dst, rows, cols, ah, al, bh, bl, depth, lower=False):
     if depth == 0:
         return
-
-    def body(r, nr, c, nc):
-        a = (ah[ds(r, nr), :depth], al[ds(r, nr), :depth])
-        b = (bh[ds(c, nc), :depth], bl[ds(c, nc), :depth])
-        dst[ds(r, nr), ds(c, nc)] = dst[ds(r, nr), ds(c, nc)] - dot3(a, b, NT)
-
-    tiles(rows, cols, body)
+    tile = min(256, cols)
+    for c in range(0, cols, tile):
+        top = c if lower else 0
+        a = (ah[top:rows, :depth], al[top:rows, :depth])
+        b = (bh[c : c + tile, :depth], bl[c : c + tile, :depth])
+        dst[top:rows, c : c + tile] = dst[top:rows, c : c + tile] - dot3(a, b, NT)
 
 
 def times_inverse(src, outh, outl, out_at, rows, width, invh, invl):
-    def body(r, nr, c, nc):
-        a = split(src[ds(r, nr), :])
-        b = (invh[ds(c, nc), :], invl[ds(c, nc), :])
-        high, low = split(dot3(a, b, NT))
-        outh[ds(r, nr), pl.ds(pl.multiple_of(out_at + c, nc), nc)] = high
-        outl[ds(r, nr), pl.ds(pl.multiple_of(out_at + c, nc), nc)] = low
-
-    tiles(rows, width, body)
+    tile = min(256, width)
+    a = split(src[:rows, :])
+    for c in range(0, width, tile):
+        part = tuple(x[:, : c + tile] for x in a)
+        b = (invh[c : c + tile, : c + tile], invl[c : c + tile, : c + tile])
+        high, low = split(dot3(part, b, NT))
+        outh[:rows, out_at + c : out_at + c + tile] = high
+        outl[:rows, out_at + c : out_at + c + tile] = low
 
 
 def clear_inverse(invh, invl):
@@ -167,6 +166,16 @@
     none = jnp.zeros((width, LANES), BF16)
     last = width // LANES - 1
 
+    def column(r, some):
+        here = ds(r * LANES, LANES)
+        inv = (invh[here, here], invl[here, here])
+        solved = dot3(split(s_ref[:, here]), inv, NT)
+        solved = jnp.where(jnp.logical_and(row_id >= col_id + r * LANES, some), solved, 0.0)
+        high, low = split(solved)
+        lh[:, ds(at + r * LANES, LANES)] = high
+        ll[:, ds(at + r * LANES, LANES)] = low
+        return high, low
+
     def panel(p, carry):
         first = p * LANES
         here = ds(first, LANES)
@@ -175,14 +184,15 @@
             for i in range(LANES // SUB)
         ]
         before = jnp.maximum(p - 1, 0)
-        done = ds(at + before * LANES, LANES)
-        later = jnp.logical_and(row_id >= first + LANES, p > 0)
-        old = tuple(jnp.where(later, ref[:, done], none) for ref in (lh, ll))
+        high, low = column(before, p > 0)
+        high = jnp.where(row_id >= first, high, none)
+        low = jnp.where(row_id >= first, low, none)
+        below = tuple(jnp.where(row_id >= first + LANES, x, none) for x in (high, low))
         for c in range(1, last + 1):
+            rows = slice(c * LANES, None)
             cols = slice(c * LANES, (c + 1) * LANES)
-            some = (old[0][cols], old[1][cols])
-            s_ref[c * LANES :, cols] = s_ref[c * LANES :, cols] - dot3(
-                (old[0][c * LANES :], old[1][c * LANES :]), some, NT
+            s_ref[rows, cols] = s_ref[rows, cols] - dot3(
+                (below[0][rows], below[1][rows]), (high[cols], low[cols]), NT
             )
         inverse_row(before, at, width, lh, ll, invh, invl)
         if job is not None:
@@ -191,20 +201,14 @@
         inv = split(jnp.concatenate(factor_block(block), axis=0))
         invh[here, here] = inv[0]
         invl[here, here] = inv[1]
-        solved = dot3(split(s_ref[:, here]), inv, NT)
-        high, low = split(jnp.where(row_id >= col_id + first, solved, 0.0))
-        lh[:, ds(at + first, LANES)] = high
-        ll[:, ds(at + first, LANES)] = low
-        below = row_id >= first + LANES
         following = ds(jnp.minimum(p + 1, last) * LANES, LANES)
-        some = (lh[following, ds(at + first, LANES)], ll[following, ds(at + first, LANES)])
-        s_ref[:, following] = s_ref[:, following] - dot3(
-            (jnp.where(below, high, none), jnp.where(below, low, none)), some, NT
-        )
+        beside = split(jnp.where(p < last, dot3(split(s_ref[following, here]), inv, NT), 0.0))
+        s_ref[following, following] = s_ref[following, following] - dot3(beside, beside, NT)
         return carry
 
     lax.fori_loop(start, stop, panel, 0)
     if stop == last + 1:
+        column(last, True)
         inverse_row(last, at, width, lh, ll, invh, invl)
 
 
@@ -221,7 +225,8 @@
 
 
 def vmem_call(body, out_shapes, in_kinds, scratch, cost=None, aliases=None):
-    specs = [pl.BlockSpec(memory_space=pltpu.SMEM if k else pltpu.VMEM) for k in in_kinds]
+    spaces = {True: pltpu.SMEM, False: pltpu.VMEM, None: pl.ANY}
+    specs = [pl.BlockSpec(memory_space=spaces[k]) for k in in_kinds]
     return pl.pallas_call(
         body,
         out_shape=out_shapes,
@@ -348,13 +353,18 @@
     return [x] + moved
 
 
-def bulk_gather(x, axis, size):
+def bulk_gather(x, axis, size, low_first=False, beside=None):
     held = {0: x}
-    step = size // 2
-    while step:
-        for mask in list(held):
-            held[mask | step] = lax.ppermute(held[mask], axis, [(i, i ^ step) for i in range(size)])
-        step //= 2
+    steps = [1 << bit for bit in range(size.bit_length() - 1)]
+    for step in steps if low_first else reversed(steps):
+        new = {
+            mask | step: lax.ppermute(held[mask], axis, [(i, i ^ step) for i in range(size)])
+            for mask in held
+        }
+        if beside is not None:
+            new = {mask: after(value, beside()) for mask, value in new.items()}
+            beside = None
+        held.update(new)
     return [held[m] for m in range(size)]
 
 
@@ -430,8 +440,20 @@
     if start == 0:
         a_ref = take(1)[0]
     if landing:
-        t_ref = take(1)[0]
-
+        t_ref, copy_sems = take(2)
+
+    copies = []
+    if landing:
+        total, front, sources, cap = shapes
+        share = cap * sources // front
+        for f in range(front):
+            at = (f % sources) * cap + (f // sources) * share
+            copies.append(
+                pltpu.make_async_copy(
+                    raw_ref.at[f, :share, :], t_ref.at[at : at + share, :], copy_sems.at[f]
+                )
+            )
+            copies[-1].start()
     if start == 0:
         assemble_rows(q, width, own, groups, owner_ref, table_ref, chunks, late_rounds, a_ref)
         for j in range(q):
@@ -439,7 +461,7 @@
             subtract_products(part, width, width, lh, ll, prev_lh[j], prev_ll[j], j * width)
             times_inverse(part, lh, ll, j * width, width, width, prev_ih[j], prev_il[j])
         s_out[...] = a_ref[:, q * width : (q + 1) * width]
-        subtract_products(s_out, width, width, lh, ll, lh, ll, q * width)
+        subtract_products(s_out, width, width, lh, ll, lh, ll, q * width, True)
         clear_inverse(invh, invl)
     else:
         for new, held in zip((s_out, lh, ll, invh, invl), state, strict=True):
@@ -447,12 +469,8 @@
     if couples and q > 1:
         xh[:, : (q - 1) * width] = old_x[0][...]
         xl[:, : (q - 1) * width] = old_x[1][...]
-    if landing:
-        total, front, sources, cap = shapes
-        share = cap * sources // front
-        for f in range(front):
-            at = (f % sources) * cap + (f // sources) * share
-            t_ref[at : at + share, :] = raw_ref[f * share : (f + 1) * share, :]
+    for copy in copies:
+        copy.wait()
 
     def job(p):
         if couples:
@@ -532,7 +550,7 @@
     refs = list(refs)
     place_ref, spread_ref = refs[:2]
     tops, squares = refs[2 : 2 + children], refs[2 + children : 2 + 2 * children]
-    lh, ll, invh, invl, lower, s_ref, top_ref = refs[2 + 2 * children :]
+    lh, ll, invh, invl, s_ref, top_ref = refs[2 + 2 * children :]
     pivots = lh.shape[0]
     dense = pivots // blocks
     groups, part_rows, _ = tops[0].shape
@@ -570,10 +588,9 @@
             subtract_products(part, width, width, lhq, llq, lh.at[cut, :], ll.at[cut, :], j * width)
             times_inverse(part, lhq, llq, j * width, width, width, invh.at[j], invl.at[j])
         part = s_ref.at[rows, q * width : (q + 1) * width]
-        subtract_products(part, width, width, lhq, llq, lhq, llq, q * width)
+        subtract_products(part, width, width, lhq, llq, lhq, llq, q * width, True)
         clear_inverse(invh.at[q], invl.at[q])
         factor_panels(0, width // LANES, part, q * width, width, lhq, llq, invh.at[q], invl.at[q])
-    lower[...] = lh[...].astype(F32) + ll[...].astype(F32)
 
 
 def rest_kernel(children, blocks, width, refs):
@@ -644,15 +661,17 @@
     head = jnp.concatenate([own_block, jnp.where(me % 2 == 0, even, odd)], axis=1)
     tail = jnp.pad(own_map.astype(F32)[None], ((0, SUB - 1), (0, half)))
     chunks = [jnp.concatenate([head, tail], axis=0)]
+    mine_later, table_me = after((mine, jnp.asarray(table)[:, me]), chunks[0])
     for rnd in range(rounds):
-        col = jnp.maximum(jnp.asarray(table[rnd])[me], 0)
-        chunks.append(lax.dynamic_slice_in_dim(mine, col * own, own, 1))
+        col = jnp.maximum(table_me[rnd], 0)
+        chunks.append(lax.dynamic_slice_in_dim(mine_later, col * own, own, 1))
     owners = slot_owners("front", front)
     gathered = [ring_gather(chunks[0], "front", front)]
     started = gathered[0][-1]
     for rnd in range(1, early + 1):
         gathered.append(ring_gather(after(chunks[rnd], gathered[-1][-1]), "front", front))
-    late = Ring(after(jnp.concatenate(chunks[early + 1 :], axis=1), gathered[-1][-1]), "front", front)
+    here = gathered[-1][1:]
+    late = Ring(after(jnp.concatenate(chunks[early + 1 :], axis=1), here), "front", front)
     table_in = jnp.asarray(table)
     place = jnp.stack([(me % per_stage) * own, first_row, bulk_me]).astype(jnp.int32)
 
@@ -674,24 +693,33 @@
         return part
 
     compact = jnp.dot(pick, coupling, precision=HIGHEST_PRECISION)
-    raw_landing = lax.all_gather(spread_out(after(compact, started)), "front", axis=0, tiled=True)
+    landing_part = spread_out(after(compact, started))
+    place = after(place, here)
 
     block_rows = (first_row + jnp.arange(count)) // BLOCK
     row_mask = jnp.take(block_pattern, block_rows, axis=0).astype(F32)
     arrow = parent_arrow * jnp.repeat(row_mask, BLOCK, axis=1)
     piece = count // bulk
-    part = after(arrow, gathered[early][-1])
+    part = after(arrow, chunks[0])
     pieces = part[:piece]
     for g in range(1, bulk):
         moved = lax.ppermute(part[g * piece : (g + 1) * piece], "bulk", [(0, g)])
         pieces = jnp.where(bulk_me == g, moved, pieces)
-    line = lax.all_gather(after(spread_out(pieces), raw_landing), "front", axis=0, tiled=False)
+    line_part = spread_out(pieces)
+    share = landing_part.shape[0]
+    extra = line_part.reshape(-1, total)
+    padding = jnp.zeros((-extra.shape[0] % SUB, total), F32)
+    both = jnp.concatenate([landing_part, extra, padding], axis=0)
+    place = after(place, both)
+    both = lax.all_gather(both, "front", axis=0, tiled=False)
+    line = both[:, share : share + extra.shape[0]].reshape((front,) + line_part.shape)
 
     my_maps = jnp.stack([slot[own, :own] for slot in gathered[0]])
     ordered = jnp.sum(
         jnp.where(owners[None, :, None] == jnp.arange(front)[:, None, None], my_maps[None], 0.0), axis=1
     )
     maps = jnp.stack(bulk_gather(ordered, "bulk", bulk)).astype(jnp.int32)
+    place = after(place, maps)
     lands = maps[:, :sources] < pivots
     rank = jnp.cumsum(lands.astype(jnp.int32), axis=2) - 1
     overflow = jnp.any(rank[:, :, -1] >= cap)
@@ -745,7 +773,7 @@
                 if q > 1:
                     operands += xs
             if landing:
-                operands.append(raw_landing)
+                operands.append(both)
             outs = [
                 shaped((width, width), F32),
                 shaped((width, deep), BF16),
@@ -765,6 +793,7 @@
                 scratch.append(pltpu.VMEM((width, deep), F32))
             if landing:
                 scratch.append(pltpu.VMEM((total_landing, total), F32))
+                scratch.append(pltpu.SemaphoreType.DMA((front,)))
             out = list(
                 vmem_call(
                     functools.partial(
@@ -775,7 +804,9 @@
                         ),
                     ),
                     outs,
-                    [True] * smem + [False] * (len(operands) - smem),
+                    [True] * smem
+                    + [False] * (len(operands) - smem - landing)
+                    + [None] * landing,
                     scratch,
                     pl.CostEstimate(
                         flops=6_000_000_000 * (stop - start), bytes_accessed=1 << 20, transcendentals=0
@@ -802,7 +833,6 @@
         padded = jnp.pad(owned[q], ((0, 0), (0, total - (q + 1) * width)))
         lower_rows = jnp.where(me // per_stage == q, padded, lower_rows)
 
-    all_squares = bulk_gather(squares, "bulk", bulk)
     solved = max(stages - 2, 0)
     operands = [coupling[:, solved * width :]] + (xs if solved > 0 else [])
     operands += lh[solved:] + ll[solved:] + ih[solved:] + il[solved:] + [th, tl]
@@ -813,6 +843,7 @@
         [pltpu.VMEM((own, total), BF16)] * 2,
         pl.CostEstimate(flops=10_000_000_000, bytes_accessed=1 << 20, transcendentals=0),
     )(*operands)
+    all_squares = bulk_gather(squares, "bulk", bulk, beside=lambda: con)
 
     def unchanged(lines, arrow, x_own):
         return lines, arrow
@@ -842,15 +873,14 @@
     lines = bulk_gather(line, "bulk", bulk)
     lines, arrow = lax.cond(overflow, landing_whole, unchanged, lines, arrow, x_own)
 
-    all_con = bulk_gather(after(con, all_squares[-1]), "bulk", bulk)
-    plh, pll, pih, pil, plow = vmem_call(
+    all_con = bulk_gather(con, "bulk", bulk, low_first=True)
+    plh, pll, pih, pil = vmem_call(
         lambda *refs: parent_kernel(bulk, blocks, width, sources, refs),
         [
             shaped((pivots, pivots), BF16),
             shaped((pivots, pivots), BF16),
             shaped((pivots // width, width, width), BF16),
             shaped((pivots // width, width, width), BF16),
-            shaped((pivots, pivots), F32),
         ],
         [True] + [False] * (1 + 2 * bulk),
         [pltpu.VMEM((pivots, pivots), F32)] * 2,

time: 487 us -> 447 us (0.918)
  the two profiles are of different devices: /device:TPU:1 before, /device:TPU:20 now
where the time goes in v4:
time: 447 us; the launch traced here: 438 us
  Pallas kernels  225 us (50%)
  waiting for transfers between devices  113 us (25%)
  starting transfers between devices  33.6 us (8%)
  local copies, waits for them, and re-layouts  23.9 us (5%)
  other arithmetic  23.4 us (5%)
  between operations  17.7 us (4%)
    pallas_call x6, Pallas kernels, on_device(): vmem_call(functools.partial(lambda *refs, args: child_stage(*args, refs),...  152 us
    ppermute x8, waiting for transfers between devices, ring_gather(): going = lax.ppermute(going, axis, ahead)  61.5 us
    pallas_call x1, Pallas kernels, on_device(): vmem_call(lambda *refs: parent_kernel(bulk, blocks, width, sources, refs)...  52.6 us
    ppermute x4, waiting for transfers between devices, advance(): self.going = lax.ppermute(self.going, self.axis, self.ahead)  21.9 us
    pallas_call x1, Pallas kernels, on_device(): vmem_call(lambda *refs: own_kernel(solved, stages, width, refs), [shaped(...  11.9 us
    ppermute x2, waiting for transfers between devices, spread_out(): lax.ppermute(x[k * rows:(k + 1) * rows], 'front', [(s, s + k * sources) f...  11.6 us
    ppermute x6, waiting for transfers between devices, ring_gather(): coming = lax.ppermute(coming, axis, back)  9.2 us
  transfers between devices with their start and end apart: 39, of which 12 were waited for; matrix products, arithmetic and copies ran while one was open for 10% of the time, Pallas kernels for 50%

profile of v4, /device:TPU:20, one launch (start us, length us, event | category | flops | bytes accessed | tf_op | source)
XLA Modules:
  0.0 437.7 jit_solution(15480892102661400313)
XLA Ops:
  21.0 1.8 fusion.11
  25.0 8.7 %collective-permute-done.1.refs_9_ = f32[264,384]{1,0:T(8,128)} collective-permute-done((f32[264,384]{1,0:T(8,128)}, f32[264,384]{1,0:T(8,128)}, u32[]{:S(2)}, u32[]{:S(2)}) %collective-permute-start.1) | collective-permute-done | bytes 405536 | tf_op jit(solution)/shard_map/ppermute | solution.py:300
  34.2 1.9 compare_select_fusion.2
  41.2 2.0 constant_dynamic-slice_fusion.2
  43.7 1.9 slice.98
  54.6 11.6 %collective-permute-done.14 = f32[32,1024]{1,0:T(8,128)S(1)} collective-permute-done((f32[32,1024]{1,0:T(8,128)}, f32[32,1024]{1,0:T(8,128)S(1)}, u32[]{:S(2)}, u32[]{:S(2)}) %collective-permute-start.14) | collective-permute-done | bytes 131104 | tf_op jit(solution)/shard_map/ppermute | solution.py:687
  67.2 18.2 %collective-permute-done.17.refs_6_ = f32[264,384]{1,0:T(8,128)} collective-permute-done((f32[264,384]{1,0:T(8,128)}, f32[264,384]{1,0:T(8,128)}, u32[]{:S(2)}, u32[]{:S(2)}) %collective-permute-start.17) | collective-permute-done | bytes 405536 | tf_op jit(solution)/shard_map/ppermute | solution.py:297
  90.4 2.0 collective-permute-start.7
  93.8 4.6 %collective-permute-done.18.refs_7_ = f32[264,384]{1,0:T(8,128)} collective-permute-done((f32[264,384]{1,0:T(8,128)}, f32[264,384]{1,0:T(8,128)}, u32[]{:S(2)}, u32[]{:S(2)}) %collective-permute-start.18) | collective-permute-done | bytes 405536 | tf_op jit(solution)/shard_map/ppermute | solution.py:297
  99.5 3.5 collective-permute-done.20
  104.7 10.1 %collective-permute-done.3.refs_12_ = f32[256,256]{1,0:T(8,128)} collective-permute-done((f32[256,256]{1,0:T(8,128)S(1)}, f32[256,256]{1,0:T(8,128)}, u32[]{:S(2)}, u32[]{:S(2)}) %collective-permute-start.3) | collective-permute-done | bytes 262176 | tf_op jit(solution)/shard_map/ppermute | solution.py:297
  114.8 2.0 collective-permute-start.8
  116.9 4.8 %reduce-window.19 = s32[4,4,2,128]{3,2,1,0:T(2,128)S(1)} reduce-window(s32[4,4,2,128]{3,2,1,0:T(2,128)S(1)} %reshape.225, s32[]{:T(128)} %constant.185.clone.1), window={size=1x1x1x128 pad=0_0x0_0x0_0x127_0}, to_apply=%region_3.4 | reduce-window | flops 520192 | bytes 32772 | tf_op jit(solution)/shard_map/reduce-window.2
  122.6 6.7 %collective-permute-done.4.refs_13_ = f32[256,256]{1,0:T(8,128)S(1)} collective-permute-done((f32[256,256]{1,0:T(8,128)}, f32[256,256]{1,0:T(8,128)S(1)}, u32[]{:S(2)}, u32[]{:S(2)}) %collective-permute-start.4) | collective-permute-done | bytes 262176 | tf_op jit(solution)/shard_map/ppermute | solution.py:297
  132.7 3.6 collective-permute-done.5.refs_14_
  138.0 18.2 %collective-permute-done.6.refs_15_ = f32[256,256]{1,0:T(8,128)} collective-permute-done((f32[256,256]{1,0:T(8,128)S(1)}, f32[256,256]{1,0:T(8,128)}, u32[]{:S(2)}, u32[]{:S(2)}) %collective-permute-start.6) | collective-permute-done | bytes 262176 | tf_op jit(solution)/shard_map/ppermute | solution.py:297
  156.2 2.0 collective-permute-start.23
  158.2 13.5 %shard_map.112 = (f32[512,512]{1,0:T(8,128)}, bf16[512,512]{1,0:T(8,128)(2,1)}, bf16[512,512]{1,0:T(8,128)(2,1)}, bf16[512,512]{1,0:T(8,128)(2,1)}, bf16[512,512]{1,0:T(8,128)(2,1)}) custom-call(s32[3]{0:T(128)} %pad_add_fusion.refs_0_, s32[8]{0:T(128)} %copy-done.12, s32[3,8]{1,0:T(4,128)} %constant.204.clone.refs_2_, f32[264,384]{1,0:T(8,128)} %copy-done.5, ...), custom_call_target="tpu_custom_call" | custom-call | flops 12000000000 | bytes 1048576 | tf_op jit(solution)/shard_map/pallas_call | solution.py:798
  171.8 21.9 %collective-permute-done.22.refs_20_ = f32[256,512]{1,0:T(8,128)S(1)} collective-permute-done((f32[256,512]{1,0:T(8,128)}, f32[256,512]{1,0:T(8,128)S(1)}, u32[]{:S(2)}, u32[]{:S(2)}) %collective-permute-start.22) | collective-permute-done | bytes 524320 | tf_op jit(solution)/shard_map/ppermute | solution.py:319
  193.7 2.2 collective-permute-start.25
  195.9 14.2 %shard_map.113 = (f32[512,512]{1,0:T(8,128)}, bf16[512,512]{1,0:T(8,128)(2,1)}, bf16[512,512]{1,0:T(8,128)(2,1)}, bf16[512,512]{1,0:T(8,128)(2,1)}, bf16[512,512]{1,0:T(8,128)(2,1)}, /*index=5*/f32[256,512]{1,0:T(8,128)}) custom-call(s32[3]{0:T(128)} %pad_add_fusion.refs_0_, ...), custom_call_target="tpu_custom_call", output_to_operand_aliasing={{0}: (1, {}), {1}: (2, {}), {2}: (3, {}), {3}: (4, {}), {4}... | custom-call | flops 12000000000 | bytes 1048576 | tf_op jit(solution)/shard_map/pallas_call | solution.py:798
  210.3 1.9 collective-permute-start.27
  212.2 17.3 %shard_map.114 = (f32[512,512]{1,0:T(8,128)}, bf16[512,1024]{1,0:T(8,128)(2,1)}, bf16[512,1024]{1,0:T(8,128)(2,1)}, bf16[512,512]{1,0:T(8,128)(2,1)}, bf16[512,512]{1,0:T(8,128)(2,1)}) custom-call(s32[3]{0:T(128)} %pad_add_fusion.refs_0_, s32[8]{0:T(128)} %copy-done.12, s32[3,8]{1,0:T(4,128)} %constant.204.clone.refs_2_, f32[264,384]{1,0:T(8,128)} %copy-done.5, ...), custom_call_target="tpu_custom_call" | custom-call | flops 12000000000 | bytes 1048576 | tf_op jit(solution)/shard_map/pallas_call | solution.py:798
  230.1 15.8 %shard_map.115 = (f32[512,512]{1,0:T(8,128)}, bf16[512,1024]{1,0:T(8,128)(2,1)}, bf16[512,1024]{1,0:T(8,128)(2,1)}, bf16[512,512]{1,0:T(8,128)(2,1)}, bf16[512,5...) custom-call(s32[3]{0:T(128)} %pad_add_fusion.refs_0_, ...), custom_call_target="tpu_custom_call", output_to_operand_aliasing={{0}: (1, {}), {1}: (2, {}), {2}: (3, {}), {3}: (4, {}), {4}... | custom-call | flops 12000000000 | bytes 1048576 | tf_op jit(solution)/shard_map/pallas_call | solution.py:798
  246.7 34.5 %shard_map.116 = (f32[512,512]{1,0:T(8,128)}, bf16[512,1536]{1,0:T(8,128)(2,1)}, bf16[512,1536]{1,0:T(8,128)(2,1)}, bf16[512,512]{1,0:T(8,128)(2,1)}, bf16[512,5...) custom-call(s32[3]{0:T(128)} %pad_add_fusion.refs_0_, ...), custom_call_target="tpu_custom_call" | custom-call | flops 24000000000 | bytes 1048576 | tf_op jit(solution)/shard_map/pallas_call | solution.py:798
  283.7 3.8 collective-permute-start.30
  287.4 57.0 %shard_map.117 = (f32[512,512]{1,0:T(8,128)}, bf16[512,2048]{1,0:T(8,128)(2,1)}, bf16[512,2048]{1,0:T(8,128)(2,1)}, bf16[512,512]{1,0:T(8,128)(2,1)}, bf16[512,5...) custom-call(s32[3]{0:T(128)} %pad_add_fusion.refs_0_, ...), custom_call_target="tpu_custom_call" | custom-call | flops 24000000000 | bytes 1048576 | tf_op jit(solution)/shard_map/pallas_call | solution.py:798
  345.2 11.9 %shard_map.118 = (f32[256,2048]{1,0:T(8,128)S(1)}, f32[256,512]{1,0:T(8,128)}) custom-call(f32[256,1024]{1,0:T(8,128)} %slice.139.refs_0_, bf16[256,1024]{1,0:T(8,128)(2,1)} %get-tuple-element.154.refs_1_, bf16[256,1024]{1,0:T(8,128)(2,1)} %get-tuple-element.155.refs_2_, bf16[512,1536]{1,0:T(8,128)(2,1)} %get-tuple-element.146.refs_29_.refs_3_, ...), custom_call_target="tpu_custom_call" | custom-call | flops 10000000000 | bytes 1048576 | tf_op jit(solution)/shard_map/pallas_call | solution.py:839
  357.2 4.8 %collective-permute-done.36.refs_8_ = f32[10,128,128]{2,1,0:T(8,128)} collective-permute-done((f32[10,128,128]{2,1,0:T(8,128)}, f32[10,128,128]{2,1,0:T(8,128)}, u32[]{:S(2)}, u32[]{:S(2)}) %collective-permute-start.36) | collective-permute-done | bytes 655392 | tf_op jit(solution)/shard_map/ppermute | solution.py:361
  364.2 3.7 select_bitcast_fusion
  370.0 52.6 %shard_map.119 = (bf16[1024,1024]{1,0:T(8,128)(2,1)}, bf16[1024,1024]{1,0:T(8,128)(2,1)}, bf16[2,512,512]{2,1,0:T(8,128)(2,1)}, bf16[2,512,512]{2,1,0:T(8,128)(2,1)}) custom-call(s32[3]{0:T(128)} %pad_add_fusion.refs_0_, bf16[4,256,512]{2,1,0:T(8,128)(2,1)} %compare_convert_fusion.refs_1_.refs_3_, f32[8,32,1024]{2,1,0:T(8,128)} %get-tuple-element.165.refs_2_, ...), custom_call_target="tpu_custom_call" | custom-call | flops 60000002048 | bytes 16777216 | tf_op jit(solution)/shard_map/pallas_call | solution.py:877
  422.6 7.8 %shard_map.120 = f32[256,1024]{1,0:T(8,128)} custom-call(s32[3]{0:T(128)} %pad_add_fusion.refs_0_, f32[256,1024]{1,0:T(8,128)S(1)} %get-tuple-element.163.refs_1_, bf16[4,256,256]{2,1,0:T(8,128)(2,1)} %compare_convert_fusion.1.refs_2_, bf16[4,256,512]{2,1,0:T(8,128)(2,1)} %compare_convert_fusion.refs_1_.refs_3_, f32[256,512]{1,0:T(8,128)} %get-tuple-element.164.refs_4_, ...), custom_call_target="tpu_custom_call" | custom-call | tf_op jit(solution)/shard_map/pallas_call | solution.py:890
  (185 shorter events, 53.3 us)
Async XLA Ops:
  7.2 274.0 %all-gather.6.cloned.1.call-start = ((), (), s32[]{:S(2)}) async-start(), calls=%async_computation.4 | async-start | bytes 5898240 | tf_op jit(solution)/shard_map/all_gather | solution.py:714
  10.2 26.7 %collective-permute-start.15 = (f32[264,384]{1,0:T(8,128)S(1)}, f32[264,384]{1,0:T(8,128)}, u32[]{:S(2)}, u32[]{:S(2)}) collective-permute-start(f32[264,384]{1,0:T(8,128)S(1)} %select_maximum_fusion.refs_3_), channel_id=1, source_target_pairs={{0,2},{2,4},{4,6},{6,7},{7,5},{5,3},{3,1},{1,0},{8,10},{10,12},{12... | collective-permute-start | bytes 1216520 | tf_op jit(solution)/shard_map/ppermute | solution.py:297
  11.9 11.0 %collective-permute-start = (f32[264,384]{1,0:T(8,128)S(1)}, f32[264,384]{1,0:T(8,128)}, u32[]{:S(2)}, u32[]{:S(2)}) collective-permute-start(f32[264,384]{1,0:T(8,128)S(1)} %select_maximum_fusion.refs_3_), channel_id=1, source_target_pairs={{2,0},{4,2},{6,4},{7,6},{5,7},{3,5},{1,3},{0,1},{10,8},{12,10},{14... | collective-permute-start | bytes 1216520 | tf_op jit(solution)/shard_map/ppermute | solution.py:300
  17.0 29.9 %collective-permute-start.11 = (f32[64,1024]{1,0:T(8,128)}, f32[64,1024]{1,0:T(8,128)}, u32[]{:S(2)}, u32[]{:S(2)}) collective-permute-start(f32[64,1024]{1,0:T(8,128)} %get-tuple-element.190), channel_id=1, source_target_pairs={{0,24},{1,25},{2,26},{3,27},{4,28},{5,29},{6,30},{7,31}} | collective-permute-start | bytes 786440 | tf_op jit(solution)/shard_map/ppermute | solution.py:706
  18.3 28.5 %collective-permute-start.12 = (f32[64,1024]{1,0:T(8,128)}, f32[64,1024]{1,0:T(8,128)}, u32[]{:S(2)}, u32[]{:S(2)}) collective-permute-start(f32[64,1024]{1,0:T(8,128)} %get-tuple-element.189), channel_id=1, source_target_pairs={{0,16},{1,17},{2,18},{3,19},{4,20},{5,21},{6,22},{7,23}} | collective-permute-start | bytes 786440 | tf_op jit(solution)/shard_map/ppermute | solution.py:706
  19.6 27.2 %collective-permute-start.13 = (f32[64,1024]{1,0:T(8,128)}, f32[64,1024]{1,0:T(8,128)}, u32[]{:S(2)}, u32[]{:S(2)}) collective-permute-start(f32[64,1024]{1,0:T(8,128)} %get-tuple-element.188), channel_id=1, source_target_pairs={{0,8},{1,9},{2,10},{3,11},{4,12},{5,13},{6,14},{7,15}} | collective-permute-start | bytes 786440 | tf_op jit(solution)/shard_map/ppermute | solution.py:706
  36.9 13.6 %collective-permute-start.16 = (f32[264,384]{1,0:T(8,128)}, f32[264,384]{1,0:T(8,128)}, u32[]{:S(2)}, u32[]{:S(2)}) collective-permute-start(f32[264,384]{1,0:T(8,128)} %collective-permute-done.15.refs_4_), channel_id=1, source_target_pairs={{0,2},{2,4},{4,6},{6,7},{7,5},{5,3},{3,1},{1,0},{8,10},{10,12},{12... | collective-permute-start | bytes 1216520 | tf_op jit(solution)/shard_map/ppermute | solution.py:297
  45.5 39.9 %collective-permute-start.10 = (f32[64,2048]{1,0:T(8,128)}, f32[64,2048]{1,0:T(8,128)}, u32[]{:S(2)}, u32[]{:S(2)}) collective-permute-start(f32[64,2048]{1,0:T(8,128)} %slice.98), channel_id=1, source_target_pairs={{0,4},{1,5},{2,6},{3,7},{8,12},{9,13},{10,14},{11,15},{16,20},{17,... | collective-permute-start | bytes 1572872 | tf_op jit(solution)/shard_map/ppermute | solution.py:687
  49.2 17.0 %collective-permute-start.14 = (f32[32,1024]{1,0:T(8,128)}, f32[32,1024]{1,0:T(8,128)S(1)}, u32[]{:S(2)}, u32[]{:S(2)}) collective-permute-start(f32[32,1024]{1,0:T(8,128)} %slice.128), channel_id=1, source_target_pairs={{0,4},{1,5},{2,6},{3,7},{8,12},{9,13},{10,14},{11,15},{16,20},{17,... | collective-permute-start | bytes 393224 | tf_op jit(solution)/shard_map/ppermute | solution.py:687
  50.5 34.9 %collective-permute-start.17 = (f32[264,384]{1,0:T(8,128)}, f32[264,384]{1,0:T(8,128)}, u32[]{:S(2)}, u32[]{:S(2)}) collective-permute-start(f32[264,384]{1,0:T(8,128)} %collective-permute-done.16.refs_5_), channel_id=1, source_target_pairs={{0,2},{2,4},{4,6},{6,7},{7,5},{5,3},{3,1},{1,0},{8,10},{10,12},{12... | collective-permute-start | bytes 1216520 | tf_op jit(solution)/shard_map/ppermute | solution.py:297
  85.4 13.0 %collective-permute-start.18 = (f32[264,384]{1,0:T(8,128)}, f32[264,384]{1,0:T(8,128)}, u32[]{:S(2)}, u32[]{:S(2)}) collective-permute-start(f32[264,384]{1,0:T(8,128)} %collective-permute-done.17.refs_6_), channel_id=1, source_target_pairs={{0,2},{2,4},{4,6},{6,7},{7,5},{5,3},{3,1},{1,0},{8,10},{10,12},{12... | collective-permute-start | bytes 1216520 | tf_op jit(solution)/shard_map/ppermute | solution.py:297
  90.4 24.4 %collective-permute-start.3 = (f32[256,256]{1,0:T(8,128)S(1)}, f32[256,256]{1,0:T(8,128)}, u32[]{:S(2)}, u32[]{:S(2)}) collective-permute-start(f32[256,256]{1,0:T(8,128)S(1)} %copy-done.6), channel_id=1, source_target_pairs={{0,2},{2,4},{4,6},{6,7},{7,5},{5,3},{3,1},{1,0},{8,10},{10,12},{12... | collective-permute-start | bytes 786440 | tf_op jit(solution)/shard_map/ppermute | solution.py:297
  90.4 24.4 %collective-permute-start.7 = (f32[256,256]{1,0:T(8,128)S(1)}, f32[256,256]{1,0:T(8,128)}, u32[]{:S(2)}, u32[]{:S(2)}) collective-permute-start(f32[256,256]{1,0:T(8,128)S(1)} %copy-done.6), channel_id=1, source_target_pairs={{2,0},{4,2},{6,4},{7,6},{5,7},{3,5},{1,3},{0,1},{10,8},{12,10},{14... | collective-permute-start | bytes 786440 | tf_op jit(solution)/shard_map/ppermute | solution.py:300
  99.4 17.4 %collective-permute-start.19 = (f32[8,256]{1,0:T(8,128)S(1)}, f32[8,256]{1,0:T(8,128)S(1)}, u32[]{:S(2)}, u32[]{:S(2)}) collective-permute-start(f32[8,256]{1,0:T(8,128)S(1)} %select_reduce_fusion.1), channel_id=1, source_target_pairs={{0,8},{8,0},{16,24},{24,16},{1,9},{9,1},{17,25},{25,17},{2,10},{10... | collective-permute-start | bytes 24584 | tf_op jit(solution)/shard_map/ppermute | solution.py:361
  103.0 13.8 %collective-permute-start.21 = (f32[8,256]{1,0:T(8,128)S(1)}, f32[8,256]{1,0:T(8,128)S(1)}, u32[]{:S(2)}, u32[]{:S(2)}) collective-permute-start(f32[8,256]{1,0:T(8,128)S(1)} %collective-permute-done.20), channel_id=1, source_target_pairs={{0,8},{8,0},{16,24},{24,16},{1,9},{9,1},{17,25},{25,17},{2,10},{10... | collective-permute-start | bytes 24584 | tf_op jit(solution)/shard_map/ppermute | solution.py:361
  114.8 14.5 %collective-permute-start.4 = (f32[256,256]{1,0:T(8,128)}, f32[256,256]{1,0:T(8,128)S(1)}, u32[]{:S(2)}, u32[]{:S(2)}) collective-permute-start(f32[256,256]{1,0:T(8,128)} %collective-permute-done.3.refs_12_), channel_id=1, source_target_pairs={{0,2},{2,4},{4,6},{6,7},{7,5},{5,3},{3,1},{1,0},{8,10},{10,12},{12... | collective-permute-start | bytes 786440 | tf_op jit(solution)/shard_map/ppermute | solution.py:297
  114.8 16.1 %collective-permute-start.8 = (f32[256,256]{1,0:T(8,128)}, f32[256,256]{1,0:T(8,128)S(1)}, u32[]{:S(2)}, u32[]{:S(2)}) collective-permute-start(f32[256,256]{1,0:T(8,128)} %collective-permute-done.7.refs_16_), channel_id=1, source_target_pairs={{2,0},{4,2},{6,4},{7,6},{5,7},{3,5},{1,3},{0,1},{10,8},{12,10},{14... | collective-permute-start | bytes 786440 | tf_op jit(solution)/shard_map/ppermute | solution.py:300
  136.3 19.9 %collective-permute-start.6 = (f32[256,256]{1,0:T(8,128)S(1)}, f32[256,256]{1,0:T(8,128)}, u32[]{:S(2)}, u32[]{:S(2)}) collective-permute-start(f32[256,256]{1,0:T(8,128)S(1)} %collective-permute-done.5.refs_14_), channel_id=1, source_target_pairs={{0,2},{2,4},{4,6},{6,7},{7,5},{5,3},{3,1},{1,0},{8,10},{10,12},{12... | collective-permute-start | bytes 786440 | tf_op jit(solution)/shard_map/ppermute | solution.py:297
  156.2 37.4 %collective-permute-start.22 = (f32[256,512]{1,0:T(8,128)}, f32[256,512]{1,0:T(8,128)S(1)}, u32[]{:S(2)}, u32[]{:S(2)}) collective-permute-start(f32[256,512]{1,0:T(8,128)} %pad_maximum_fusion.1.refs_19_), channel_id=1, source_target_pairs={{0,2},{2,4},{4,6},{6,7},{7,5},{5,3},{3,1},{1,0},{8,10},{10,12},{12... | collective-permute-start | bytes 1572872 | tf_op jit(solution)/shard_map/ppermute | solution.py:319
  156.2 37.4 %collective-permute-start.23 = (f32[256,512]{1,0:T(8,128)}, f32[256,512]{1,0:T(8,128)S(1)}, u32[]{:S(2)}, u32[]{:S(2)}) collective-permute-start(f32[256,512]{1,0:T(8,128)} %pad_maximum_fusion.1.refs_19_), channel_id=1, source_target_pairs={{2,0},{4,2},{6,4},{7,6},{5,7},{3,5},{1,3},{0,1},{10,8},{12,10},{14... | collective-permute-start | bytes 1572872 | tf_op jit(solution)/shard_map/ppermute | solution.py:322
  193.7 16.5 %collective-permute-start.24 = (f32[256,512]{1,0:T(8,128)S(1)}, f32[256,512]{1,0:T(8,128)S(1)}, u32[]{:S(2)}, u32[]{:S(2)}) collective-permute-start(f32[256,512]{1,0:T(8,128)S(1)} %collective-permute-done.22.refs_20_), channel_id=1, source_target_pairs={{0,2},{2,4},{4,6},{6,7},{7,5},{5,3},{3,1},{1,0},{8,10},{10,12},{12... | collective-permute-start | bytes 1572872 | tf_op jit(solution)/shard_map/ppermute | solution.py:319
  193.7 16.4 %collective-permute-start.25 = (f32[256,512]{1,0:T(8,128)S(1)}, f32[256,512]{1,0:T(8,128)S(1)}, u32[]{:S(2)}, u32[]{:S(2)}) collective-permute-start(f32[256,512]{1,0:T(8,128)S(1)} %collective-permute-done.23.refs_24_), channel_id=1, source_target_pairs={{2,0},{4,2},{6,4},{7,6},{5,7},{3,5},{1,3},{0,1},{10,8},{12,10},{14... | collective-permute-start | bytes 1572872 | tf_op jit(solution)/shard_map/ppermute | solution.py:322
  210.2 19.4 %collective-permute-start.26 = (f32[256,512]{1,0:T(8,128)S(1)}, f32[256,512]{1,0:T(8,128)S(1)}, u32[]{:S(2)}, u32[]{:S(2)}) collective-permute-start(f32[256,512]{1,0:T(8,128)S(1)} %collective-permute-done.24.refs_21_), channel_id=1, source_target_pairs={{0,2},{2,4},{4,6},{6,7},{7,5},{5,3},{3,1},{1,0},{8,10},{10,12},{12... | collective-permute-start | bytes 1572872 | tf_op jit(solution)/shard_map/ppermute | solution.py:319
  210.3 19.2 %collective-permute-start.27 = (f32[256,512]{1,0:T(8,128)S(1)}, f32[256,512]{1,0:T(8,128)S(1)}, u32[]{:S(2)}, u32[]{:S(2)}) collective-permute-start(f32[256,512]{1,0:T(8,128)S(1)} %collective-permute-done.25.refs_25_), channel_id=1, source_target_pairs={{2,0},{4,2},{6,4},{7,6},{5,7},{3,5},{1,3},{0,1},{10,8},{12,10},{14... | collective-permute-start | bytes 1572872 | tf_op jit(solution)/shard_map/ppermute | solution.py:322
  229.6 16.3 %collective-permute-start.28 = (f32[256,512]{1,0:T(8,128)S(1)}, f32[256,512]{1,0:T(8,128)S(1)}, u32[]{:S(2)}, u32[]{:S(2)}) collective-permute-start(f32[256,512]{1,0:T(8,128)S(1)} %collective-permute-done.26.refs_22_), channel_id=1, source_target_pairs={{0,2},{2,4},{4,6},{6,7},{7,5},{5,3},{3,1},{1,0},{8,10},{10,12},{12... | collective-permute-start | bytes 1572872 | tf_op jit(solution)/shard_map/ppermute | solution.py:319
  283.7 61.5 %collective-permute-start.30 = (f32[8,32,1024]{2,1,0:T(8,128)}, f32[8,32,1024]{2,1,0:T(8,128)}, u32[]{:S(2)}, u32[]{:S(2)}) collective-permute-start(f32[8,32,1024]{2,1,0:T(8,128)} %reshape.223), channel_id=1, source_target_pairs={{0,16},{8,24},{16,0},{24,8},{1,17},{9,25},{17,1},{25,9},{2,18},{10... | collective-permute-start | bytes 3145736 | tf_op jit(solution)/shard_map/ppermute | solution.py:361
  287.4 80.8 %collective-permute-start.29 = (f32[8,32,1024]{2,1,0:T(8,128)}, f32[8,32,1024]{2,1,0:T(8,128)}, u32[]{:S(2)}, u32[]{:S(2)}) collective-permute-start(f32[8,32,1024]{2,1,0:T(8,128)} %reshape.223), channel_id=1, source_target_pairs={{0,8},{8,0},{16,24},{24,16},{1,9},{9,1},{17,25},{25,17},{2,10},{10... | collective-permute-start | bytes 3145736 | tf_op jit(solution)/shard_map/ppermute | solution.py:361
  344.5 17.5 %collective-permute-start.36 = (f32[10,128,128]{2,1,0:T(8,128)}, f32[10,128,128]{2,1,0:T(8,128)}, u32[]{:S(2)}, u32[]{:S(2)}) collective-permute-start(f32[10,128,128]{2,1,0:T(8,128)} %get-tuple-element.169.refs_6_), channel_id=1, source_target_pairs={{0,16},{8,24},{16,0},{24,8},{1,17},{9,25},{17,1},{25,9},{2,18},{10... | collective-permute-start | bytes 1966088 | tf_op jit(solution)/shard_map/ppermute | solution.py:361
  344.6 25.4 %collective-permute-start.35 = (f32[10,128,128]{2,1,0:T(8,128)}, f32[10,128,128]{2,1,0:T(8,128)}, u32[]{:S(2)}, u32[]{:S(2)}) collective-permute-start(f32[10,128,128]{2,1,0:T(8,128)} %get-tuple-element.169.refs_6_), channel_id=1, source_target_pairs={{0,8},{8,0},{16,24},{24,16},{1,9},{9,1},{17,25},{25,17},{2,10},{10... | collective-permute-start | bytes 1966088 | tf_op jit(solution)/shard_map/ppermute | solution.py:361
  345.1 24.8 %collective-permute-start.31 = (f32[8,32,1024]{2,1,0:T(8,128)}, f32[8,32,1024]{2,1,0:T(8,128)}, u32[]{:S(2)}, u32[]{:S(2)}) collective-permute-start(f32[8,32,1024]{2,1,0:T(8,128)} %collective-permute-done.30), channel_id=1, source_target_pairs={{0,8},{8,0},{16,24},{24,16},{1,9},{9,1},{17,25},{25,17},{2,10},{10... | collective-permute-start | bytes 3145736 | tf_op jit(solution)/shard_map/ppermute | solution.py:361
  367.9 54.7 %collective-permute-start.33 = (f32[256,512]{1,0:T(8,128)}, f32[256,512]{1,0:T(8,128)}, u32[]{:S(2)}, u32[]{:S(2)}) collective-permute-start(f32[256,512]{1,0:T(8,128)} %get-tuple-element.164.refs_4_), channel_id=1, source_target_pairs={{0,16},{8,24},{16,0},{24,8},{1,17},{9,25},{17,1},{25,9},{2,18},{10... | collective-permute-start | bytes 1572872 | tf_op jit(solution)/shard_map/ppermute | solution.py:361
  368.2 54.4 %collective-permute-start.34 = (f32[256,512]{1,0:T(8,128)}, f32[256,512]{1,0:T(8,128)}, u32[]{:S(2)}, u32[]{:S(2)}) collective-permute-start(f32[256,512]{1,0:T(8,128)} %collective-permute-done.32.refs_5_), channel_id=1, source_target_pairs={{0,16},{8,24},{16,0},{24,8},{1,17},{9,25},{17,1},{25,9},{2,18},{10... | collective-permute-start | bytes 1572872 | tf_op jit(solution)/shard_map/ppermute | solution.py:361
  (33 other events, 477.4 us)
Sparse Core Ops, SparseCore 0:
  87.7 109.8 all-gather.5

commit v5 on v4

--- a/solution.py
+++ b/solution.py
@@ -285,21 +285,11 @@
 
 
 def ring_gather(chunk, axis, groups):
-    order = ring_order(groups)
-    ahead = [(order[i], order[(i + 1) % groups]) for i in range(groups)]
-    back = [(b, a) for a, b in ahead]
-    out = [chunk]
-    going, coming = chunk, chunk
-    steps_ahead = groups // 2
-    steps_back = groups - 1 - steps_ahead
-    aheads, backs = [], []
-    for step in range(steps_ahead):
-        going = lax.ppermute(going, axis, ahead)
-        aheads.append(going)
-        if step < steps_back:
-            coming = lax.ppermute(coming, axis, back)
-            backs.append(coming)
-    return out + aheads + backs
+    ring = Ring(chunk, axis, groups)
+    for _ in range(ring.steps):
+        ring.advance(None)
+        ring.going, ring.coming = lax.optimization_barrier((ring.going, ring.coming))
+    return ring.slots()
 
 
 class Ring:
@@ -368,6 +358,13 @@
     return [held[m] for m in range(size)]
 
 
+def ranks(chosen):
+    size = chosen.shape[-1]
+    upto = jnp.arange(size)[:, None] <= jnp.arange(size)[None, :]
+    counts = jnp.matmul(chosen.astype(BF16), upto.astype(BF16), preferred_element_type=F32)
+    return counts.astype(jnp.int32) - 1
+
+
 def after(x, dep):
     return lax.optimization_barrier((x, dep))[0]
 
@@ -409,7 +406,7 @@
                 a_ref[ds(row, own), ds(col, own)] = chunk[k][:, cut : cut + own].T
 
 
-def child_stage(q, width, own, groups, late_rounds, counts, span, shapes, couples, landing, refs):
+def child_stage(q, width, own, groups, late_rounds, counts, span, couples, refs):
     start, stop = span
     panels = width // LANES
     refs = list(refs)
@@ -428,32 +425,14 @@
     if couples:
         b_ref = take(1)[0]
         old_x = take(2) if q > 1 else None
-    if landing:
-        raw_ref = take(1)[0]
     s_out, lh, ll, invh, invl = take(5)
     if couples:
         xh, xl = take(2)
     if stop == panels:
         own_ref = take(1)[0]
-    if landing:
-        th, tl, sq_ref = take(3)
     if start == 0:
         a_ref = take(1)[0]
-    if landing:
-        t_ref, copy_sems = take(2)
-
-    copies = []
-    if landing:
-        total, front, sources, cap = shapes
-        share = cap * sources // front
-        for f in range(front):
-            at = (f % sources) * cap + (f // sources) * share
-            copies.append(
-                pltpu.make_async_copy(
-                    raw_ref.at[f, :share, :], t_ref.at[at : at + share, :], copy_sems.at[f]
-                )
-            )
-            copies[-1].start()
+
     if start == 0:
         assemble_rows(q, width, own, groups, owner_ref, table_ref, chunks, late_rounds, a_ref)
         for j in range(q):
@@ -469,9 +448,6 @@
     if couples and q > 1:
         xh[:, : (q - 1) * width] = old_x[0][...]
         xl[:, : (q - 1) * width] = old_x[1][...]
-    for copy in copies:
-        copy.wait()
-
     def job(p):
         if couples:
             some = own // (stop - start)
@@ -480,34 +456,52 @@
                 rows, b_ref[rows, :], q - 1, width, xh, xl,
                 (prev_lh[q - 1], prev_ll[q - 1]), (prev_ih[q - 1], prev_il[q - 1]),
             )
-        if landing:
-            some = total // (stop - start)
-            rows = ds((p - start) * some, some)
-            for j in range(q):
-                solve_some(
-                    rows, t_ref[rows, j * width : (j + 1) * width], j, width, th, tl,
-                    (prev_lh[j], prev_ll[j]), (prev_ih[j], prev_il[j]),
-                )
 
     factor_panels(start, stop, s_out, q * width, width, lh, ll, invh, invl, job)
     if stop == panels:
         at = place_ref[0]
         own_ref[...] = lh[ds(at, own), :].astype(F32) + ll[ds(at, own), :].astype(F32)
-    if landing:
+
+
+def landing_kernel(stages, sources, cap, refs):
+    refs = list(refs)
+
+    def take(count):
+        out, refs[:count] = refs[:count], []
+        return out
+
+    lh, ll, ih, il = (take(stages) for _ in range(4))
+    (raw_ref, th, tl, sq_ref, t_ref, copy_sems) = take(6)
+    front = raw_ref.shape[0]
+    total = sources * cap
+    width = ih[0].shape[0]
+    share = total // front
+    copies = []
+    for f in range(front):
+        at = (f % sources) * cap + (f // sources) * share
+        copies.append(
+            pltpu.make_async_copy(
+                raw_ref.at[f, :share, :], t_ref.at[at : at + share, :], copy_sems.at[f]
+            )
+        )
+        copies[-1].start()
+    for copy in copies:
+        copy.wait()
+    for q in range(stages):
         part = t_ref.at[:, q * width : (q + 1) * width]
-        subtract_products(part, total, width, th, tl, lh, ll, q * width)
-        times_inverse(part, th, tl, q * width, total, width, invh, invl)
-
-        def square(t, carry):
-            i, j = carry
-            a = (th[ds(i * LANES, LANES), :], tl[ds(i * LANES, LANES), :])
-            b = (th[ds(j * LANES, LANES), :], tl[ds(j * LANES, LANES), :])
-            sq_ref[t] = dot3(a, b, NT)
-            end = j == i
-            return (jnp.where(end, i + 1, i), jnp.where(end, 0, j + 1))
-
-        blocks = total // LANES
-        lax.fori_loop(0, blocks * (blocks + 1) // 2, square, (jnp.int32(0), jnp.int32(0)))
+        subtract_products(part, total, width, th, tl, lh[q], ll[q], q * width)
+        times_inverse(part, th, tl, q * width, total, width, ih[q], il[q])
+
+    def square(t, carry):
+        i, j = carry
+        a = (th[ds(i * LANES, LANES), :], tl[ds(i * LANES, LANES), :])
+        b = (th[ds(j * LANES, LANES), :], tl[ds(j * LANES, LANES), :])
+        sq_ref[t] = dot3(a, b, NT)
+        end = j == i
+        return (jnp.where(end, i + 1, i), jnp.where(end, 0, j + 1))
+
+    blocks = total // LANES
+    lax.fori_loop(0, blocks * (blocks + 1) // 2, square, (jnp.int32(0), jnp.int32(0)))
 
 
 def own_kernel(first, stages, width, refs):
@@ -667,16 +661,16 @@
         chunks.append(lax.dynamic_slice_in_dim(mine_later, col * own, own, 1))
     owners = slot_owners("front", front)
     gathered = [ring_gather(chunks[0], "front", front)]
-    started = gathered[0][-1]
+    started = gathered[0][1:]
     for rnd in range(1, early + 1):
-        gathered.append(ring_gather(after(chunks[rnd], gathered[-1][-1]), "front", front))
+        gathered.append(ring_gather(after(chunks[rnd], gathered[-1][1:]), "front", front))
     here = gathered[-1][1:]
     late = Ring(after(jnp.concatenate(chunks[early + 1 :], axis=1), here), "front", front)
     table_in = jnp.asarray(table)
     place = jnp.stack([(me % per_stage) * own, first_row, bulk_me]).astype(jnp.int32)
 
     own_lands = own_map < pivots
-    own_rank = jnp.where(own_lands, jnp.cumsum(own_lands.astype(jnp.int32)) - 1, -1)
+    own_rank = jnp.where(own_lands, ranks(own_lands), -1)
     pick = (own_rank[None, :] == jnp.arange(cap)[:, None]).astype(F32)
     spreads = front // sources
 
@@ -693,47 +687,43 @@
         return part
 
     compact = jnp.dot(pick, coupling, precision=HIGHEST_PRECISION)
-    landing_part = spread_out(after(compact, started))
     place = after(place, here)
-
     block_rows = (first_row + jnp.arange(count)) // BLOCK
     row_mask = jnp.take(block_pattern, block_rows, axis=0).astype(F32)
     arrow = parent_arrow * jnp.repeat(row_mask, BLOCK, axis=1)
     piece = count // bulk
-    part = after(arrow, chunks[0])
-    pieces = part[:piece]
-    for g in range(1, bulk):
-        moved = lax.ppermute(part[g * piece : (g + 1) * piece], "bulk", [(0, g)])
-        pieces = jnp.where(bulk_me == g, moved, pieces)
-    line_part = spread_out(pieces)
-    share = landing_part.shape[0]
-    extra = line_part.reshape(-1, total)
-    padding = jnp.zeros((-extra.shape[0] % SUB, total), F32)
-    both = jnp.concatenate([landing_part, extra, padding], axis=0)
-    place = after(place, both)
-    both = lax.all_gather(both, "front", axis=0, tiled=False)
-    line = both[:, share : share + extra.shape[0]].reshape((front,) + line_part.shape)
-
     my_maps = jnp.stack([slot[own, :own] for slot in gathered[0]])
     ordered = jnp.sum(
         jnp.where(owners[None, :, None] == jnp.arange(front)[:, None, None], my_maps[None], 0.0), axis=1
     )
-    maps = jnp.stack(bulk_gather(ordered, "bulk", bulk)).astype(jnp.int32)
-    place = after(place, maps)
-    lands = maps[:, :sources] < pivots
-    rank = jnp.cumsum(lands.astype(jnp.int32), axis=2) - 1
-    overflow = jnp.any(rank[:, :, -1] >= cap)
-    chosen = jnp.where(lands, rank, -1)[:, :, None, :] == jnp.arange(cap)[:, None]
-    target = jnp.max(jnp.where(chosen, maps[:, :sources, None, :], -1), axis=3)
-    target = jnp.where(overflow, -1, target).reshape(bulk, blocks, LANES)
-    dense = pivots // blocks
-    rows_of = (jnp.arange(blocks)[:, None] * dense + jnp.arange(dense)[None, :])[:, :, None, None]
-    spread = (jnp.transpose(target, (1, 0, 2))[:, None] == rows_of).astype(BF16)
-    spread = spread.reshape(blocks, dense, bulk * LANES)
-    route = (
-        lax.dynamic_index_in_dim(maps, me, 1, False)[:, None, :]
-        == (first_row + jnp.arange(count))[None, :, None]
-    ).astype(BF16)
+    sent = {}
+
+    def send_first(token):
+        part = after(arrow, token)
+        pieces = part[:piece]
+        for g in range(1, bulk):
+            moved = lax.ppermute(part[g * piece : (g + 1) * piece], "bulk", [(0, g)])
+            pieces = jnp.where(bulk_me == g, moved, pieces)
+        sent["pieces"] = pieces
+        sent["maps"] = jnp.stack(bulk_gather(after(ordered, token), "bulk", bulk)).astype(jnp.int32)
+        return pieces, sent["maps"]
+
+    def send_second(token):
+        sent["landing"] = spread_out(after(compact, token))
+        sent["line"] = spread_out(after(sent["pieces"], token))
+        return sent["landing"], sent["line"]
+
+    def send_third(token):
+        landing, line = sent["landing"], sent["line"]
+        extra = line.reshape(-1, total)
+        padding = jnp.zeros((-extra.shape[0] % SUB, total), F32)
+        both = after(jnp.concatenate([landing, extra, padding], axis=0), token)
+        sent["all"] = lax.all_gather(both, "front", axis=0, tiled=False)
+        share = landing.shape[0]
+        sent["lines"] = sent["all"][:, share : share + extra.shape[0]].reshape((front,) + line.shape)
+        return both
+
+    hooks = [send_first, send_second, send_third]
 
     panels = width // LANES
     total_landing = sources * cap
@@ -755,7 +745,6 @@
         state = None
         for start, stop in zip(split_at[:-1], split_at[1:], strict=True):
             couples = 0 < q < stages - 1 and stop == panels
-            landing = final
             if q < 2 and not final:
                 place = late.advance(place)
             operands = [place]
@@ -772,8 +761,6 @@
                 operands.append(coupling[:, (q - 1) * width : q * width])
                 if q > 1:
                     operands += xs
-            if landing:
-                operands.append(both)
             outs = [
                 shaped((width, width), F32),
                 shaped((width, deep), BF16),
@@ -786,27 +773,20 @@
                 outs += [shaped((own, q * width), BF16)] * 2
             if stop == panels:
                 outs.append(shaped((own, deep), F32))
-            if landing:
-                outs += [shaped((total_landing, total), BF16)] * 2
-                outs.append(shaped((blocks * (blocks + 1) // 2, LANES, LANES), F32))
             if start == 0:
                 scratch.append(pltpu.VMEM((width, deep), F32))
-            if landing:
-                scratch.append(pltpu.VMEM((total_landing, total), F32))
-                scratch.append(pltpu.SemaphoreType.DMA((front,)))
             out = list(
                 vmem_call(
                     functools.partial(
                         lambda *refs, args: child_stage(*args, refs),
                         args=(
                             q, width, own, front, late_rounds, counts, (start, stop),
-                            (total_landing, front, sources, cap), couples, landing,
+                            couples,
                         ),
                     ),
                     outs,
                     [True] * smem
-                    + [False] * (len(operands) - smem - landing)
-                    + [None] * landing,
+                    + [False] * (len(operands) - smem),
                     scratch,
                     pl.CostEstimate(
                         flops=6_000_000_000 * (stop - start), bytes_accessed=1 << 20, transcendentals=0
@@ -821,12 +801,43 @@
             if stop == panels:
                 owned.append(rest[0])
                 rest = rest[1:]
-            if landing:
-                th, tl, squares = rest
             if q < 2 and not final:
                 place = late.arrive(place, state[0])
+                if hooks:
+                    place = after(place, hooks.pop(0)((late.going, late.coming, place)))
         for held, new in zip((lh, ll, ih, il), state[1:], strict=True):
             held.append(new)
+
+    for hook in hooks:
+        hook(place)
+    maps = sent["maps"]
+    lands = maps[:, :sources] < pivots
+    rank = ranks(lands)
+    overflow = jnp.any(rank[:, :, -1] >= cap)
+    chosen = jnp.where(lands, rank, -1)[:, :, None, :] == jnp.arange(cap)[:, None]
+    target = jnp.max(jnp.where(chosen, maps[:, :sources, None, :], -1), axis=3)
+    target = jnp.where(overflow, -1, target).reshape(bulk, blocks, LANES)
+    dense = pivots // blocks
+    rows_of = (jnp.arange(blocks)[:, None] * dense + jnp.arange(dense)[None, :])[:, :, None, None]
+    spread = (jnp.transpose(target, (1, 0, 2))[:, None] == rows_of).astype(BF16)
+    spread = spread.reshape(blocks, dense, bulk * LANES)
+    route = (
+        lax.dynamic_index_in_dim(maps, me, 1, False)[:, None, :]
+        == (first_row + jnp.arange(count))[None, :, None]
+    ).astype(BF16)
+
+    operands = lh + ll + ih + il
+    th, tl, squares = vmem_call(
+        lambda *refs: landing_kernel(stages, sources, cap, refs),
+        [
+            shaped((total_landing, total), BF16),
+            shaped((total_landing, total), BF16),
+            shaped((blocks * (blocks + 1) // 2, LANES, LANES), F32),
+        ],
+        [False] * len(operands) + [None],
+        [pltpu.VMEM((total_landing, total), F32), pltpu.SemaphoreType.DMA((front,))],
+        pl.CostEstimate(flops=20_000_000_000, bytes_accessed=1 << 20, transcendentals=0),
+    )(*operands, sent["all"])
 
     lower_rows = jnp.zeros((own, total), F32)
     for q in range(stages):
@@ -870,7 +881,7 @@
         ]
         return changed, arrow - added
 
-    lines = bulk_gather(line, "bulk", bulk)
+    lines = bulk_gather(sent["lines"], "bulk", bulk)
     lines, arrow = lax.cond(overflow, landing_whole, unchanged, lines, arrow, x_own)
 
     all_con = bulk_gather(con, "bulk", bulk, low_first=True)

time: 447 us -> 423 us (0.946)
  the two profiles are of different devices: /device:TPU:20 before, /device:TPU:28 now
where the time goes in v5:
time: 423 us; the launch traced here: 415 us
  Pallas kernels  233 us (55%)
  waiting for transfers between devices  91.1 us (22%)
  starting transfers between devices  33.7 us (8%)
  local copies, waits for them, and re-layouts  18.5 us (4%)
  between operations  17.4 us (4%)
  other arithmetic  15.3 us (4%)
    pallas_call x6, Pallas kernels, on_device(): vmem_call(functools.partial(lambda *refs, args: child_stage(*args, refs),...  136 us
    ppermute x12, waiting for transfers between devices, advance(): self.going = lax.ppermute(self.going, self.axis, self.ahead)  61.8 us
    pallas_call x1, Pallas kernels, on_device(): vmem_call(lambda *refs: parent_kernel(bulk, blocks, width, sources, refs)...  54.4 us
    pallas_call x1, Pallas kernels, on_device(): vmem_call(lambda *refs: landing_kernel(stages, sources, cap, refs), [shap...  23.7 us
    ppermute x2, waiting for transfers between devices, spread_out(): lax.ppermute(x[k * rows:(k + 1) * rows], 'front', [(s, s + k * sources) f...  13.4 us
    ppermute x9, starting transfers between devices, advance(): self.coming = lax.ppermute(self.coming, self.axis, self.back)  12.6 us
    pallas_call x1, Pallas kernels, on_device(): vmem_call(lambda *refs: own_kernel(solved, stages, width, refs), [shaped(...  11.7 us
  transfers between devices with their start and end apart: 39, of which 18 were waited for; matrix products, arithmetic and copies ran while one was open for 7% of the time, Pallas kernels for 54%

profile of v5, /device:TPU:28, one launch (start us, length us, event | category | flops | bytes accessed | tf_op | source)
XLA Modules:
  0.0 414.7 jit_solution(981517102025925126)
XLA Ops:
  11.7 9.1 %collective-permute-done.refs_4_ = f32[264,384]{1,0:T(8,128)S(1)} collective-permute-done((f32[264,384]{1,0:T(8,128)S(1)}, f32[264,384]{1,0:T(8,128)S(1)}, u32[]{:S(2)}, u32[]{:S(2)}) %collective-permute-start) | collective-permute-done | bytes 405536 | tf_op jit(solution)/shard_map/ppermute | solution.py:309
  24.0 8.0 %collective-permute-done.2.refs_5_ = f32[264,384]{1,0:T(8,128)} collective-permute-done((f32[264,384]{1,0:T(8,128)S(1)}, f32[264,384]{1,0:T(8,128)}, u32[]{:S(2)}, u32[]{:S(2)}) %collective-permute-start.2) | collective-permute-done | bytes 405536 | tf_op jit(solution)/shard_map/ppermute | solution.py:309
  33.6 1.6 collective-permute-start.5
  35.9 6.6 %collective-permute-done.4.refs_6_ = f32[264,384]{1,0:T(8,128)} collective-permute-done((f32[264,384]{1,0:T(8,128)}, f32[264,384]{1,0:T(8,128)}, u32[]{:S(2)}, u32[]{:S(2)}) %collective-permute-start.4) | collective-permute-done | bytes 405536 | tf_op jit(solution)/shard_map/ppermute | solution.py:309
  46.9 5.6 %collective-permute-done.6.refs_7_ = f32[264,384]{1,0:T(8,128)} collective-permute-done((f32[264,384]{1,0:T(8,128)}, f32[264,384]{1,0:T(8,128)}, u32[]{:S(2)}, u32[]{:S(2)}) %collective-permute-start.6) | collective-permute-done | bytes 405536 | tf_op jit(solution)/shard_map/ppermute | solution.py:309
  56.5 4.9 %collective-permute-done.7.refs_12_ = f32[256,256]{1,0:T(8,128)S(1)} collective-permute-done((f32[256,256]{1,0:T(8,128)S(1)}, f32[256,256]{1,0:T(8,128)S(1)}, u32[]{:S(2)}, u32[]{:S(2)}) %collective-permute-start.7) | collective-permute-done | bytes 262176 | tf_op jit(solution)/shard_map/ppermute | solution.py:309
  64.7 5.6 %collective-permute-done.9.refs_13_ = f32[256,256]{1,0:T(8,128)S(1)} collective-permute-done((f32[256,256]{1,0:T(8,128)S(1)}, f32[256,256]{1,0:T(8,128)S(1)}, u32[]{:S(2)}, u32[]{:S(2)}) %collective-permute-start.9) | collective-permute-done | bytes 262176 | tf_op jit(solution)/shard_map/ppermute | solution.py:309
  71.0 1.6 collective-permute-start.12
  72.7 5.2 %collective-permute-done.11.refs_14_ = f32[256,256]{1,0:T(8,128)S(1)} collective-permute-done((f32[256,256]{1,0:T(8,128)S(1)}, f32[256,256]{1,0:T(8,128)S(1)}, u32[]{:S(2)}, u32[]{:S(2)}) %collective-permute-start.11) | collective-permute-done | bytes 262176 | tf_op jit(solution)/shard_map/ppermute | solution.py:309
  84.9 2.4 collective-permute-done.13.refs_15_
  87.8 1.6 collective-permute-start.15
  89.4 13.7 %shard_map.112 = (f32[512,512]{1,0:T(8,128)}, bf16[512,512]{1,0:T(8,128)(2,1)}, bf16[512,512]{1,0:T(8,128)(2,1)}, bf16[512,512]{1,0:T(8,128)(2,1)}, bf16[512,512]{1,0:T(8,128)(2,1)}) custom-call(s32[3]{0:T(128)} %pad_add_fusion.refs_0_, s32[8]{0:T(128)} %copy-done.11, s32[3,8]{1,0:T(4,128)} %constant.198.clone.refs_2_, f32[264,384]{1,0:T(8,128)} %copy-done.6, ...), custom_call_target="tpu_custom_call" | custom-call | flops 12000000000 | bytes 1048576 | tf_op jit(solution)/shard_map/pallas_call | solution.py:779
  111.1 1.8 fusion.15
  113.0 6.3 %collective-permute-done.17 = f32[64,1024]{1,0:T(8,128)} collective-permute-done((f32[64,1024]{1,0:T(8,128)}, f32[64,1024]{1,0:T(8,128)}, u32[]{:S(2)}, u32[]{:S(2)}) %collective-permute-start.17) | collective-permute-done | bytes 262176 | tf_op jit(solution)/shard_map/ppermute | solution.py:705
  120.2 1.9 slice.96
  123.4 1.8 collective-permute-start.25
  125.2 14.2 %shard_map.113 = (f32[512,512]{1,0:T(8,128)}, bf16[512,512]{1,0:T(8,128)(2,1)}, bf16[512,512]{1,0:T(8,128)(2,1)}, bf16[512,512]{1,0:T(8,128)(2,1)}, bf16[512,512]{1,0:T(8,128)(2,1)}, /*index=5*/f32[256,512]{1,0:T(8,128)}) custom-call(s32[3]{0:T(128)} %pad_add_fusion.refs_0_, ...), custom_call_target="tpu_custom_call", output_to_operand_aliasing={{0}: (1, {}), {1}: (2, {}), {2}: (3, {}), {3}: (4, {}), {4}... | custom-call | flops 12000000000 | bytes 1048576 | tf_op jit(solution)/shard_map/pallas_call | solution.py:779
  141.4 13.4 %collective-permute-done.25 = f32[32,1024]{1,0:T(8,128)S(1)} collective-permute-done((f32[32,1024]{1,0:T(8,128)S(1)}, f32[32,1024]{1,0:T(8,128)S(1)}, u32[]{:S(2)}, u32[]{:S(2)}) %collective-permute-start.25) | collective-permute-done | bytes 131104 | tf_op jit(solution)/shard_map/ppermute | solution.py:681
  156.2 17.4 %shard_map.114 = (f32[512,512]{1,0:T(8,128)}, bf16[512,1024]{1,0:T(8,128)(2,1)}, bf16[512,1024]{1,0:T(8,128)(2,1)}, bf16[512,512]{1,0:T(8,128)(2,1)}, bf16[512,512]{1,0:T(8,128)(2,1)}) custom-call(s32[3]{0:T(128)} %pad_add_fusion.refs_0_, s32[8]{0:T(128)} %copy-done.11, s32[3,8]{1,0:T(4,128)} %constant.198.clone.refs_2_, f32[264,384]{1,0:T(8,128)} %copy-done.6, ...), custom_call_target="tpu_custom_call" | custom-call | flops 12000000000 | bytes 1048576 | tf_op jit(solution)/shard_map/pallas_call | solution.py:779
  181.2 16.2 %shard_map.115 = (f32[512,512]{1,0:T(8,128)}, bf16[512,1024]{1,0:T(8,128)(2,1)}, bf16[512,1024]{1,0:T(8,128)(2,1)}, bf16[512,512]{1,0:T(8,128)(2,1)}, bf16[512,5...) custom-call(s32[3]{0:T(128)} %pad_add_fusion.refs_0_, ...), custom_call_target="tpu_custom_call", output_to_operand_aliasing={{0}: (1, {}), {1}: (2, {}), {2}: (3, {}), {3}: (4, {}), {4}... | custom-call | flops 12000000000 | bytes 1048576 | tf_op jit(solution)/shard_map/pallas_call | solution.py:779
  197.4 14.3 %collective-permute-done.28.refs_23_ = f32[256,512]{1,0:T(8,128)S(1)} collective-permute-done((f32[256,512]{1,0:T(8,128)}, f32[256,512]{1,0:T(8,128)S(1)}, u32[]{:S(2)}, u32[]{:S(2)}) %collective-permute-start.28) | collective-permute-done | bytes 524320 | tf_op jit(solution)/shard_map/ppermute | solution.py:309
  212.6 34.7 %shard_map.116 = (f32[512,512]{1,0:T(8,128)}, bf16[512,1536]{1,0:T(8,128)(2,1)}, bf16[512,1536]{1,0:T(8,128)(2,1)}, bf16[512,512]{1,0:T(8,128)(2,1)}, bf16[512,5...) custom-call(s32[3]{0:T(128)} %pad_add_fusion.refs_0_, ...), custom_call_target="tpu_custom_call" | custom-call | flops 24000000000 | bytes 1048576 | tf_op jit(solution)/shard_map/pallas_call | solution.py:779
  247.2 39.5 %shard_map.117 = (f32[512,512]{1,0:T(8,128)}, bf16[512,2048]{1,0:T(8,128)(2,1)}, bf16[512,2048]{1,0:T(8,128)(2,1)}, bf16[512,512]{1,0:T(8,128)(2,1)}, bf16[512,512]{1,0:T(8,128)(2,1)}, /*index=5*/f32[256,2048]{1,0:T(8,128)}) custom-call(s32[3]{0:T(128)} %pad_add_fusion.refs_0_, s32[8]{0:T(128)} %copy-done.11, s32[3,8]{1,0:T(4,128)} %constant.198.clone.refs_2_, ...), custom_call_target="tpu_custom_call" | custom-call | flops 24000000000 | bytes 1048576 | tf_op jit(solution)/shard_map/pallas_call | solution.py:779
  289.2 3.1 collective-permute-start.30
  292.3 23.7 %shard_map.118 = (bf16[512,2048]{1,0:T(8,128)(2,1)}, bf16[512,2048]{1,0:T(8,128)(2,1)}, f32[10,128,128]{2,1,0:T(8,128)}) custom-call(bf16[512,512]{1,0:T(8,128)(2,1)} %get-tuple-element.154.refs_19_.refs_6_.refs_27_.refs_0_, bf16[512,1024]{1,0:T(8,128)(2,1)} %get-tuple-element.169.refs_28_.refs_1_, ...), custom_call_target="tpu_custom_call" | custom-call | flops 20000000000 | bytes 1048576 | tf_op jit(solution)/shard_map/pallas_call | solution.py:830
  316.6 11.7 %shard_map.119 = (f32[256,2048]{1,0:T(8,128)S(1)}, f32[256,512]{1,0:T(8,128)}) custom-call(f32[256,1024]{1,0:T(8,128)} %slice.120.refs_0_, bf16[256,1024]{1,0:T(8,128)(2,1)} %get-tuple-element.183.refs_1_, bf16[256,1024]{1,0:T(8,128)(2,1)} %get-tuple-element.184.refs_2_, bf16[512,1536]{1,0:T(8,128)(2,1)} %get-tuple-element.175.refs_29_.refs_2_.refs_3_, ...), custom_call_target="tpu_custom_call" | custom-call | flops 10000000000 | bytes 1048576 | tf_op jit(solution)/shard_map/pallas_call | solution.py:850
  328.3 5.2 %collective-permute-done.36.refs_8_ = f32[10,128,128]{2,1,0:T(8,128)} collective-permute-done((f32[10,128,128]{2,1,0:T(8,128)}, f32[10,128,128]{2,1,0:T(8,128)}, u32[]{:S(2)}, u32[]{:S(2)}) %collective-permute-start.36) | collective-permute-done | bytes 655392 | tf_op jit(solution)/shard_map/ppermute | solution.py:351
  335.8 4.4 %select_bitcast_fusion = f32[1,256,2048]{2,1,0:T(8,128)} fusion(f32[256,2048]{1,0:T(8,128)} %get-tuple-element.179, f32[256,512]{1,0:T(8,128)} %get-tuple-element.182, f32[256,1024]{1,0:T(8,128)} %get-tuple-element.181, f32[256,1536]{1,0:T(8,128)} %get-tuple-element.180, pred[]{:T(512)S(6)} %eq.150, pred[]{:T(512)S(6)} %eq.149, pred[]{:T(512)S(6)} %eq.148, ...), kind=kLoop, calls=%fused_computation.30 | loop fusion | flops 2097152 | bytes 7340036 | tf_op jit(solution)/shard_map/broadcast_in_dim | solution.py:911
  340.4 1.7 collective-permute-start.34
  342.2 3.2 conditional.1
  345.5 54.4 %shard_map.120 = (bf16[1024,1024]{1,0:T(8,128)(2,1)}, bf16[1024,1024]{1,0:T(8,128)(2,1)}, bf16[2,512,512]{2,1,0:T(8,128)(2,1)}, bf16[2,512,512]{2,1,0:T(8,128)(2,1)}) custom-call(s32[3]{0:T(128)} %pad_add_fusion.refs_0_, bf16[4,256,512]{2,1,0:T(8,128)(2,1)} %compare_convert_fusion.refs_1_.refs_3_, f32[8,32,1024]{2,1,0:T(8,128)} %get-tuple-element.194.refs_2_, ...), custom_call_target="tpu_custom_call" | custom-call | flops 60000002048 | bytes 16777216 | tf_op jit(solution)/shard_map/pallas_call | solution.py:888
  399.8 7.8 %shard_map.121 = f32[256,1024]{1,0:T(8,128)} custom-call(s32[3]{0:T(128)} %pad_add_fusion.refs_0_, f32[256,1024]{1,0:T(8,128)S(1)} %get-tuple-element.192.refs_1_, bf16[4,256,256]{2,1,0:T(8,128)(2,1)} %compare_convert_fusion.1.refs_2_, bf16[4,256,512]{2,1,0:T(8,128)(2,1)} %compare_convert_fusion.refs_1_.refs_3_, f32[256,512]{1,0:T(8,128)} %get-tuple-element.193.refs_4_, ...), custom_call_target="tpu_custom_call" | custom-call | tf_op jit(solution)/shard_map/pallas_call | solution.py:901
  (170 shorter events, 54.6 us)
Async XLA Ops:
  7.2 279.6 %all-gather.6.cloned.1.call-start = ((), (), s32[]{:S(2)}) async-start(), calls=%async_computation.4 | async-start | bytes 5898240 | tf_op jit(solution)/shard_map/all_gather | solution.py:721
  9.6 11.2 %collective-permute-start = (f32[264,384]{1,0:T(8,128)S(1)}, f32[264,384]{1,0:T(8,128)S(1)}, u32[]{:S(2)}, u32[]{:S(2)}) collective-permute-start(f32[264,384]{1,0:T(8,128)S(1)} %select_maximum_fusion.refs_3_), channel_id=1, source_target_pairs={{0,2},{2,4},{4,6},{6,7},{7,5},{5,3},{3,1},{1,0},{8,10},{10,12},{12... | collective-permute-start | bytes 1216520 | tf_op jit(solution)/shard_map/ppermute | solution.py:309
  11.1 10.8 %collective-permute-start.1 = (f32[264,384]{1,0:T(8,128)S(1)}, f32[264,384]{1,0:T(8,128)S(1)}, u32[]{:S(2)}, u32[]{:S(2)}) collective-permute-start(f32[264,384]{1,0:T(8,128)S(1)} %select_maximum_fusion.refs_3_), channel_id=1, source_target_pairs={{2,0},{4,2},{6,4},{7,6},{5,7},{3,5},{1,3},{0,1},{10,8},{12,10},{14... | collective-permute-start | bytes 1216520 | tf_op jit(solution)/shard_map/ppermute | solution.py:312
  22.0 10.0 %collective-permute-start.2 = (f32[264,384]{1,0:T(8,128)S(1)}, f32[264,384]{1,0:T(8,128)}, u32[]{:S(2)}, u32[]{:S(2)}) collective-permute-start(f32[264,384]{1,0:T(8,128)S(1)} %collective-permute-done.refs_4_), channel_id=1, source_target_pairs={{0,2},{2,4},{4,6},{6,7},{7,5},{5,3},{3,1},{1,0},{8,10},{10,12},{12... | collective-permute-start | bytes 1216520 | tf_op jit(solution)/shard_map/ppermute | solution.py:309
  23.0 10.1 %collective-permute-start.3 = (f32[264,384]{1,0:T(8,128)S(1)}, f32[264,384]{1,0:T(8,128)}, u32[]{:S(2)}, u32[]{:S(2)}) collective-permute-start(f32[264,384]{1,0:T(8,128)S(1)} %collective-permute-done.1.refs_8_), channel_id=1, source_target_pairs={{2,0},{4,2},{6,4},{7,6},{5,7},{3,5},{1,3},{0,1},{10,8},{12,10},{14... | collective-permute-start | bytes 1216520 | tf_op jit(solution)/shard_map/ppermute | solution.py:312
  33.1 9.4 %collective-permute-start.4 = (f32[264,384]{1,0:T(8,128)}, f32[264,384]{1,0:T(8,128)}, u32[]{:S(2)}, u32[]{:S(2)}) collective-permute-start(f32[264,384]{1,0:T(8,128)} %collective-permute-done.2.refs_5_), channel_id=1, source_target_pairs={{0,2},{2,4},{4,6},{6,7},{7,5},{5,3},{3,1},{1,0},{8,10},{10,12},{12... | collective-permute-start | bytes 1216520 | tf_op jit(solution)/shard_map/ppermute | solution.py:309
  33.6 9.2 %collective-permute-start.5 = (f32[264,384]{1,0:T(8,128)}, f32[264,384]{1,0:T(8,128)}, u32[]{:S(2)}, u32[]{:S(2)}) collective-permute-start(f32[264,384]{1,0:T(8,128)} %collective-permute-done.3.refs_9_), channel_id=1, source_target_pairs={{2,0},{4,2},{6,4},{7,6},{5,7},{3,5},{1,3},{0,1},{10,8},{12,10},{14... | collective-permute-start | bytes 1216520 | tf_op jit(solution)/shard_map/ppermute | solution.py:312
  42.8 9.7 %collective-permute-start.6 = (f32[264,384]{1,0:T(8,128)}, f32[264,384]{1,0:T(8,128)}, u32[]{:S(2)}, u32[]{:S(2)}) collective-permute-start(f32[264,384]{1,0:T(8,128)} %collective-permute-done.4.refs_6_), channel_id=1, source_target_pairs={{0,2},{2,4},{4,6},{6,7},{7,5},{5,3},{3,1},{1,0},{8,10},{10,12},{12... | collective-permute-start | bytes 1216520 | tf_op jit(solution)/shard_map/ppermute | solution.py:309
  52.5 8.9 %collective-permute-start.7 = (f32[256,256]{1,0:T(8,128)S(1)}, f32[256,256]{1,0:T(8,128)S(1)}, u32[]{:S(2)}, u32[]{:S(2)}) collective-permute-start(f32[256,256]{1,0:T(8,128)S(1)} %get-tuple-element.129.refs_11_), channel_id=1, source_target_pairs={{0,2},{2,4},{4,6},{6,7},{7,5},{5,3},{3,1},{1,0},{8,10},{10,12},{12... | collective-permute-start | bytes 786440 | tf_op jit(solution)/shard_map/ppermute | solution.py:309
  53.0 9.1 %collective-permute-start.8 = (f32[256,256]{1,0:T(8,128)S(1)}, f32[256,256]{1,0:T(8,128)S(1)}, u32[]{:S(2)}, u32[]{:S(2)}) collective-permute-start(f32[256,256]{1,0:T(8,128)S(1)} %get-tuple-element.129.refs_11_), channel_id=1, source_target_pairs={{2,0},{4,2},{6,4},{7,6},{5,7},{3,5},{1,3},{0,1},{10,8},{12,10},{14... | collective-permute-start | bytes 786440 | tf_op jit(solution)/shard_map/ppermute | solution.py:312
  62.0 8.3 %collective-permute-start.9 = (f32[256,256]{1,0:T(8,128)S(1)}, f32[256,256]{1,0:T(8,128)S(1)}, u32[]{:S(2)}, u32[]{:S(2)}) collective-permute-start(f32[256,256]{1,0:T(8,128)S(1)} %collective-permute-done.7.refs_12_), channel_id=1, source_target_pairs={{0,2},{2,4},{4,6},{6,7},{7,5},{5,3},{3,1},{1,0},{8,10},{10,12},{12... | collective-permute-start | bytes 786440 | tf_op jit(solution)/shard_map/ppermute | solution.py:309
  62.5 8.0 %collective-permute-start.10 = (f32[256,256]{1,0:T(8,128)S(1)}, f32[256,256]{1,0:T(8,128)S(1)}, u32[]{:S(2)}, u32[]{:S(2)}) collective-permute-start(f32[256,256]{1,0:T(8,128)S(1)} %collective-permute-done.8.refs_16_), channel_id=1, source_target_pairs={{2,0},{4,2},{6,4},{7,6},{5,7},{3,5},{1,3},{0,1},{10,8},{12,10},{14... | collective-permute-start | bytes 786440 | tf_op jit(solution)/shard_map/ppermute | solution.py:312
  77.9 9.4 %collective-permute-start.13 = (f32[256,256]{1,0:T(8,128)S(1)}, f32[256,256]{1,0:T(8,128)}, u32[]{:S(2)}, u32[]{:S(2)}) collective-permute-start(f32[256,256]{1,0:T(8,128)S(1)} %collective-permute-done.11.refs_14_), channel_id=1, source_target_pairs={{0,2},{2,4},{4,6},{6,7},{7,5},{5,3},{3,1},{1,0},{8,10},{10,12},{12... | collective-permute-start | bytes 786440 | tf_op jit(solution)/shard_map/ppermute | solution.py:309
  87.3 15.8 %collective-permute-start.14 = (f32[256,512]{1,0:T(8,128)}, f32[256,512]{1,0:T(8,128)}, u32[]{:S(2)}, u32[]{:S(2)}) collective-permute-start(f32[256,512]{1,0:T(8,128)} %pad_maximum_fusion.1.refs_19_), channel_id=1, source_target_pairs={{0,2},{2,4},{4,6},{6,7},{7,5},{5,3},{3,1},{1,0},{8,10},{10,12},{12... | collective-permute-start | bytes 1572872 | tf_op jit(solution)/shard_map/ppermute | solution.py:309
  87.8 15.3 %collective-permute-start.15 = (f32[256,512]{1,0:T(8,128)}, f32[256,512]{1,0:T(8,128)}, u32[]{:S(2)}, u32[]{:S(2)}) collective-permute-start(f32[256,512]{1,0:T(8,128)} %pad_maximum_fusion.1.refs_19_), channel_id=1, source_target_pairs={{2,0},{4,2},{6,4},{7,6},{5,7},{3,5},{1,3},{0,1},{10,8},{12,10},{14... | collective-permute-start | bytes 1572872 | tf_op jit(solution)/shard_map/ppermute | solution.py:312
  103.7 16.5 %collective-permute-start.22 = (f32[256,512]{1,0:T(8,128)}, f32[256,512]{1,0:T(8,128)}, u32[]{:S(2)}, u32[]{:S(2)}) collective-permute-start(f32[256,512]{1,0:T(8,128)} %collective-permute-done.14.refs_20_), channel_id=1, source_target_pairs={{0,2},{2,4},{4,6},{6,7},{7,5},{5,3},{3,1},{1,0},{8,10},{10,12},{12... | collective-permute-start | bytes 1572872 | tf_op jit(solution)/shard_map/ppermute | solution.py:309
  104.2 16.0 %collective-permute-start.23 = (f32[256,512]{1,0:T(8,128)}, f32[256,512]{1,0:T(8,128)}, u32[]{:S(2)}, u32[]{:S(2)}) collective-permute-start(f32[256,512]{1,0:T(8,128)} %collective-permute-done.15.refs_24_), channel_id=1, source_target_pairs={{2,0},{4,2},{6,4},{7,6},{5,7},{3,5},{1,3},{0,1},{10,8},{12,10},{14... | collective-permute-start | bytes 1572872 | tf_op jit(solution)/shard_map/ppermute | solution.py:312
  108.4 10.8 %collective-permute-start.17 = (f32[64,1024]{1,0:T(8,128)}, f32[64,1024]{1,0:T(8,128)}, u32[]{:S(2)}, u32[]{:S(2)}) collective-permute-start(f32[64,1024]{1,0:T(8,128)} %get-tuple-element.216), channel_id=1, source_target_pairs={{0,16},{1,17},{2,18},{3,19},{4,20},{5,21},{6,22},{7,23}} | collective-permute-start | bytes 786440 | tf_op jit(solution)/shard_map/ppermute | solution.py:705
  109.7 9.5 %collective-permute-start.18 = (f32[64,1024]{1,0:T(8,128)}, f32[64,1024]{1,0:T(8,128)}, u32[]{:S(2)}, u32[]{:S(2)}) collective-permute-start(f32[64,1024]{1,0:T(8,128)} %get-tuple-element.215), channel_id=1, source_target_pairs={{0,8},{1,9},{2,10},{3,11},{4,12},{5,13},{6,14},{7,15}} | collective-permute-start | bytes 786440 | tf_op jit(solution)/shard_map/ppermute | solution.py:705
  122.1 32.8 %collective-permute-start.24 = (f32[64,2048]{1,0:T(8,128)}, f32[64,2048]{1,0:T(8,128)}, u32[]{:S(2)}, u32[]{:S(2)}) collective-permute-start(f32[64,2048]{1,0:T(8,128)} %slice.96), channel_id=1, source_target_pairs={{0,4},{1,5},{2,6},{3,7},{8,12},{9,13},{10,14},{11,15},{16,20},{17,... | collective-permute-start | bytes 1572872 | tf_op jit(solution)/shard_map/ppermute | solution.py:681
  123.4 31.4 %collective-permute-start.25 = (f32[32,1024]{1,0:T(8,128)S(1)}, f32[32,1024]{1,0:T(8,128)S(1)}, u32[]{:S(2)}, u32[]{:S(2)}) collective-permute-start(f32[32,1024]{1,0:T(8,128)S(1)} %slice.98), channel_id=1, source_target_pairs={{0,4},{1,5},{2,6},{3,7},{8,12},{9,13},{10,14},{11,15},{16,20},{17,... | collective-permute-start | bytes 393224 | tf_op jit(solution)/shard_map/ppermute | solution.py:681
  139.4 34.2 %collective-permute-start.26 = (f32[256,512]{1,0:T(8,128)}, f32[256,512]{1,0:T(8,128)}, u32[]{:S(2)}, u32[]{:S(2)}) collective-permute-start(f32[256,512]{1,0:T(8,128)} %collective-permute-done.22.refs_21_), channel_id=1, source_target_pairs={{0,2},{2,4},{4,6},{6,7},{7,5},{5,3},{3,1},{1,0},{8,10},{10,12},{12... | collective-permute-start | bytes 1572872 | tf_op jit(solution)/shard_map/ppermute | solution.py:309
  139.9 33.8 %collective-permute-start.27 = (f32[256,512]{1,0:T(8,128)}, f32[256,512]{1,0:T(8,128)}, u32[]{:S(2)}, u32[]{:S(2)}) collective-permute-start(f32[256,512]{1,0:T(8,128)} %collective-permute-done.23.refs_25_), channel_id=1, source_target_pairs={{2,0},{4,2},{6,4},{7,6},{5,7},{3,5},{1,3},{0,1},{10,8},{12,10},{14... | collective-permute-start | bytes 1572872 | tf_op jit(solution)/shard_map/ppermute | solution.py:312
  180.1 31.7 %collective-permute-start.28 = (f32[256,512]{1,0:T(8,128)}, f32[256,512]{1,0:T(8,128)S(1)}, u32[]{:S(2)}, u32[]{:S(2)}) collective-permute-start(f32[256,512]{1,0:T(8,128)} %collective-permute-done.26.refs_22_), channel_id=1, source_target_pairs={{0,2},{2,4},{4,6},{6,7},{7,5},{5,3},{3,1},{1,0},{8,10},{10,12},{12... | collective-permute-start | bytes 1572872 | tf_op jit(solution)/shard_map/ppermute | solution.py:309
  289.2 51.2 %collective-permute-start.29 = (f32[8,32,1024]{2,1,0:T(8,128)}, f32[8,32,1024]{2,1,0:T(8,128)}, u32[]{:S(2)}, u32[]{:S(2)}) collective-permute-start(f32[8,32,1024]{2,1,0:T(8,128)} %reshape.168), channel_id=1, source_target_pairs={{0,8},{8,0},{16,24},{24,16},{1,9},{9,1},{17,25},{25,17},{2,10},{10... | collective-permute-start | bytes 3145736 | tf_op jit(solution)/shard_map/ppermute | solution.py:351
  289.2 27.4 %collective-permute-start.30 = (f32[8,32,1024]{2,1,0:T(8,128)}, f32[8,32,1024]{2,1,0:T(8,128)}, u32[]{:S(2)}, u32[]{:S(2)}) collective-permute-start(f32[8,32,1024]{2,1,0:T(8,128)} %reshape.168), channel_id=1, source_target_pairs={{0,16},{8,24},{16,0},{24,8},{1,17},{9,25},{17,1},{25,9},{2,18},{10... | collective-permute-start | bytes 3145736 | tf_op jit(solution)/shard_map/ppermute | solution.py:351
  316.0 29.4 %collective-permute-start.35 = (f32[10,128,128]{2,1,0:T(8,128)}, f32[10,128,128]{2,1,0:T(8,128)}, u32[]{:S(2)}, u32[]{:S(2)}) collective-permute-start(f32[10,128,128]{2,1,0:T(8,128)} %get-tuple-element.198.refs_6_), channel_id=1, source_target_pairs={{0,8},{8,0},{16,24},{24,16},{1,9},{9,1},{17,25},{25,17},{2,10},{10... | collective-permute-start | bytes 1966088 | tf_op jit(solution)/shard_map/ppermute | solution.py:351
  316.3 17.2 %collective-permute-start.36 = (f32[10,128,128]{2,1,0:T(8,128)}, f32[10,128,128]{2,1,0:T(8,128)}, u32[]{:S(2)}, u32[]{:S(2)}) collective-permute-start(f32[10,128,128]{2,1,0:T(8,128)} %get-tuple-element.198.refs_6_), channel_id=1, source_target_pairs={{0,16},{8,24},{16,0},{24,8},{1,17},{9,25},{17,1},{25,9},{2,18},{10... | collective-permute-start | bytes 1966088 | tf_op jit(solution)/shard_map/ppermute | solution.py:351
  316.6 25.6 %collective-permute-start.31 = (f32[8,32,1024]{2,1,0:T(8,128)}, f32[8,32,1024]{2,1,0:T(8,128)}, u32[]{:S(2)}, u32[]{:S(2)}) collective-permute-start(f32[8,32,1024]{2,1,0:T(8,128)} %collective-permute-done.30), channel_id=1, source_target_pairs={{0,8},{8,0},{16,24},{24,16},{1,9},{9,1},{17,25},{25,17},{2,10},{10... | collective-permute-start | bytes 3145736 | tf_op jit(solution)/shard_map/ppermute | solution.py:351
  333.5 11.9 %collective-permute-start.37 = (f32[10,128,128]{2,1,0:T(8,128)}, f32[10,128,128]{2,1,0:T(8,128)}, u32[]{:S(2)}, u32[]{:S(2)}) collective-permute-start(f32[10,128,128]{2,1,0:T(8,128)} %collective-permute-done.36.refs_8_), channel_id=1, source_target_pairs={{0,8},{8,0},{16,24},{24,16},{1,9},{9,1},{17,25},{25,17},{2,10},{10... | collective-permute-start | bytes 1966088 | tf_op jit(solution)/shard_map/ppermute | solution.py:351
  340.1 59.7 %collective-permute-start.33 = (f32[256,512]{1,0:T(8,128)}, f32[256,512]{1,0:T(8,128)}, u32[]{:S(2)}, u32[]{:S(2)}) collective-permute-start(f32[256,512]{1,0:T(8,128)} %get-tuple-element.193.refs_4_), channel_id=1, source_target_pairs={{0,16},{8,24},{16,0},{24,8},{1,17},{9,25},{17,1},{25,9},{2,18},{10... | collective-permute-start | bytes 1572872 | tf_op jit(solution)/shard_map/ppermute | solution.py:351
  340.4 59.4 %collective-permute-start.34 = (f32[256,512]{1,0:T(8,128)}, f32[256,512]{1,0:T(8,128)}, u32[]{:S(2)}, u32[]{:S(2)}) collective-permute-start(f32[256,512]{1,0:T(8,128)} %collective-permute-done.32.refs_5_), channel_id=1, source_target_pairs={{0,16},{8,24},{16,0},{24,8},{1,17},{9,25},{17,1},{25,9},{2,18},{10... | collective-permute-start | bytes 1572872 | tf_op jit(solution)/shard_map/ppermute | solution.py:351
  (31 other events, 404.4 us)
Sparse Core Ops, SparseCore 0:
  174.7 90.2 all-gather.5

commit v6 on v5

--- a/solution.py
+++ b/solution.py
@@ -18,6 +18,7 @@
 HIGHEST_PRECISION = lax.Precision.HIGHEST
 NT = (((1,), (1,)), ((), ()))
 NN = (((1,), (0,)), ((), ()))
+TN = (((0,), (0,)), ((), ()))
 F32 = jnp.float32
 BF16 = jnp.bfloat16
 
@@ -202,8 +203,8 @@
         invh[here, here] = inv[0]
         invl[here, here] = inv[1]
         following = ds(jnp.minimum(p + 1, last) * LANES, LANES)
-        beside = split(jnp.where(p < last, dot3(split(s_ref[following, here]), inv, NT), 0.0))
-        s_ref[following, following] = s_ref[following, following] - dot3(beside, beside, NT)
+        beside = split(jnp.where(p < last, dot3(inv, split(s_ref[following, here]), NT), 0.0))
+        s_ref[following, following] = s_ref[following, following] - dot3(beside, beside, TN)
         return carry
 
     lax.fori_loop(start, stop, panel, 0)
@@ -224,14 +225,16 @@
     xl[rows, q * width : (q + 1) * width] = low
 
 
-def vmem_call(body, out_shapes, in_kinds, scratch, cost=None, aliases=None):
+def vmem_call(body, out_shapes, in_kinds, scratch, cost=None, aliases=None, out_kinds=None):
     spaces = {True: pltpu.SMEM, False: pltpu.VMEM, None: pl.ANY}
     specs = [pl.BlockSpec(memory_space=spaces[k]) for k in in_kinds]
     return pl.pallas_call(
         body,
         out_shape=out_shapes,
         in_specs=specs,
-        out_specs=[pl.BlockSpec(memory_space=pltpu.VMEM)] * len(out_shapes),
+        out_specs=[
+            pl.BlockSpec(memory_space=spaces[k]) for k in out_kinds or [False] * len(out_shapes)
+        ],
         scratch_shapes=scratch,
         compiler_params=pltpu.CompilerParams(vmem_limit_bytes=VMEM_LIMIT),
         cost_estimate=cost,
@@ -425,13 +428,17 @@
     if couples:
         b_ref = take(1)[0]
         old_x = take(2) if q > 1 else None
+    if stop == panels:
+        take(1)
     s_out, lh, ll, invh, invl = take(5)
     if couples:
         xh, xl = take(2)
     if stop == panels:
-        own_ref = take(1)[0]
+        lower_ref = take(1)[0]
     if start == 0:
         a_ref = take(1)[0]
+    if stop == panels:
+        own_ref, own_sem = take(2)
 
     if start == 0:
         assemble_rows(q, width, own, groups, owner_ref, table_ref, chunks, late_rounds, a_ref)
@@ -459,8 +466,14 @@
 
     factor_panels(start, stop, s_out, q * width, width, lh, ll, invh, invl, job)
     if stop == panels:
-        at = place_ref[0]
-        own_ref[...] = lh[ds(at, own), :].astype(F32) + ll[ds(at, own), :].astype(F32)
+
+        @pl.when(place_ref[3] == q)
+        def _():
+            rows = ds(place_ref[0], own)
+            own_ref[...] = lh[rows, :].astype(F32) + ll[rows, :].astype(F32)
+            copy = pltpu.make_async_copy(own_ref, lower_ref.at[:, : own_ref.shape[1]], own_sem)
+            copy.start()
+            copy.wait()
 
 
 def landing_kernel(stages, sources, cap, refs):
@@ -470,8 +483,11 @@
         out, refs[:count] = refs[:count], []
         return out
 
-    lh, ll, ih, il = (take(stages) for _ in range(4))
-    (raw_ref, th, tl, sq_ref, t_ref, copy_sems) = take(6)
+    given = take(4 * stages)
+    (raw_ref, th, tl, sq_ref, t_ref) = take(5)
+    held = take(4 * stages)
+    (copy_sems,) = take(1)
+    lh, ll, ih, il = (held[k * stages : (k + 1) * stages] for k in range(4))
     front = raw_ref.shape[0]
     total = sources * cap
     width = ih[0].shape[0]
@@ -485,9 +501,23 @@
             )
         )
         copies[-1].start()
+    factors = [
+        [
+            pltpu.make_async_copy(
+                given[k * stages + q], held[k * stages + q], copy_sems.at[front + 4 * q + k]
+            )
+            for k in range(4)
+        ]
+        for q in range(stages)
+    ]
+    for stage in factors:
+        for copy in stage:
+            copy.start()
     for copy in copies:
         copy.wait()
     for q in range(stages):
+        for copy in factors[q]:
+            copy.wait()
         part = t_ref.at[:, q * width : (q + 1) * width]
         subtract_products(part, total, width, th, tl, lh[q], ll[q], q * width)
         times_inverse(part, th, tl, q * width, total, width, ih[q], il[q])
@@ -667,7 +697,7 @@
     here = gathered[-1][1:]
     late = Ring(after(jnp.concatenate(chunks[early + 1 :], axis=1), here), "front", front)
     table_in = jnp.asarray(table)
-    place = jnp.stack([(me % per_stage) * own, first_row, bulk_me]).astype(jnp.int32)
+    place = jnp.stack([(me % per_stage) * own, first_row, bulk_me, me // per_stage]).astype(jnp.int32)
 
     own_lands = own_map < pivots
     own_rank = jnp.where(own_lands, ranks(own_lands), -1)
@@ -723,11 +753,13 @@
         sent["lines"] = sent["all"][:, share : share + extra.shape[0]].reshape((front,) + line.shape)
         return both
 
-    hooks = [send_first, send_second, send_third]
+    place = after(place, send_first(started))
+    hooks = [lambda token: place, send_second, send_third]
 
     panels = width // LANES
     total_landing = sources * cap
-    lh, ll, ih, il, owned = ([] for _ in range(5))
+    lh, ll, ih, il = ([] for _ in range(4))
+    lower_rows = jnp.zeros((own, total), F32)
     xs = None
     for q in range(stages):
         final = q == stages - 1
@@ -771,10 +803,16 @@
             scratch = []
             if couples:
                 outs += [shaped((own, q * width), BF16)] * 2
+            out_kinds = [False] * len(outs)
             if stop == panels:
-                outs.append(shaped((own, deep), F32))
+                aliases[len(operands)] = len(outs)
+                operands.append(lower_rows)
+                outs.append(shaped((own, total), F32))
+                out_kinds.append(None)
             if start == 0:
                 scratch.append(pltpu.VMEM((width, deep), F32))
+            if stop == panels:
+                scratch += [pltpu.VMEM((own, deep), F32), pltpu.SemaphoreType.DMA(())]
             out = list(
                 vmem_call(
                     functools.partial(
@@ -786,12 +824,14 @@
                     ),
                     outs,
                     [True] * smem
-                    + [False] * (len(operands) - smem),
+                    + [False] * (len(operands) - smem - (stop == panels))
+                    + [None] * (stop == panels),
                     scratch,
                     pl.CostEstimate(
                         flops=6_000_000_000 * (stop - start), bytes_accessed=1 << 20, transcendentals=0
                     ),
                     aliases,
+                    out_kinds,
                 )(*operands)
             )
             state = out[:5]
@@ -799,8 +839,7 @@
             if couples:
                 xs, rest = rest[:2], rest[2:]
             if stop == panels:
-                owned.append(rest[0])
-                rest = rest[1:]
+                lower_rows = rest[0]
             if q < 2 and not final:
                 place = late.arrive(place, state[0])
                 if hooks:
@@ -834,15 +873,12 @@
             shaped((total_landing, total), BF16),
             shaped((blocks * (blocks + 1) // 2, LANES, LANES), F32),
         ],
-        [False] * len(operands) + [None],
-        [pltpu.VMEM((total_landing, total), F32), pltpu.SemaphoreType.DMA((front,))],
+        [None] * (len(operands) + 1),
+        [pltpu.VMEM((total_landing, total), F32)]
+        + [pltpu.VMEM(x.shape, x.dtype) for x in operands]
+        + [pltpu.SemaphoreType.DMA((front + 4 * stages,))],
         pl.CostEstimate(flops=20_000_000_000, bytes_accessed=1 << 20, transcendentals=0),
     )(*operands, sent["all"])
-
-    lower_rows = jnp.zeros((own, total), F32)
-    for q in range(stages):
-        padded = jnp.pad(owned[q], ((0, 0), (0, total - (q + 1) * width)))
-        lower_rows = jnp.where(me // per_stage == q, padded, lower_rows)
 
     solved = max(stages - 2, 0)
     operands = [coupling[:, solved * width :]] + (xs if solved > 0 else [])

time: 423 us -> 406 us (0.960)
  the two profiles are of different devices: /device:TPU:28 before, /device:TPU:24 now
where the time goes in v6:
time: 406 us; the launch traced here: 399 us
  Pallas kernels  231 us (57%)
  waiting for transfers between devices  80.2 us (20%)
  starting transfers between devices  36.5 us (9%)
  local copies, waits for them, and re-layouts  18.5 us (5%)
  between operations  17.7 us (4%)
  other arithmetic  10.6 us (3%)
    pallas_call x6, Pallas kernels, on_device(): vmem_call(functools.partial(lambda *refs, args: child_stage(*args, refs),...  137 us
    ppermute x12, waiting for transfers between devices, advance(): self.going = lax.ppermute(self.going, self.axis, self.ahead)  61.8 us
    pallas_call x1, Pallas kernels, on_device(): vmem_call(lambda *refs: parent_kernel(bulk, blocks, width, sources, refs)...  53.4 us
    pallas_call x1, Pallas kernels, on_device(): vmem_call(lambda *refs: landing_kernel(stages, sources, cap, refs), [shap...  20.9 us
    ppermute x9, starting transfers between devices, advance(): self.coming = lax.ppermute(self.coming, self.axis, self.back)  12.4 us
    pallas_call x1, Pallas kernels, on_device(): vmem_call(lambda *refs: own_kernel(solved, stages, width, refs), [shaped(...  11.7 us
    ppermute x2, waiting for transfers between devices, spread_out(): lax.ppermute(x[k * rows:(k + 1) * rows], 'front', [(s, s + k * sources) f...  11.3 us
    ppermute x12, starting transfers between devices, advance(): self.going = lax.ppermute(self.going, self.axis, self.ahead)  8.43 us
  transfers between devices with their start and end apart: 39, of which 17 were waited for; matrix products, arithmetic and copies ran while one was open for 6% of the time, Pallas kernels for 56%

profile of v6, /device:TPU:24, one launch (start us, length us, event | category | flops | bytes accessed | tf_op | source)
XLA Modules:
  0.0 398.8 jit_solution(8423117776211795843)
XLA Ops:
  16.0 5.6 %collective-permute-done.refs_4_ = f32[264,384]{1,0:T(8,128)S(1)} collective-permute-done((f32[264,384]{1,0:T(8,128)S(1)}, f32[264,384]{1,0:T(8,128)S(1)}, u32[]{:S(2)}, u32[]{:S(2)}) %collective-permute-start) | collective-permute-done | bytes 405536 | tf_op jit(solution)/shard_map/ppermute | solution.py:312
  23.3 1.6 collective-permute-start.3
  25.7 7.2 %collective-permute-done.2.refs_5_ = f32[264,384]{1,0:T(8,128)} collective-permute-done((f32[264,384]{1,0:T(8,128)S(1)}, f32[264,384]{1,0:T(8,128)}, u32[]{:S(2)}, u32[]{:S(2)}) %collective-permute-start.2) | collective-permute-done | bytes 405536 | tf_op jit(solution)/shard_map/ppermute | solution.py:312
  33.7 1.6 collective-permute-start.5
  36.1 6.3 %collective-permute-done.4.refs_6_ = f32[264,384]{1,0:T(8,128)S(1)} collective-permute-done((f32[264,384]{1,0:T(8,128)}, f32[264,384]{1,0:T(8,128)S(1)}, u32[]{:S(2)}, u32[]{:S(2)}) %collective-permute-start.4) | collective-permute-done | bytes 405536 | tf_op jit(solution)/shard_map/ppermute | solution.py:312
  45.8 7.4 %collective-permute-done.6.refs_7_ = f32[264,384]{1,0:T(8,128)S(1)} collective-permute-done((f32[264,384]{1,0:T(8,128)S(1)}, f32[264,384]{1,0:T(8,128)S(1)}, u32[]{:S(2)}, u32[]{:S(2)}) %collective-permute-start.6) | collective-permute-done | bytes 405536 | tf_op jit(solution)/shard_map/ppermute | solution.py:312
  53.5 1.8 collective-permute-start.8
  56.1 6.2 %collective-permute-done.7.refs_12_ = f32[256,256]{1,0:T(8,128)S(1)} collective-permute-done((f32[256,256]{1,0:T(8,128)S(1)}, f32[256,256]{1,0:T(8,128)S(1)}, u32[]{:S(2)}, u32[]{:S(2)}) %collective-permute-start.7) | collective-permute-done | bytes 262176 | tf_op jit(solution)/shard_map/ppermute | solution.py:312
  63.0 1.6 collective-permute-start.10
  69.6 1.6 collective-permute-start.18
  74.6 2.9 collective-permute-start.15
  81.4 8.0 %collective-permute-done.13.refs_15_ = f32[256,256]{1,0:T(8,128)S(1)} collective-permute-done((f32[256,256]{1,0:T(8,128)}, f32[256,256]{1,0:T(8,128)S(1)}, u32[]{:S(2)}, u32[]{:S(2)}) %collective-permute-start.13) | collective-permute-done | bytes 262176 | tf_op jit(solution)/shard_map/ppermute | solution.py:312
  89.8 1.6 collective-permute-start.21
  91.4 13.2 %shard_map.112 = (f32[512,512]{1,0:T(8,128)}, bf16[512,512]{1,0:T(8,128)(2,1)}, bf16[512,512]{1,0:T(8,128)(2,1)}, bf16[512,512]{1,0:T(8,128)(2,1)}, bf16[512,512]{1,0:T(8,128)(2,1)}) custom-call(s32[4]{0:T(128)} %pad_add_fusion.refs_0_, s32[8]{0:T(128)} %copy-done.9, s32[3,8]{1,0:T(4,128)} %constant.192.clone.refs_2_, f32[264,384]{1,0:T(8,128)} %copy-done.4, ...), custom_call_target="tpu_custom_call" | custom-call | flops 12000000000 | bytes 1048576 | tf_op jit(solution)/shard_map/pallas_call | solution.py:817
  105.0 1.6 collective-permute-start.23
  107.6 9.9 %collective-permute-done.22.refs_21_ = f32[256,512]{1,0:T(8,128)S(1)} collective-permute-done((f32[256,512]{1,0:T(8,128)}, f32[256,512]{1,0:T(8,128)S(1)}, u32[]{:S(2)}, u32[]{:S(2)}) %collective-permute-start.22) | collective-permute-done | bytes 524320 | tf_op jit(solution)/shard_map/ppermute | solution.py:312
  119.8 1.8 collective-permute-start.25
  123.2 14.6 %shard_map.113 = (f32[512,512]{1,0:T(8,128)}, bf16[512,512]{1,0:T(8,128)(2,1)}, bf16[512,512]{1,0:T(8,128)(2,1)}, bf16[512,512]{1,0:T(8,128)(2,1)}, bf16[512,512]{1,0:T(8,128)(2,1)}, /*index=5*/f32[256,2048]{1,0:T(8,128)}) custom-call(s32[4]{0:T(128)} %pad_add_fusion.refs_0_, ...), custom_call_target="tpu_custom_call", output_to_operand_aliasing={{0}: (1, {}), {1}: (2, {}), {2}: (3, {}), {3}: (4, {}), {4}... | custom-call | flops 12000000000 | bytes 1048576 | tf_op jit(solution)/shard_map/pallas_call | solution.py:817
  139.8 11.3 %collective-permute-done.25 = f32[32,1024]{1,0:T(8,128)S(1)} collective-permute-done((f32[32,1024]{1,0:T(8,128)S(1)}, f32[32,1024]{1,0:T(8,128)S(1)}, u32[]{:S(2)}, u32[]{:S(2)}) %collective-permute-start.25) | collective-permute-done | bytes 131104 | tf_op jit(solution)/shard_map/ppermute | solution.py:711
  152.5 16.9 %shard_map.114 = (f32[512,512]{1,0:T(8,128)}, bf16[512,1024]{1,0:T(8,128)(2,1)}, bf16[512,1024]{1,0:T(8,128)(2,1)}, bf16[512,512]{1,0:T(8,128)(2,1)}, bf16[512,512]{1,0:T(8,128)(2,1)}) custom-call(s32[4]{0:T(128)} %pad_add_fusion.refs_0_, s32[8]{0:T(128)} %copy-done.9, s32[3,8]{1,0:T(4,128)} %constant.192.clone.refs_2_, f32[264,384]{1,0:T(8,128)} %copy-done.4, ...), custom_call_target="tpu_custom_call" | custom-call | flops 12000000000 | bytes 1048576 | tf_op jit(solution)/shard_map/pallas_call | solution.py:817
  173.7 1.6 collective-permute-start.28
  175.4 16.3 %shard_map.115 = (f32[512,512]{1,0:T(8,128)}, bf16[512,1024]{1,0:T(8,128)(2,1)}, bf16[512,1024]{1,0:T(8,128)(2,1)}, bf16[512,512]{1,0:T(8,128)(2,1)}, bf16[512,5...) custom-call(s32[4]{0:T(128)} %pad_add_fusion.refs_0_, ...), custom_call_target="tpu_custom_call", output_to_operand_aliasing={{0}: (1, {}), {1}: (2, {}), {2}: (3, {}), {3}: (4, {}), {4}... | custom-call | flops 12000000000 | bytes 1048576 | tf_op jit(solution)/shard_map/pallas_call | solution.py:817
  191.7 11.1 %collective-permute-done.28.refs_23_ = f32[256,512]{1,0:T(8,128)S(1)} collective-permute-done((f32[256,512]{1,0:T(8,128)}, f32[256,512]{1,0:T(8,128)S(1)}, u32[]{:S(2)}, u32[]{:S(2)}) %collective-permute-start.28) | collective-permute-done | bytes 524320 | tf_op jit(solution)/shard_map/ppermute | solution.py:312
  203.6 35.0 %shard_map.116 = (f32[512,512]{1,0:T(8,128)}, bf16[512,1536]{1,0:T(8,128)(2,1)}, bf16[512,1536]{1,0:T(8,128)(2,1)}, bf16[512,512]{1,0:T(8,128)(2,1)}, bf16[512,5...) custom-call(s32[4]{0:T(128)} %pad_add_fusion.refs_0_, ...), custom_call_target="tpu_custom_call", output_to_operand_aliasing={{7}: (38, {})} | custom-call | flops 24000000000 | bytes 1048576 | tf_op jit(solution)/shard_map/pallas_call | solution.py:817
  238.5 41.2 %shard_map.117 = (f32[512,512]{1,0:T(8,128)}, bf16[512,2048]{1,0:T(8,128)(2,1)}, bf16[512,2048]{1,0:T(8,128)(2,1)}, bf16[512,512]{1,0:T(8,128)(2,1)}, bf16[512,512]{1,0:T(8,128)(2,1)}, /*index=5*/f32[256,2048]{1,0:T(8,128)}) custom-call(s32[4]{0:T(128)} %pad_add_fusion.refs_0_, s32[8]{0:T(128)} %copy-done.9, ...), custom_call_target="tpu_custom_call", output_to_operand_aliasing={{5}: (39, {})} | custom-call | flops 24000000000 | bytes 1048576 | tf_op jit(solution)/shard_map/pallas_call | solution.py:817
  282.5 20.9 %shard_map.118 = (bf16[512,2048]{1,0:T(8,128)(2,1)}, bf16[512,2048]{1,0:T(8,128)(2,1)}, f32[10,128,128]{2,1,0:T(8,128)}) custom-call(bf16[512,512]{1,0:T(8,128)(2,1)} %get-tuple-element.154.refs_19_.refs_6_.refs_27_.refs_0_, bf16[512,1024]{1,0:T(8,128)(2,1)} %get-tuple-element.170.refs_28_.refs_1_, ...), custom_call_target="tpu_custom_call" | custom-call | flops 20000000000 | bytes 1048576 | tf_op jit(solution)/shard_map/pallas_call | solution.py:869
  304.6 2.4 collective-permute-done.30
  307.1 11.7 %shard_map.119 = (f32[256,2048]{1,0:T(8,128)}, f32[256,512]{1,0:T(8,128)}) custom-call(f32[256,1024]{1,0:T(8,128)} %slice.120.refs_0_, bf16[256,1024]{1,0:T(8,128)(2,1)} %get-tuple-element.183.refs_1_, bf16[256,1024]{1,0:T(8,128)(2,1)} %get-tuple-element.184.refs_2_, bf16[512,1536]{1,0:T(8,128)(2,1)} %get-tuple-element.177.refs_29_.refs_2_.refs_3_, ...), custom_call_target="tpu_custom_call" | custom-call | flops 10000000000 | bytes 1048576 | tf_op jit(solution)/shard_map/pallas_call | solution.py:886
  318.8 2.3 collective-permute-done.36.refs_8_
  327.2 3.0 conditional.1
  330.2 53.4 %shard_map.120 = (bf16[1024,1024]{1,0:T(8,128)(2,1)}, bf16[1024,1024]{1,0:T(8,128)(2,1)}, bf16[2,512,512]{2,1,0:T(8,128)(2,1)}, bf16[2,512,512]{2,1,0:T(8,128)(2,1)}) custom-call(s32[4]{0:T(128)} %pad_add_fusion.refs_0_, bf16[4,256,512]{2,1,0:T(8,128)(2,1)} %compare_convert_fusion.refs_1_.refs_3_, f32[8,32,1024]{2,1,0:T(8,128)S(1)} %get-tuple-element.194.refs_2_, ...), custom_call_target="tpu_custom_call" | custom-call | flops 60000002048 | bytes 16777216 | tf_op jit(solution)/shard_map/pallas_call | solution.py:924
  383.6 7.8 %shard_map.121 = f32[256,1024]{1,0:T(8,128)} custom-call(s32[4]{0:T(128)} %pad_add_fusion.refs_0_, f32[256,1024]{1,0:T(8,128)S(1)} %get-tuple-element.192.refs_1_, bf16[4,256,256]{2,1,0:T(8,128)(2,1)} %compare_convert_fusion.1.refs_2_, bf16[4,256,512]{2,1,0:T(8,128)(2,1)} %compare_convert_fusion.refs_1_.refs_3_, f32[256,512]{1,0:T(8,128)} %get-tuple-element.193.refs_4_, ...), custom_call_target="tpu_custom_call" | custom-call | tf_op jit(solution)/shard_map/pallas_call | solution.py:937
  (170 shorter events, 51.6 us)
Async XLA Ops:
  7.2 272.6 %all-gather.6.cloned.1.call-start = ((), (), s32[]{:S(2)}) async-start(), calls=%async_computation.4 | async-start | bytes 5898240 | tf_op jit(solution)/shard_map/all_gather | solution.py:751
  10.5 11.2 %collective-permute-start = (f32[264,384]{1,0:T(8,128)S(1)}, f32[264,384]{1,0:T(8,128)S(1)}, u32[]{:S(2)}, u32[]{:S(2)}) collective-permute-start(f32[264,384]{1,0:T(8,128)S(1)} %select_maximum_fusion.refs_3_), channel_id=1, source_target_pairs={{0,2},{2,4},{4,6},{6,7},{7,5},{5,3},{3,1},{1,0},{8,10},{10,12},{12... | collective-permute-start | bytes 1216520 | tf_op jit(solution)/shard_map/ppermute | solution.py:312
  12.0 10.8 %collective-permute-start.1 = (f32[264,384]{1,0:T(8,128)S(1)}, f32[264,384]{1,0:T(8,128)S(1)}, u32[]{:S(2)}, u32[]{:S(2)}) collective-permute-start(f32[264,384]{1,0:T(8,128)S(1)} %select_maximum_fusion.refs_3_), channel_id=1, source_target_pairs={{2,0},{4,2},{6,4},{7,6},{5,7},{3,5},{1,3},{0,1},{10,8},{12,10},{14... | collective-permute-start | bytes 1216520 | tf_op jit(solution)/shard_map/ppermute | solution.py:315
  22.9 10.0 %collective-permute-start.2 = (f32[264,384]{1,0:T(8,128)S(1)}, f32[264,384]{1,0:T(8,128)}, u32[]{:S(2)}, u32[]{:S(2)}) collective-permute-start(f32[264,384]{1,0:T(8,128)S(1)} %collective-permute-done.refs_4_), channel_id=1, source_target_pairs={{0,2},{2,4},{4,6},{6,7},{7,5},{5,3},{3,1},{1,0},{8,10},{10,12},{12... | collective-permute-start | bytes 1216520 | tf_op jit(solution)/shard_map/ppermute | solution.py:312
  23.3 10.0 %collective-permute-start.3 = (f32[264,384]{1,0:T(8,128)S(1)}, f32[264,384]{1,0:T(8,128)}, u32[]{:S(2)}, u32[]{:S(2)}) collective-permute-start(f32[264,384]{1,0:T(8,128)S(1)} %collective-permute-done.1.refs_8_), channel_id=1, source_target_pairs={{2,0},{4,2},{6,4},{7,6},{5,7},{3,5},{1,3},{0,1},{10,8},{12,10},{14... | collective-permute-start | bytes 1216520 | tf_op jit(solution)/shard_map/ppermute | solution.py:315
  33.3 9.1 %collective-permute-start.4 = (f32[264,384]{1,0:T(8,128)}, f32[264,384]{1,0:T(8,128)S(1)}, u32[]{:S(2)}, u32[]{:S(2)}) collective-permute-start(f32[264,384]{1,0:T(8,128)} %collective-permute-done.2.refs_5_), channel_id=1, source_target_pairs={{0,2},{2,4},{4,6},{6,7},{7,5},{5,3},{3,1},{1,0},{8,10},{10,12},{12... | collective-permute-start | bytes 1216520 | tf_op jit(solution)/shard_map/ppermute | solution.py:312
  33.7 9.0 %collective-permute-start.5 = (f32[264,384]{1,0:T(8,128)}, f32[264,384]{1,0:T(8,128)S(1)}, u32[]{:S(2)}, u32[]{:S(2)}) collective-permute-start(f32[264,384]{1,0:T(8,128)} %collective-permute-done.3.refs_9_), channel_id=1, source_target_pairs={{2,0},{4,2},{6,4},{7,6},{5,7},{3,5},{1,3},{0,1},{10,8},{12,10},{14... | collective-permute-start | bytes 1216520 | tf_op jit(solution)/shard_map/ppermute | solution.py:315
  43.5 9.8 %collective-permute-start.6 = (f32[264,384]{1,0:T(8,128)S(1)}, f32[264,384]{1,0:T(8,128)S(1)}, u32[]{:S(2)}, u32[]{:S(2)}) collective-permute-start(f32[264,384]{1,0:T(8,128)S(1)} %collective-permute-done.4.refs_6_), channel_id=1, source_target_pairs={{0,2},{2,4},{4,6},{6,7},{7,5},{5,3},{3,1},{1,0},{8,10},{10,12},{12... | collective-permute-start | bytes 1216520 | tf_op jit(solution)/shard_map/ppermute | solution.py:312
  53.2 9.0 %collective-permute-start.7 = (f32[256,256]{1,0:T(8,128)S(1)}, f32[256,256]{1,0:T(8,128)S(1)}, u32[]{:S(2)}, u32[]{:S(2)}) collective-permute-start(f32[256,256]{1,0:T(8,128)S(1)} %get-tuple-element.129.refs_11_), channel_id=1, source_target_pairs={{0,2},{2,4},{4,6},{6,7},{7,5},{5,3},{3,1},{1,0},{8,10},{10,12},{12... | collective-permute-start | bytes 786440 | tf_op jit(solution)/shard_map/ppermute | solution.py:312
  53.5 9.1 %collective-permute-start.8 = (f32[256,256]{1,0:T(8,128)S(1)}, f32[256,256]{1,0:T(8,128)S(1)}, u32[]{:S(2)}, u32[]{:S(2)}) collective-permute-start(f32[256,256]{1,0:T(8,128)S(1)} %get-tuple-element.129.refs_11_), channel_id=1, source_target_pairs={{2,0},{4,2},{6,4},{7,6},{5,7},{3,5},{1,3},{0,1},{10,8},{12,10},{14... | collective-permute-start | bytes 786440 | tf_op jit(solution)/shard_map/ppermute | solution.py:315
  62.5 8.6 %collective-permute-start.9 = (f32[256,256]{1,0:T(8,128)S(1)}, f32[256,256]{1,0:T(8,128)}, u32[]{:S(2)}, u32[]{:S(2)}) collective-permute-start(f32[256,256]{1,0:T(8,128)S(1)} %collective-permute-done.7.refs_12_), channel_id=1, source_target_pairs={{0,2},{2,4},{4,6},{6,7},{7,5},{5,3},{3,1},{1,0},{8,10},{10,12},{12... | collective-permute-start | bytes 786440 | tf_op jit(solution)/shard_map/ppermute | solution.py:312
  63.0 8.2 %collective-permute-start.10 = (f32[256,256]{1,0:T(8,128)S(1)}, f32[256,256]{1,0:T(8,128)}, u32[]{:S(2)}, u32[]{:S(2)}) collective-permute-start(f32[256,256]{1,0:T(8,128)S(1)} %collective-permute-done.8.refs_16_), channel_id=1, source_target_pairs={{2,0},{4,2},{6,4},{7,6},{5,7},{3,5},{1,3},{0,1},{10,8},{12,10},{14... | collective-permute-start | bytes 786440 | tf_op jit(solution)/shard_map/ppermute | solution.py:315
  71.2 8.5 %collective-permute-start.11 = (f32[256,256]{1,0:T(8,128)}, f32[256,256]{1,0:T(8,128)}, u32[]{:S(2)}, u32[]{:S(2)}) collective-permute-start(f32[256,256]{1,0:T(8,128)} %collective-permute-done.9.refs_13_), channel_id=1, source_target_pairs={{0,2},{2,4},{4,6},{6,7},{7,5},{5,3},{3,1},{1,0},{8,10},{10,12},{12... | collective-permute-start | bytes 786440 | tf_op jit(solution)/shard_map/ppermute | solution.py:312
  71.6 8.0 %collective-permute-start.12 = (f32[256,256]{1,0:T(8,128)}, f32[256,256]{1,0:T(8,128)}, u32[]{:S(2)}, u32[]{:S(2)}) collective-permute-start(f32[256,256]{1,0:T(8,128)} %collective-permute-done.10.refs_17_), channel_id=1, source_target_pairs={{2,0},{4,2},{6,4},{7,6},{5,7},{3,5},{1,3},{0,1},{10,8},{12,10},{14... | collective-permute-start | bytes 786440 | tf_op jit(solution)/shard_map/ppermute | solution.py:315
  80.8 8.6 %collective-permute-start.13 = (f32[256,256]{1,0:T(8,128)}, f32[256,256]{1,0:T(8,128)S(1)}, u32[]{:S(2)}, u32[]{:S(2)}) collective-permute-start(f32[256,256]{1,0:T(8,128)} %collective-permute-done.11.refs_14_), channel_id=1, source_target_pairs={{0,2},{2,4},{4,6},{6,7},{7,5},{5,3},{3,1},{1,0},{8,10},{10,12},{12... | collective-permute-start | bytes 786440 | tf_op jit(solution)/shard_map/ppermute | solution.py:312
  89.4 15.2 %collective-permute-start.20 = (f32[256,512]{1,0:T(8,128)}, f32[256,512]{1,0:T(8,128)}, u32[]{:S(2)}, u32[]{:S(2)}) collective-permute-start(f32[256,512]{1,0:T(8,128)} %pad_maximum_fusion.1.refs_19_), channel_id=1, source_target_pairs={{0,2},{2,4},{4,6},{6,7},{7,5},{5,3},{3,1},{1,0},{8,10},{10,12},{12... | collective-permute-start | bytes 1572872 | tf_op jit(solution)/shard_map/ppermute | solution.py:312
  89.8 14.8 %collective-permute-start.21 = (f32[256,512]{1,0:T(8,128)}, f32[256,512]{1,0:T(8,128)}, u32[]{:S(2)}, u32[]{:S(2)}) collective-permute-start(f32[256,512]{1,0:T(8,128)} %pad_maximum_fusion.1.refs_19_), channel_id=1, source_target_pairs={{2,0},{4,2},{6,4},{7,6},{5,7},{3,5},{1,3},{0,1},{10,8},{12,10},{14... | collective-permute-start | bytes 1572872 | tf_op jit(solution)/shard_map/ppermute | solution.py:315
  104.6 12.9 %collective-permute-start.22 = (f32[256,512]{1,0:T(8,128)}, f32[256,512]{1,0:T(8,128)S(1)}, u32[]{:S(2)}, u32[]{:S(2)}) collective-permute-start(f32[256,512]{1,0:T(8,128)} %collective-permute-done.20.refs_20_), channel_id=1, source_target_pairs={{0,2},{2,4},{4,6},{6,7},{7,5},{5,3},{3,1},{1,0},{8,10},{10,12},{12... | collective-permute-start | bytes 1572872 | tf_op jit(solution)/shard_map/ppermute | solution.py:312
  105.0 12.5 %collective-permute-start.23 = (f32[256,512]{1,0:T(8,128)}, f32[256,512]{1,0:T(8,128)S(1)}, u32[]{:S(2)}, u32[]{:S(2)}) collective-permute-start(f32[256,512]{1,0:T(8,128)} %collective-permute-done.21.refs_24_), channel_id=1, source_target_pairs={{2,0},{4,2},{6,4},{7,6},{5,7},{3,5},{1,3},{0,1},{10,8},{12,10},{14... | collective-permute-start | bytes 1572872 | tf_op jit(solution)/shard_map/ppermute | solution.py:315
  118.5 32.7 %collective-permute-start.24 = (f32[64,2048]{1,0:T(8,128)}, f32[64,2048]{1,0:T(8,128)}, u32[]{:S(2)}, u32[]{:S(2)}) collective-permute-start(f32[64,2048]{1,0:T(8,128)} %slice.96), channel_id=1, source_target_pairs={{0,4},{1,5},{2,6},{3,7},{8,12},{9,13},{10,14},{11,15},{16,20},{17,... | collective-permute-start | bytes 1572872 | tf_op jit(solution)/shard_map/ppermute | solution.py:711
  119.8 31.3 %collective-permute-start.25 = (f32[32,1024]{1,0:T(8,128)S(1)}, f32[32,1024]{1,0:T(8,128)S(1)}, u32[]{:S(2)}, u32[]{:S(2)}) collective-permute-start(f32[32,1024]{1,0:T(8,128)S(1)} %slice.98), channel_id=1, source_target_pairs={{0,4},{1,5},{2,6},{3,7},{8,12},{9,13},{10,14},{11,15},{16,20},{17,... | collective-permute-start | bytes 393224 | tf_op jit(solution)/shard_map/ppermute | solution.py:711
  137.8 31.6 %collective-permute-start.26 = (f32[256,512]{1,0:T(8,128)}, f32[256,512]{1,0:T(8,128)}, u32[]{:S(2)}, u32[]{:S(2)}) collective-permute-start(f32[256,512]{1,0:T(8,128)} %copy-done.15), channel_id=1, source_target_pairs={{0,2},{2,4},{4,6},{6,7},{7,5},{5,3},{3,1},{1,0},{8,10},{10,12},{12... | collective-permute-start | bytes 1572872 | tf_op jit(solution)/shard_map/ppermute | solution.py:312
  139.3 30.0 %collective-permute-start.27 = (f32[256,512]{1,0:T(8,128)}, f32[256,512]{1,0:T(8,128)}, u32[]{:S(2)}, u32[]{:S(2)}) collective-permute-start(f32[256,512]{1,0:T(8,128)} %copy-done.16), channel_id=1, source_target_pairs={{2,0},{4,2},{6,4},{7,6},{5,7},{3,5},{1,3},{0,1},{10,8},{12,10},{14... | collective-permute-start | bytes 1572872 | tf_op jit(solution)/shard_map/ppermute | solution.py:315
  173.7 29.0 %collective-permute-start.28 = (f32[256,512]{1,0:T(8,128)}, f32[256,512]{1,0:T(8,128)S(1)}, u32[]{:S(2)}, u32[]{:S(2)}) collective-permute-start(f32[256,512]{1,0:T(8,128)} %collective-permute-done.26.refs_22_), channel_id=1, source_target_pairs={{0,2},{2,4},{4,6},{6,7},{7,5},{5,3},{3,1},{1,0},{8,10},{10,12},{12... | collective-permute-start | bytes 1572872 | tf_op jit(solution)/shard_map/ppermute | solution.py:312
  281.3 44.9 %collective-permute-start.29 = (f32[8,32,1024]{2,1,0:T(8,128)S(1)}, f32[8,32,1024]{2,1,0:T(8,128)S(1)}, u32[]{:S(2)}, u32[]{:S(2)}) collective-permute-start(f32[8,32,1024]{2,1,0:T(8,128)S(1)} %reshape.168), channel_id=1, source_target_pairs={{0,8},{8,0},{16,24},{24,16},{1,9},{9,1},{17,25},{25,17},{2,10},{10... | collective-permute-start | bytes 3145736 | tf_op jit(solution)/shard_map/ppermute | solution.py:354
  281.4 25.7 %collective-permute-start.30 = (f32[8,32,1024]{2,1,0:T(8,128)S(1)}, f32[8,32,1024]{2,1,0:T(8,128)}, u32[]{:S(2)}, u32[]{:S(2)}) collective-permute-start(f32[8,32,1024]{2,1,0:T(8,128)S(1)} %reshape.168), channel_id=1, source_target_pairs={{0,16},{8,24},{16,0},{24,8},{1,17},{9,25},{17,1},{25,9},{2,18},{10... | collective-permute-start | bytes 3145736 | tf_op jit(solution)/shard_map/ppermute | solution.py:354
  303.5 26.7 %collective-permute-start.35 = (f32[10,128,128]{2,1,0:T(8,128)}, f32[10,128,128]{2,1,0:T(8,128)}, u32[]{:S(2)}, u32[]{:S(2)}) collective-permute-start(f32[10,128,128]{2,1,0:T(8,128)} %get-tuple-element.198.refs_6_), channel_id=1, source_target_pairs={{0,8},{8,0},{16,24},{24,16},{1,9},{9,1},{17,25},{25,17},{2,10},{10... | collective-permute-start | bytes 1966088 | tf_op jit(solution)/shard_map/ppermute | solution.py:354
  303.7 17.4 %collective-permute-start.36 = (f32[10,128,128]{2,1,0:T(8,128)}, f32[10,128,128]{2,1,0:T(8,128)}, u32[]{:S(2)}, u32[]{:S(2)}) collective-permute-start(f32[10,128,128]{2,1,0:T(8,128)} %get-tuple-element.198.refs_6_), channel_id=1, source_target_pairs={{0,16},{8,24},{16,0},{24,8},{1,17},{9,25},{17,1},{25,9},{2,18},{10... | collective-permute-start | bytes 1966088 | tf_op jit(solution)/shard_map/ppermute | solution.py:354
  307.1 20.1 %collective-permute-start.31 = (f32[8,32,1024]{2,1,0:T(8,128)}, f32[8,32,1024]{2,1,0:T(8,128)}, u32[]{:S(2)}, u32[]{:S(2)}) collective-permute-start(f32[8,32,1024]{2,1,0:T(8,128)} %collective-permute-done.30), channel_id=1, source_target_pairs={{0,8},{8,0},{16,24},{24,16},{1,9},{9,1},{17,25},{25,17},{2,10},{10... | collective-permute-start | bytes 3145736 | tf_op jit(solution)/shard_map/ppermute | solution.py:354
  321.1 9.1 %collective-permute-start.37 = (f32[10,128,128]{2,1,0:T(8,128)}, f32[10,128,128]{2,1,0:T(8,128)}, u32[]{:S(2)}, u32[]{:S(2)}) collective-permute-start(f32[10,128,128]{2,1,0:T(8,128)} %collective-permute-done.36.refs_8_), channel_id=1, source_target_pairs={{0,8},{8,0},{16,24},{24,16},{1,9},{9,1},{17,25},{25,17},{2,10},{10... | collective-permute-start | bytes 1966088 | tf_op jit(solution)/shard_map/ppermute | solution.py:354
  325.1 58.5 %collective-permute-start.33 = (f32[256,512]{1,0:T(8,128)}, f32[256,512]{1,0:T(8,128)}, u32[]{:S(2)}, u32[]{:S(2)}) collective-permute-start(f32[256,512]{1,0:T(8,128)} %get-tuple-element.193.refs_4_), channel_id=1, source_target_pairs={{0,16},{8,24},{16,0},{24,8},{1,17},{9,25},{17,1},{25,9},{2,18},{10... | collective-permute-start | bytes 1572872 | tf_op jit(solution)/shard_map/ppermute | solution.py:354
  326.2 57.4 %collective-permute-start.34 = (f32[256,512]{1,0:T(8,128)}, f32[256,512]{1,0:T(8,128)}, u32[]{:S(2)}, u32[]{:S(2)}) collective-permute-start(f32[256,512]{1,0:T(8,128)} %collective-permute-done.32.refs_5_), channel_id=1, source_target_pairs={{0,16},{8,24},{16,0},{24,8},{1,17},{9,25},{17,1},{25,9},{2,18},{10... | collective-permute-start | bytes 1572872 | tf_op jit(solution)/shard_map/ppermute | solution.py:354
  (31 other events, 344.9 us)
Sparse Core Ops, SparseCore 0:
  170.4 89.9 all-gather.5
